TPU v7x, 256 devices: a whole 4x4x8 slice. The times are simulated.
256 devices in a mesh: aux: 32 (over y, z), orb: 4 (over x_hi, core), rdm: 2 (over x_lo).
Axes of the slice: x: 4 (x_hi: 2, x_lo: 2; x = x_hi * 2 + x_lo), y: 4, z: 8, core: 2. Of those that a mesh axis runs over, the one named last changes fastest.
Arguments:
- pair_coeffs: float32 [1536, 9216], P('aux', ('orb', 'rdm')), may hold values from -6 to 6
- rdm: float32 [9216, 9216], P('aux', ('orb', 'rdm')), may hold values from -0.625 to 0.625
- b_tensor: float32 [1536, 96, 4000], P('aux', None, ('orb', 'rdm')), may hold values from -4.6875 to 4.6875
- gen_coeffs: float32 [4000, 4000], P('aux', ('orb', 'rdm')), may hold values from -6 to 6
- act_coeffs: float32 [4000, 96], P('aux'), may hold values from -38.418747 to 38.418747
Outputs:
- direction: float32 [96, 4000], P(None, ('orb', 'rdm'))
- active_shift: float32 [4000, 96], P('aux')
- general_shift: float32 [4000, 4000], P('aux', ('orb', 'rdm'))
All inputs are finite; a program needn't handle non-finite values.
Results may differ from a plain program's by a relative error of at most 0.0001.
Values sent between devices are 32-bit elements; how exact they have to be, the bound alone decides.
No kernel may reach another device: no remote copies, remote signals or barrier semaphores. Data moves between devices by JAX's collectives and lax.ppermute only.
A program may use at most 64 MiB of HBM per device.

v0:
```python
import math

import jax
import jax.numpy as jnp
from jax import lax
from jax.sharding import PartitionSpec as P

NORB = 4000


def on_device(pair_coeffs, rdm, b_tensor, gen_coeffs, act_coeffs):
    highest = lax.Precision.HIGHEST
    nact = b_tensor.shape[1]
    partial_fit = lax.dot_general(
        lax.all_gather(pair_coeffs, "aux", axis=0, tiled=True),
        rdm,
        (((1,), (1,)), ((), ())),
        precision=highest,
        preferred_element_type=jnp.float32,
    )
    summed = lax.psum(partial_fit, ("orb", "rdm"))
    fitted = lax.all_to_all(summed, "aux", split_axis=0, concat_axis=1, tiled=True)
    fitted_three = fitted.reshape(fitted.shape[0], nact, nact)
    fock_part = jnp.einsum("qtu,qup->tp", fitted_three, b_tensor, precision=highest)
    fock = lax.psum(fock_part, "aux")
    grad = 2.0 * fock
    squares = jnp.sum(grad * grad)
    step_scale = math.sqrt(nact)
    total = lax.psum(squares, ("orb", "rdm"))
    inverse = 1.0 / jnp.sqrt(total + 1e-06)
    kappa = -step_scale * grad * inverse
    active_part = jnp.dot(
        gen_coeffs, kappa.T, precision=highest, preferred_element_type=jnp.float32
    )
    active_shift = lax.psum(active_part, ("orb", "rdm"))
    general_shift = -jnp.dot(
        act_coeffs, kappa, precision=highest, preferred_element_type=jnp.float32
    )
    direction = math.sqrt(nact * NORB) * grad * inverse
    return (direction, active_shift, general_shift)


def solution(mesh):
    return jax.shard_map(
        on_device,
        mesh=mesh,
        in_specs=(
            P("aux", ("orb", "rdm")),
            P("aux", ("orb", "rdm")),
            P("aux", None, ("orb", "rdm")),
            P("aux", ("orb", "rdm")),
            P("aux", None),
        ),
        out_specs=(P(None, ("orb", "rdm")), P("aux", None), P("aux", ("orb", "rdm"))),
        check_vma=False,
    )
```

profile of v0, /device:TPU:6, one launch (start us, length us, event | category | flops | bytes accessed | tf_op | source)
XLA Modules:
  0.0 463.1 jit_solution(17464890987083338225)
XLA Ops:
  7.2 0.0 copy-start
  7.2 0.0 all-gather.2.cloned.1.call-start
  7.2 0.7 all-gather.2.cloned.1.call-update
  7.9 0.0 all-reduce.3.cloned.1.call-start
  8.0 97.6 %all-gather.2.cloned.1.call-done = f32[1536,1152]{1,0:T(8,128)} async-done(((f32[48,1152]{1,0:T(8,128)}), f32[1536,1152]{1,0:T(8,128)}) %all-gather.2.cloned.1.call-update) | async-done | bytes 7077904 | tf_op jit(solution)/shard_map/all_gather | solution.py:15
  105.6 0.0 copy-done
  105.6 15.1 %fusion.5 = f32[1536,288]{1,0:T(8,128)} fusion(f32[1536,1152]{1,0:T(8,128)} %all-gather.2.cloned.1.call-done, f32[288,1152]{1,0:T(8,128)S(1)} %copy-done), kind=kOutput, calls=%fused_computation.10 | convolution fusion | flops 6115295232 | bytes 10174464 | tf_op jit(solution)/shard_map/dot_general | solution.py:14
  120.7 0.0 all-reduce.3.cloned.1.call-update
  120.7 0.0 all-reduce.5.cloned.1.call-start
  120.7 66.4 %all-reduce.3.cloned.1.call-done = f32[32,48,288]{2,1,0:T(8,128)} async-done(((f32[32,48,288]{2,1,0:T(8,128)}), f32[32,48,288]{2,1,0:T(8,128)}) %all-reduce.3.cloned.1.call-update) | async-done | bytes 1769488 | tf_op jit(solution)/shard_map/psum | solution.py:21
  187.2 67.1 %all_to_all.16 = f32[32,48,288]{2,1,0:T(8,128)S(1)} all-to-all(f32[32,48,288]{2,1,0:T(8,128)} %all-reduce.3.cloned.1.call-done), channel_id=1, replica_groups=mesh['aux'=32,'orb'=4,'rdm'=2] {'aux'}, dimensions={0} | all-to-all | bytes 3538944 | tf_op jit(solution)/shard_map/all_to_all | solution.py:22
  254.3 2.1 copy.10
  256.4 4.1 reshape.13
  260.5 0.0 copy-start.1
  260.5 0.0 copy-start.2
  260.5 11.2 %convolution_bitcast_fusion = f32[96,500]{1,0:T(8,128)} fusion(f32[48,96,96]{2,1,0:T(8,128)} %reshape.13, f32[48,96,500]{2,1,0:T(8,128)} %param.7), kind=kOutput, calls=%fused_computation.2 | convolution fusion | flops 2654208000 | bytes 11177472 | tf_op jit(solution)/shard_map/qtu,qup->tp/dot_general | solution.py:24
  271.7 0.0 all-reduce.5.cloned.1.call-update
  271.8 139.9 %all-reduce.5.cloned.1.call-done = f32[96,500]{1,0:T(8,128)} async-done(((f32[96,500]{1,0:T(8,128)}), f32[96,500]{1,0:T(8,128)}) %all-reduce.5.cloned.1.call-update) | async-done | bytes 192016 | tf_op jit(solution)/shard_map/psum | solution.py:25
  411.6 1.6 multiply_reduce_fusion
  413.2 13.3 %psum.30 = f32[]{:T(128)} all-reduce(f32[]{:T(128)} %multiply_reduce_fusion), channel_id=1, replica_groups=mesh['aux'=32,'orb'=4,'rdm'=2] {'orb','rdm'}, use_global_device_ids=true, to_apply=%region_3.0 | all-reduce | flops 1 | bytes 8 | tf_op jit(solution)/shard_map/psum | solution.py:29
  427.2 0.0 copy-done.1
  427.2 1.3 convolution_bitcast_fusion.1
  428.5 24.3 %psum.31 = f32[125,96]{0,1:T(8,128)} all-reduce(f32[125,96]{0,1:T(8,128)S(1)} %convolution_bitcast_fusion.1), channel_id=1, replica_groups=mesh['aux'=32,'orb'=4,'rdm'=2] {'orb','rdm'}, use_global_device_ids=true, to_apply=%region_4.0 | all-reduce | flops 12000 | bytes 96000 | tf_op jit(solution)/shard_map/psum | solution.py:35
  452.7 1.6 broadcast_multiply_fusion
  454.3 0.0 copy-done.2
  454.3 2.2 fusion
Async XLA Ops:
  7.2 98.4 %copy-start = (f32[288,1152]{1,0:T(8,128)S(1)}, f32[288,1152]{1,0:T(8,128)}, u32[]{:S(2)}) copy-start(f32[288,1152]{1,0:T(8,128)} %param.6) | copy-start | bytes 3981316
  7.2 98.4 %all-gather.2.cloned.1.call-start = ((), (), s32[]{:S(2)}) async-start(), calls=%async_computation.1 | async-start | bytes 7299072 | tf_op jit(solution)/shard_map/all_gather | solution.py:15
  7.9 179.3 %all-reduce.3.cloned.1.call-start = ((), (), s32[]{:S(2)}) async-start(), calls=%async_computation.2 | async-start | bytes 4718592 | tf_op jit(solution)/shard_map/psum | solution.py:21
  120.7 290.9 %all-reduce.5.cloned.1.call-start = ((), (), s32[]{:S(2)}) async-start(), calls=%async_computation.3 | async-start | bytes 393216 | tf_op jit(solution)/shard_map/psum | solution.py:25
  260.5 166.7 %copy-start.1 = (f32[125,500]{0,1:T(8,128)S(1)}, f32[125,500]{0,1:T(8,128)}, u32[]{:S(2)}) copy-start(f32[125,500]{0,1:T(8,128)} %param.8) | copy-start | bytes 750004
  260.5 193.9 %copy-start.2 = (f32[125,96]{0,1:T(8,128)S(1)}, f32[125,96]{0,1:T(8,128)}, u32[]{:S(2)}) copy-start(f32[125,96]{0,1:T(8,128)} %param.9) | copy-start | bytes 144004
Sparse Core Ops, SparseCore 0:
  10.6 94.9 all-gather.1
  120.8 66.3 all-reduce.2
  271.9 139.6 all-reduce.4
where the time goes:
time: 467 us; the launch traced here: 463 us
  waiting for transfers between devices  305 us (65%)
  blocking collectives  105 us (22%)
  matrix products  29.9 us (6%)
  between operations  14.5 us (3%)
  local copies, waits for them, and re-layouts  6.24 us (1%)
    psum x1, waiting for transfers between devices, on_device(): fock = lax.psum(fock_part, 'aux')  140 us
    all_gather x1, waiting for transfers between devices, on_device(): lax.all_gather(pair_coeffs, 'aux', axis=0, tiled=True)  97.6 us
    all_to_all x1, blocking collectives, on_device(): lax.all_to_all(summed, 'aux', split_axis=0, concat_axis=1, tiled=True)  67.1 us
    psum x1, waiting for transfers between devices, on_device(): summed = lax.psum(partial_fit, ('orb', 'rdm'))  66.4 us
    psum x1, blocking collectives, on_device(): active_shift = lax.psum(active_part, ('orb', 'rdm'))  24.3 us
    dot_general x1, matrix products, on_device(): lax.dot_general(lax.all_gather(pair_coeffs, 'aux', axis=0, tiled=True), r...  15.1 us
    psum x1, blocking collectives, on_device(): total = lax.psum(squares, ('orb', 'rdm'))  13.3 us
    dot_general x1, matrix products, on_device(): jnp.einsum('qtu,qup->tp', fitted_three, b_tensor, precision=highest)  11.2 us
  transfers between devices with their start and end apart: 3, of which 3 were waited for; matrix products, arithmetic and copies ran while one was open for 0% of the time, Pallas kernels for 0%

commit v1 on v0

v1 whole, which is shorter than its diff:
```python
import functools
import math

import jax
import jax.numpy as jnp
from jax import lax
from jax.experimental import pallas as pl
from jax.experimental.pallas import tpu as pltpu
from jax.sharding import Mesh, PartitionSpec as P

NY, NZ, NX = 4, 8, 4
X = ("xh", "xl")
HIGH = lax.Precision.HIGH
HIGHEST = lax.Precision.HIGHEST


def shift(value, axis, size, step):
    return lax.ppermute(value, axis, [(i, (i + step) % size) for i in range(size)])


def swap_core(value):
    return lax.ppermute(value, "co", [(0, 1), (1, 0)])


def ring_gather(block, axis, size, tie):
    found = {0: block}
    half = size // 2
    for k in range(1, half):
        found[k] = shift(found[k - 1], axis, size, -1)
        found[size - k] = shift(found[(size - k + 1) % size], axis, size, 1)
    found[half] = shift(found[half - 1] + tie, axis, size, -1)
    return [found[k] for k in range(size)]


def split(value):
    head = value.astype(jnp.bfloat16)
    return head, (value - head.astype(jnp.float32)).astype(jnp.bfloat16)


def position():
    return lax.axis_index("y"), lax.axis_index("z"), lax.axis_index("xh") * 2 + lax.axis_index("xl"), lax.axis_index("co")


def product(left, right, dims):
    head, rest = left
    first, second = right
    total = lax.dot_general(head, first, dims, preferred_element_type=jnp.float32)
    total += lax.dot_general(head, second, dims, preferred_element_type=jnp.float32)
    return total + lax.dot_general(rest, first, dims, preferred_element_type=jnp.float32)


def pair_kernel(n_p, *refs):
    p_refs, r_refs = refs[:n_p], refs[n_p:-6]
    kept_ref, sent_ref, p_head, p_rest, r_head, r_rest = refs[-6:]
    _, _, x, core = position()
    half = kept_ref.shape[0]
    for k, ref in enumerate(p_refs):
        rows = ref.shape[0]
        start = ((k // NX) ^ core) * half + ((k % NX - x) & (NX - 1)) * rows
        place = pl.ds(pl.multiple_of(start, 16), rows)
        p_head[place, :], p_rest[place, :] = split(ref[...])
    start = 0
    for ref in r_refs:
        rows = ref.shape[0]
        r_head[start : start + rows, :], r_rest[start : start + rows, :] = split(ref[...])
        start += rows
    for low in range(0, start, 256):
        high = min(low + 256, start)
        pieces = (r_head[low:high, :], r_rest[low:high, :])
        total = product((p_head[...], p_rest[...]), pieces, (((1,), (1,)), ((), ())))
        kept_ref[:, low:high] = total[:half]
        sent_ref[:, low:high] = total[half:]


def pair_product(p_pieces, r_pieces):
    depth = p_pieces[0].shape[1]
    n_rows = sum(p.shape[0] for p in p_pieces)
    n_cols = sum(r.shape[0] for r in r_pieces)
    vmem = pl.BlockSpec(memory_space=pltpu.VMEM)
    shape = jax.ShapeDtypeStruct((n_rows // 2, n_cols), jnp.float32)
    return pl.pallas_call(
        functools.partial(pair_kernel, len(p_pieces)),
        out_shape=(shape, shape),
        in_specs=[vmem] * (len(p_pieces) + len(r_pieces)),
        out_specs=(vmem, vmem),
        scratch_shapes=[pltpu.VMEM((n, depth), jnp.bfloat16) for n in (n_rows, n_rows, n_cols, n_cols)],
        compiler_params=pltpu.CompilerParams(vmem_limit_bytes=20 * 2**20),
        cost_estimate=pl.CostEstimate(flops=1000, bytes_accessed=1000, transcendentals=0),
    )(*p_pieces, *r_pieces)


def join_kernel(*refs):
    chunks, (own_ref, after_ref, before_ref, low_ref, high_ref) = refs[:-5], refs[-5:]
    rows = own_ref.shape[0]
    start = 0
    for kept_ref, got_ref in zip(chunks[::2], chunks[1::2]):
        lanes = slice(start, start + kept_ref.shape[1])
        start = lanes.stop
        total = kept_ref[...] + got_ref[...]
        own_ref[:, lanes] = total[:rows]
        after_ref[:, lanes] = total[rows : 2 * rows]
        low_ref[:, lanes] = total[2 * rows : 2 * rows + rows // 2]
        high_ref[:, lanes] = total[2 * rows + rows // 2 : 3 * rows]
        before_ref[:, lanes] = total[3 * rows :]


def add_kernel(after_ref, up_ref, before_ref, down_ref, after_out, before_out):
    half = up_ref.shape[0]
    after_out[:half] = after_ref[:half] + up_ref[...]
    after_out[half:] = after_ref[half:]
    before_out[:half] = before_ref[:half]
    before_out[half:] = before_ref[half:] + down_ref[...]


def sum_over_x(chunks):
    rows = chunks[0].shape[0] // NX
    lanes = sum(chunk.shape[1] for chunk in chunks[::2])
    whole, part = (jax.ShapeDtypeStruct((n, lanes), jnp.float32) for n in (rows, rows // 2))
    small = pltpu.CompilerParams(vmem_limit_bytes=8 * 2**20)
    own, after, before, low, high = pl.pallas_call(
        join_kernel, out_shape=(whole, whole, whole, part, part), compiler_params=small
    )(*chunks)
    up, down = shift(low, X, NX, 1), shift(high, X, NX, -1)
    after, before = pl.pallas_call(add_kernel, out_shape=(whole, whole), compiler_params=small)(after, up, before, down)
    return own + shift(after, X, NX, 1) + shift(before, X, NX, -1)


def fock_kernel(sizes, nact, per_step, *refs):
    b_ref, out_ref, sorted_ref, acc_ref = refs[-4:]
    y, z, x, core = position()
    naux = b_ref.shape[0]
    steps = naux // per_step

    n_t = refs[0].shape[1] // nact // NY
    at = 0
    for g, size in enumerate(sizes):
        c, s = g // NX, g % NX
        zb = (z - ((x + s) & (NX - 1)) - NX * ((core + c) & 1)) & (NZ - 1)
        base = 0
        for ref in refs[at : at + size]:
            rows = ref.shape[0]
            for j, dy in enumerate((0, 1, 3, 2)):
                first = (((y + dy) & (NY - 1)) * NZ + zb) * n_t
                for t in range(n_t):
                    place = pl.ds(pl.multiple_of((first + t) * naux + base, 8), rows)
                    low = (j * n_t + t) * nact
                    sorted_ref[place, :] = ref[:, low : low + nact]
            base += rows
        at += size
    acc_ref[...] = jnp.zeros_like(acc_ref)

    def step(i, carry):
        total = acc_ref[...]
        for j in range(per_step):
            q = i * per_step + j
            head, rest = split(sorted_ref[pl.ds(q, nact, stride=naux), :])
            b_head, b_rest = split(b_ref[q])
            both = jnp.dot(jnp.concatenate([head, rest]), b_head, preferred_element_type=jnp.float32)
            total += jnp.dot(head, b_rest, preferred_element_type=jnp.float32) + both[:nact] + both[nact:]
        acc_ref[...] = total
        return carry

    lax.fori_loop(0, steps, step, 0)
    half, lanes = out_ref.shape[1:]
    norb = acc_ref.shape[1]
    for h in range(2):
        for j in range(NX):
            wide = min(lanes, norb - j * lanes)
            if wide < lanes:
                out_ref[h * NX + j] = jnp.zeros((half, lanes), jnp.float32)
            out_ref[h * NX + j, :, :wide] = acc_ref[h * half : (h + 1) * half, j * lanes : j * lanes + wide]


def fock_product(fitted, b_tensor, lanes):
    naux, nact, norb = b_tensor.shape
    per_step = 8
    flat = [piece for group in fitted for piece in group]
    vmem = pl.BlockSpec(memory_space=pltpu.VMEM)
    return pl.pallas_call(
        functools.partial(fock_kernel, [len(group) for group in fitted], nact, per_step),
        out_shape=jax.ShapeDtypeStruct((2 * NX, nact // 2, lanes), jnp.float32),
        in_specs=[vmem] * (len(flat) + 1),
        out_specs=vmem,
        scratch_shapes=[
            pltpu.VMEM((nact * naux, nact), jnp.float32),
            pltpu.VMEM((nact, norb), jnp.float32),
        ],
        compiler_params=pltpu.CompilerParams(vmem_limit_bytes=16 * 2**20),
    )(*flat, b_tensor)


def grad_kernel(tiles_ref, gen_ref, grad_ref, packed_ref):
    half, lanes = tiles_ref.shape[1:]
    nact, norb = grad_ref.shape
    for h in range(2):
        for j in range(NX):
            wide = min(lanes, norb - j * lanes)
            grad_ref[h * half : (h + 1) * half, j * lanes : j * lanes + wide] = 2.0 * tiles_ref[h * NX + j, :, :wide]
    grad = grad_ref[...]
    packed_ref[:nact, :] = product(split(grad), split(gen_ref[...]), (((1,), (0,)), ((), ())))
    rows, cols = packed_ref.shape
    packed_ref[nact:, :] = jnp.zeros((rows - nact, cols), jnp.float32) + jnp.sum(grad * grad)


def general_kernel(grad_ref, act_ref, out_ref):
    out_ref[...] = product(split(grad_ref[...].T), split(act_ref[...]), (((1,), (0,)), ((), ())))


def scale_kernel(step_scale, whole_scale, a_ref, b_ref, c_ref, d_ref, grad_ref, raw_ref, dir_ref, act_ref, gen_ref):
    total = (a_ref[...] + c_ref[...]) + (b_ref[...] + d_ref[...])
    nact = act_ref.shape[0]
    inverse = 1.0 / jnp.sqrt(total[nact : nact + 1, 0:1] + 1e-06)
    dir_ref[...] = (whole_scale * inverse) * grad_ref[...]
    act_ref[...] = (-step_scale * inverse) * total[:nact]
    gen_ref[...] = (step_scale * inverse) * raw_ref[...]


def tail(tiles, gen_coeffs, act_coeffs, norb):
    nact = act_coeffs.shape[1]
    nbas = gen_coeffs.shape[0]
    f32 = jnp.float32
    shape = jax.ShapeDtypeStruct
    small = pltpu.CompilerParams(vmem_limit_bytes=8 * 2**20)
    grad, packed = pl.pallas_call(
        grad_kernel, out_shape=(shape((nact, norb), f32), shape((nact + 8, nbas), f32)), compiler_params=small
    )(tiles, gen_coeffs.T)
    raw = pl.pallas_call(general_kernel, out_shape=shape((norb, nbas), f32), compiler_params=small)(grad, act_coeffs.T)
    packed = packed + swap_core(packed)
    others = [shift(packed, X, NX, s) for s in range(1, NX)]
    direction, active, general = pl.pallas_call(
        functools.partial(scale_kernel, math.sqrt(nact), math.sqrt(nact * norb * 2 * NX)),
        out_shape=(shape((nact, norb), f32), shape((nact, nbas), f32), shape((norb, nbas), f32)),
        compiler_params=small,
    )(packed, *others, grad, raw)
    return direction, active.T, general.T


def on_device(pair_coeffs, rdm, b_tensor, gen_coeffs, act_coeffs):
    naux, nact, norb = b_tensor.shape
    rows_tu = rdm.shape[0]
    nt = rows_tu // nact
    half = naux // 2
    ahead, behind = shift(rdm, "y", NY, -1), shift(rdm, "y", NY, 1)
    cut = rows_tu // 2
    lower, upper = ahead[:cut], behind[cut:]
    gathered = ring_gather(pair_coeffs, "z", NZ, 0.0 * (lower[0, 0] + upper[0, 0]))
    across = [shift(lower, "y", NY, -1), shift(upper, "y", NY, 1)]

    chunks = []
    for pieces in ([rdm, ahead, behind], across):
        kept, sent = pair_product(gathered, pieces)
        chunks += [kept, swap_core(sent)]
    total = sum_over_x(chunks)

    def rank(zz, xx, cc):
        return ((zz * 2 + xx // 2) * 2 + cc) * 2 + xx % 2

    pairs = [
        (rank(zz, xx, cc), rank((zz + xx + NX * cc) % NZ, xx, cc))
        for zz in range(NZ)
        for xx in range(NX)
        for cc in range(2)
    ]
    returned = lax.ppermute(total, ("z", "xh", "co", "xl"), pairs)

    after = shift(returned, X, NX, -1)
    before = shift(returned, X, NX, 1)
    far_low = shift(after[:half], X, NX, -1)
    far_high = shift(before[half:], X, NX, 1)
    mine = [[returned], [after], [far_low, far_high], [before]]
    theirs = [[swap_core(piece) for piece in group] for group in mine]

    lanes = 128 if norb > 128 else norb // NX
    tiles = fock_product(mine + theirs, b_tensor, lanes)
    piece = jnp.sum(lax.all_to_all(tiles, "z", split_axis=0, concat_axis=0, tiled=True), axis=0)
    piece = (piece + shift(piece, "y", NY, 2)) + (shift(piece, "y", NY, 1) + shift(piece, "y", NY, -1))
    tiles = lax.all_to_all(
        jnp.broadcast_to(piece[None], tiles.shape), "z", split_axis=0, concat_axis=0, tiled=True
    )
    return tail(tiles, gen_coeffs, act_coeffs, norb)


def solution(mesh):
    grid = Mesh(mesh.devices.reshape(NY, NZ, 2, 2, 2), ("y", "z", "xh", "co", "xl"))
    aux, cols = ("y", "z"), ("xh", "co", "xl")
    return jax.shard_map(
        on_device,
        mesh=grid,
        in_specs=(P(aux, cols), P(aux, cols), P(aux, None, cols), P(aux, cols), P(aux, None)),
        out_specs=(P(None, cols), P(aux, None), P(aux, cols)),
        check_vma=False,
    )
```

time: 467 us -> 156 us (0.33)
  waiting for transfers between devices: 305 us -> 53.2 us
  blocking collectives: 105 us -> 33.5 us
  starting transfers between devices: 0.12 us -> 52.1 us
  matrix products: 29.9 us -> 0 us
  Pallas kernels: 0 us -> 12.8 us
  between operations: 14.5 us -> 2.15 us
  local copies, waits for them, and re-layouts: 6.24 us -> 1.17 us
    psum x2 -> x0, waiting for transfers between devices: 206 us -> none  [the longest x1 140 us: on_device(): fock = lax.psum(fock_part, 'aux')]
    all_gather x1 -> x0, waiting for transfers between devices: 97.6 us -> none  [on_device(): lax.all_gather(pair_coeffs, 'aux', axis=0, tiled=True)]
    ppermute x0 -> x34, waiting for transfers between devices: none -> 53.2 us  [the longest x25 43.2 us: shift(): lax.ppermute(value, axis, [(i, (i + step) % size) for i in range(size)])]
    ppermute x0 -> x34, starting transfers between devices: none -> 52.1 us  [the longest x25 44.1 us: shift(): lax.ppermute(value, axis, [(i, (i + step) % size) for i in range(size)])]
    psum x2 -> x0, blocking collectives: 37.5 us -> none  [the longest x1 24.3 us: on_device(): active_shift = lax.psum(active_part, ('orb', 'rdm'))]
    all_to_all x1 -> x2, blocking collectives: 67.1 us -> 33.5 us  [the longest x1 21.3 us: on_device(): lax.all_to_all(tiles, 'z', split_axis=0, concat_axis=0, tiled=True)]
    dot_general x4 -> x0, matrix products: 29.9 us -> none  [the longest x1 15.1 us: on_device(): lax.dot_general(lax.all_gather(pair_coeffs, 'aux', axis=0, tiled=True), r...]
    pallas_call x0 -> x8, Pallas kernels: none -> 12.8 us  [the longest x1 5.62 us: fock_product(): pl.pallas_call(functools.partial(fock_kernel, [len(group) for group in fi...]
  transfers between devices with their start and end apart: 3 -> 34, of which waited for: 3 -> 20; matrix products, arithmetic and copies ran while one was open for 0% -> 1% of each run, Pallas kernels for 0% -> 4%
where the time goes in v1:
time: 156 us; the launch traced here: 155 us
  waiting for transfers between devices  53.2 us (34%)
  starting transfers between devices  52.1 us (33%)
  blocking collectives  33.5 us (21%)
  Pallas kernels  12.8 us (8%)
  between operations  2.15 us (1%)
    ppermute x25, starting transfers between devices, shift(): lax.ppermute(value, axis, [(i, (i + step) % size) for i in range(size)])  44.1 us
    ppermute x25, waiting for transfers between devices, shift(): lax.ppermute(value, axis, [(i, (i + step) % size) for i in range(size)])  43.2 us
    all_to_all x1, blocking collectives, on_device(): lax.all_to_all(tiles, 'z', split_axis=0, concat_axis=0, tiled=True)  21.3 us
    all_to_all x1, blocking collectives, on_device(): lax.all_to_all(jnp.broadcast_to(piece[None], tiles.shape), 'z', split_axi...  12.2 us
    ppermute x1, starting transfers between devices, on_device(): returned = lax.ppermute(total, ('z', 'xh', 'co', 'xl'), pairs)  6.53 us
    ppermute x1, waiting for transfers between devices, on_device(): returned = lax.ppermute(total, ('z', 'xh', 'co', 'xl'), pairs)  6.22 us
    pallas_call x1, Pallas kernels, fock_product(): pl.pallas_call(functools.partial(fock_kernel, [len(group) for group in fi...  5.62 us
    pallas_call x2, Pallas kernels, pair_product(): pl.pallas_call(functools.partial(pair_kernel, len(p_pieces)), out_shape=(...  5.52 us
  transfers between devices with their start and end apart: 34, of which 20 were waited for; matrix products, arithmetic and copies ran while one was open for 1% of the time, Pallas kernels for 4%

profile of v1, /device:TPU:6, one launch (start us, length us, event | category | flops | bytes accessed | tf_op | source)
XLA Modules:
  0.0 155.0 jit_solution(13473718759491077832)
XLA Ops:
  0.6 3.1 %collective-permute-start.3 = (f32[288,1152]{1,0:T(8,128)}, f32[288,1152]{1,0:T(8,128)S(1)}, u32[]{:S(2)}, u32[]{:S(2)}) collective-permute-start(f32[288,1152]{1,0:T(8,128)} %refs_8_.1), channel_id=1, source_target_pairs={{0,192},{64,0},{128,64},{192,128},{1,193},{65,1},{129,65},{193,129... | collective-permute-start | bytes 3981320 | tf_op jit(solution)/shard_map/ppermute | solution.py:18
  3.7 5.9 %collective-permute-start = (f32[48,1152]{1,0:T(8,128)}, f32[48,1152]{1,0:T(8,128)S(1)}, u32[]{:S(2)}, u32[]{:S(2)}) collective-permute-start(f32[48,1152]{1,0:T(8,128)} %refs_0_.3), channel_id=1, source_target_pairs={{0,56},{8,0},{16,8},{24,16},{32,24},{40,32},{48,40},{56,48},{1,57}... | collective-permute-start | bytes 663560 | tf_op jit(solution)/shard_map/ppermute | solution.py:18
  9.6 4.7 %collective-permute-done.refs_1_ = f32[48,1152]{1,0:T(8,128)S(1)} collective-permute-done((f32[48,1152]{1,0:T(8,128)}, f32[48,1152]{1,0:T(8,128)S(1)}, u32[]{:S(2)}, u32[]{:S(2)}) %collective-permute-start) | collective-permute-done | bytes 221216 | tf_op jit(solution)/shard_map/ppermute | solution.py:18
  14.3 3.6 %collective-permute-start.1 = (f32[48,1152]{1,0:T(8,128)S(1)}, f32[48,1152]{1,0:T(8,128)S(1)}, u32[]{:S(2)}, u32[]{:S(2)}) collective-permute-start(f32[48,1152]{1,0:T(8,128)S(1)} %collective-permute-done.refs_1_), channel_id=1, source_target_pairs={{0,56},{8,0},{16,8},{24,16},{32,24},{40,32},{48,40},{56,48},{1,57}... | collective-permute-start | bytes 663560 | tf_op jit(solution)/shard_map/ppermute | solution.py:18
  17.9 3.5 %collective-permute-done.1.refs_2_ = f32[48,1152]{1,0:T(8,128)S(1)} collective-permute-done((f32[48,1152]{1,0:T(8,128)S(1)}, f32[48,1152]{1,0:T(8,128)S(1)}, u32[]{:S(2)}, u32[]{:S(2)}) %collective-permute-start.1) | collective-permute-done | bytes 221216 | tf_op jit(solution)/shard_map/ppermute | solution.py:18
  21.4 3.7 %collective-permute-start.2 = (f32[48,1152]{1,0:T(8,128)S(1)}, f32[48,1152]{1,0:T(8,128)S(1)}, u32[]{:S(2)}, u32[]{:S(2)}) collective-permute-start(f32[48,1152]{1,0:T(8,128)S(1)} %collective-permute-done.1.refs_2_), channel_id=1, source_target_pairs={{0,56},{8,0},{16,8},{24,16},{32,24},{40,32},{48,40},{56,48},{1,57}... | collective-permute-start | bytes 663560 | tf_op jit(solution)/shard_map/ppermute | solution.py:18
  25.1 7.3 %collective-permute-done.3.refs_9_ = f32[288,1152]{1,0:T(8,128)S(1)} collective-permute-done((f32[288,1152]{1,0:T(8,128)}, f32[288,1152]{1,0:T(8,128)S(1)}, u32[]{:S(2)}, u32[]{:S(2)}) %collective-permute-start.3) | collective-permute-done | bytes 1327136 | tf_op jit(solution)/shard_map/ppermute | solution.py:18
  32.5 3.7 %collective-permute-start.10 = (f32[144,1152]{1,0:T(8,128)S(1)}, f32[144,1152]{1,0:T(8,128)S(1)}, u32[]{:S(2)}, u32[]{:S(2)}) collective-permute-start(f32[144,1152]{1,0:T(8,128)S(1)} %slice.28), channel_id=1, source_target_pairs={{0,192},{64,0},{128,64},{192,128},{1,193},{65,1},{129,65},{193,129... | collective-permute-start | bytes 1990664 | tf_op jit(solution)/shard_map/ppermute | solution.py:18
  36.3 0.5 slice.26
  36.8 0.5 slice.27
  38.7 5.9 %collective-permute-start.5 = (f32[48,1152]{1,0:T(8,128)S(1)}, f32[48,1152]{1,0:T(8,128)S(1)}, u32[]{:S(2)}, u32[]{:S(2)}) collective-permute-start(f32[48,1152]{1,0:T(8,128)S(1)} %broadcast_add_fusion), channel_id=1, source_target_pairs={{0,56},{8,0},{16,8},{24,16},{32,24},{40,32},{48,40},{56,48},{1,57}... | collective-permute-start | bytes 663560 | tf_op jit(solution)/shard_map/ppermute | solution.py:18
  44.6 3.5 %collective-permute-done.5.refs_4_ = f32[48,1152]{1,0:T(8,128)S(1)} collective-permute-done((f32[48,1152]{1,0:T(8,128)S(1)}, f32[48,1152]{1,0:T(8,128)S(1)}, u32[]{:S(2)}, u32[]{:S(2)}) %collective-permute-start.5) | collective-permute-done | bytes 221216 | tf_op jit(solution)/shard_map/ppermute | solution.py:18
  48.1 3.5 %shard_map.76 = (f32[192,864]{1,0:T(8,128)S(1)}, f32[192,864]{1,0:T(8,128)S(1)}) custom-call(f32[48,1152]{1,0:T(8,128)S(1)} %copy-done.2, f32[48,1152]{1,0:T(8,128)S(1)} %collective-permute-done.refs_1_, f32[48,1152]{1,0:T(8,128)S(1)} %collective-permute-done.1.refs_2_, f32[48,1152]{1,0:T(8,128)S(1)} %collective-permute-done.2.refs_3_, ...), custom_call_target="tpu_custom_call" | custom-call | flops 1000 | bytes 1000 | tf_op jit(solution)/shard_map/pallas_call | solution.py:81
  51.6 0.3 collective-permute-start.9
  51.9 1.1 collective-permute-done.11.refs_9_
  53.0 2.0 %shard_map.77 = (f32[192,288]{1,0:T(8,128)S(1)}, f32[192,288]{1,0:T(8,128)S(1)}) custom-call(f32[48,1152]{1,0:T(8,128)S(1)} %copy-done.2, f32[48,1152]{1,0:T(8,128)S(1)} %collective-permute-done.refs_1_, f32[48,1152]{1,0:T(8,128)S(1)} %collective-permute-done.1.refs_2_, f32[48,1152]{1,0:T(8,128)S(1)} %collective-permute-done.2.refs_3_, ...), custom_call_target="tpu_custom_call" | custom-call | flops 1000 | bytes 1000 | tf_op jit(solution)/shard_map/pallas_call | solution.py:81
  55.1 1.6 %collective-permute-done.12.refs_3_ = f32[192,288]{1,0:T(8,128)S(1)} collective-permute-done((f32[192,288]{1,0:T(8,128)S(1)}, f32[192,288]{1,0:T(8,128)S(1)}, u32[]{:S(2)}, u32[]{:S(2)}) %collective-permute-start.12) | collective-permute-done | bytes 221216 | tf_op jit(solution)/shard_map/ppermute | solution.py:22
  56.9 0.6 collective-permute-start.13
  57.4 1.5 collective-permute-start.14
  59.0 3.1 %collective-permute-done.13.up_ref = f32[24,1152]{1,0:T(8,128)S(1)} collective-permute-done((f32[24,1152]{1,0:T(8,128)S(1)}, f32[24,1152]{1,0:T(8,128)S(1)}, u32[]{:S(2)}, u32[]{:S(2)}) %collective-permute-start.13) | collective-permute-done | bytes 110624 | tf_op jit(solution)/shard_map/ppermute | solution.py:18
  62.0 1.4 collective-permute-done.14.down_ref
  63.5 0.4 collective-permute-start.15
  63.9 1.7 %collective-permute-start.16 = (f32[48,1152]{1,0:T(8,128)S(1)}, f32[48,1152]{1,0:T(8,128)S(1)}, u32[]{:S(2)}, u32[]{:S(2)}) collective-permute-start(f32[48,1152]{1,0:T(8,128)S(1)} %get-tuple-element.29), channel_id=1, source_target_pairs={{0,5},{1,0},{4,1},{5,4},{2,7},{3,2},{6,3},{7,6},{8,13},{9,8},{12,9... | collective-permute-start | bytes 663560 | tf_op jit(solution)/shard_map/ppermute | solution.py:18
  65.6 4.3 %collective-permute-done.15 = f32[48,1152]{1,0:T(8,128)S(1)} collective-permute-done((f32[48,1152]{1,0:T(8,128)S(1)}, f32[48,1152]{1,0:T(8,128)S(1)}, u32[]{:S(2)}, u32[]{:S(2)}) %collective-permute-start.15) | collective-permute-done | bytes 221216 | tf_op jit(solution)/shard_map/ppermute | solution.py:18
  69.9 1.5 collective-permute-done.16
  71.5 6.5 %collective-permute-start.17 = (f32[48,1152]{1,0:T(8,128)S(1)}, f32[48,1152]{1,0:T(8,128)S(1)}, u32[]{:S(2)}, u32[]{:S(2)}) collective-permute-start(f32[48,1152]{1,0:T(8,128)S(1)} %add_add_fusion), channel_id=1, source_target_pairs={{0,0},{2,34},{1,9},{3,43},{4,20},{6,54},{5,29},{7,63},{8,8},{10,42... | collective-permute-start | bytes 663560 | tf_op jit(solution)/shard_map/ppermute | solution.py:264
  78.0 6.2 %collective-permute-done.17.refs_0_ = f32[48,1152]{1,0:T(8,128)S(1)} collective-permute-done((f32[48,1152]{1,0:T(8,128)S(1)}, f32[48,1152]{1,0:T(8,128)S(1)}, u32[]{:S(2)}, u32[]{:S(2)}) %collective-permute-start.17) | collective-permute-done | bytes 221216 | tf_op jit(solution)/shard_map/ppermute | solution.py:264
  84.4 3.1 %collective-permute-start.20 = (f32[48,1152]{1,0:T(8,128)S(1)}, f32[48,1152]{1,0:T(8,128)S(1)}, u32[]{:S(2)}, u32[]{:S(2)}) collective-permute-start(f32[48,1152]{1,0:T(8,128)S(1)} %collective-permute-done.17.refs_0_), channel_id=1, source_target_pairs={{0,1},{1,4},{4,5},{5,0},{2,3},{3,6},{6,7},{7,2},{8,9},{9,12},{12,1... | collective-permute-start | bytes 663560 | tf_op jit(solution)/shard_map/ppermute | solution.py:18
  87.5 3.9 %collective-permute-done.18.refs_1_ = f32[48,1152]{1,0:T(8,128)S(1)} collective-permute-done((f32[48,1152]{1,0:T(8,128)S(1)}, f32[48,1152]{1,0:T(8,128)S(1)}, u32[]{:S(2)}, u32[]{:S(2)}) %collective-permute-start.18) | collective-permute-done | bytes 221216 | tf_op jit(solution)/shard_map/ppermute | solution.py:18
  91.5 3.3 %collective-permute-start.21 = (f32[24,1152]{1,0:T(8,128)S(1)}, f32[24,1152]{1,0:T(8,128)S(1)}, u32[]{:S(2)}, u32[]{:S(2)}) collective-permute-start(f32[24,1152]{1,0:T(8,128)S(1)} %slice.31), channel_id=1, source_target_pairs={{0,1},{1,4},{4,5},{5,0},{2,3},{3,6},{6,7},{7,2},{8,9},{9,12},{12,1... | collective-permute-start | bytes 331784 | tf_op jit(solution)/shard_map/ppermute | solution.py:18
  94.8 0.5 collective-permute-start.26
  95.3 2.1 %collective-permute-done.19.refs_2_ = f32[24,1152]{1,0:T(8,128)S(1)} collective-permute-done((f32[24,1152]{1,0:T(8,128)S(1)}, f32[24,1152]{1,0:T(8,128)S(1)}, u32[]{:S(2)}, u32[]{:S(2)}) %collective-permute-start.19) | collective-permute-done | bytes 110624 | tf_op jit(solution)/shard_map/ppermute | solution.py:18
  97.4 0.5 collective-permute-start.25
  98.0 0.8 collective-permute-done.24.refs_7_
  98.9 5.6 %shard_map.80 = f32[8,48,128]{2,1,0:T(8,128)S(1)} custom-call(f32[48,1152]{1,0:T(8,128)S(1)} %collective-permute-done.17.refs_0_, f32[48,1152]{1,0:T(8,128)S(1)} %collective-permute-done.18.refs_1_, f32[24,1152]{1,0:T(8,128)S(1)} %collective-permute-done.19.refs_2_, f32[24,1152]{1,0:T(8,128)S(1)} %collective-permute-done.21.refs_3_, ...), custom_call_target="tpu_custom_call" | custom-call | tf_op jit(solution)/shard_map/pallas_call | solution.py:179
  104.6 21.3 %all_to_all.10 = f32[8,48,128]{2,1,0:T(8,128)S(1)} all-to-all(f32[8,48,128]{2,1,0:T(8,128)S(1)} %shard_map.80), channel_id=1, replica_groups=mesh['y'=4,'z'=8,'xh'=2,'co'=2,'xl'=2] {'z'}, dimensions={0} | all-to-all | bytes 393216 | tf_op jit(solution)/shard_map/all_to_all | solution.py:275
  126.0 1.0 collective-permute-start.28
  127.0 2.3 %collective-permute-start.29 = (f32[48,128]{1,0:T(8,128)S(1)}, f32[48,128]{1,0:T(8,128)S(1)}, u32[]{:S(2)}, u32[]{:S(2)}) collective-permute-start(f32[48,128]{1,0:T(8,128)S(1)} %reduce_sum.9), channel_id=1, source_target_pairs={{0,192},{64,0},{128,64},{192,128},{1,193},{65,1},{129,65},{193,129... | collective-permute-start | bytes 73736 | tf_op jit(solution)/shard_map/ppermute | solution.py:18
  129.3 2.1 %collective-permute-done.27 = f32[48,128]{1,0:T(8,128)S(1)} collective-permute-done((f32[48,128]{1,0:T(8,128)S(1)}, f32[48,128]{1,0:T(8,128)S(1)}, u32[]{:S(2)}, u32[]{:S(2)}) %collective-permute-start.27) | collective-permute-done | bytes 24608 | tf_op jit(solution)/shard_map/ppermute | solution.py:18
  131.4 12.2 %all_to_all.11.tiles_ref = f32[8,48,128]{2,1,0:T(8,128)S(1)} all-to-all(f32[8,48,128]{2,1,0:T(8,128)S(1)} %broadcast_in_dim.2), channel_id=1, replica_groups=mesh['y'=4,'z'=8,'xh'=2,'co'=2,'xl'=2] {'z'}, dimensions={0} | all-to-all | bytes 393216 | tf_op jit(solution)/shard_map/all_to_all | solution.py:277
  143.6 0.3 shard_map.81
  144.0 1.2 collective-permute-done.30
  145.2 3.0 %collective-permute-start.31 = (f32[104,125]{1,0:T(8,128)S(1)}, f32[104,125]{1,0:T(8,128)S(1)}, u32[]{:S(2)}, u32[]{:S(2)}) collective-permute-start(f32[104,125]{1,0:T(8,128)S(1)} %add.36.a_ref), channel_id=1, source_target_pairs={{0,1},{1,4},{4,5},{5,0},{2,3},{3,6},{6,7},{7,2},{8,9},{9,12},{12,1... | collective-permute-start | bytes 156008 | tf_op jit(solution)/shard_map/ppermute | solution.py:18
  148.2 1.0 collective-permute-start.33
  149.2 0.3 shard_map.82.raw_ref
  149.5 1.3 collective-permute-done.31.b_ref
  150.8 3.2 %collective-permute-done.32.c_ref = f32[104,125]{1,0:T(8,128)S(1)} collective-permute-done((f32[104,125]{1,0:T(8,128)S(1)}, f32[104,125]{1,0:T(8,128)S(1)}, u32[]{:S(2)}, u32[]{:S(2)}) %collective-permute-start.32) | collective-permute-done | bytes 52032 | tf_op jit(solution)/shard_map/ppermute | solution.py:18
  154.2 0.8 shard_map.83
  (52 shorter events, 1.5 us)
Async XLA Ops:
  0.6 47.5 %copy-start.1 = (f32[288,1152]{1,0:T(8,128)S(1)}, f32[288,1152]{1,0:T(8,128)}, u32[]{:S(2)}) copy-start(f32[288,1152]{1,0:T(8,128)} %refs_8_.1) | copy-start | bytes 3981316
  0.6 47.5 %copy-start.2 = (f32[48,1152]{1,0:T(8,128)S(1)}, f32[48,1152]{1,0:T(8,128)}, u32[]{:S(2)}) copy-start(f32[48,1152]{1,0:T(8,128)} %refs_0_.3) | copy-start | bytes 663556
  0.6 31.8 %collective-permute-start.3 = (f32[288,1152]{1,0:T(8,128)}, f32[288,1152]{1,0:T(8,128)S(1)}, u32[]{:S(2)}, u32[]{:S(2)}) collective-permute-start(f32[288,1152]{1,0:T(8,128)} %refs_8_.1), channel_id=1, source_target_pairs={{0,192},{64,0},{128,64},{192,128},{1,193},{65,1},{129,65},{193,129... | collective-permute-start | bytes 3981320 | tf_op jit(solution)/shard_map/ppermute | solution.py:18
  3.7 32.4 %collective-permute-start.4 = (f32[288,1152]{1,0:T(8,128)}, f32[288,1152]{1,0:T(8,128)S(1)}, u32[]{:S(2)}, u32[]{:S(2)}) collective-permute-start(f32[288,1152]{1,0:T(8,128)} %refs_8_.1), channel_id=1, source_target_pairs={{0,64},{64,128},{128,192},{192,0},{1,65},{65,129},{129,193},{193,1... | collective-permute-start | bytes 3981320 | tf_op jit(solution)/shard_map/ppermute | solution.py:18
  3.7 10.6 %collective-permute-start = (f32[48,1152]{1,0:T(8,128)}, f32[48,1152]{1,0:T(8,128)S(1)}, u32[]{:S(2)}, u32[]{:S(2)}) collective-permute-start(f32[48,1152]{1,0:T(8,128)} %refs_0_.3), channel_id=1, source_target_pairs={{0,56},{8,0},{16,8},{24,16},{32,24},{40,32},{48,40},{56,48},{1,57}... | collective-permute-start | bytes 663560 | tf_op jit(solution)/shard_map/ppermute | solution.py:18
  9.6 8.3 %collective-permute-start.6 = (f32[48,1152]{1,0:T(8,128)}, f32[48,1152]{1,0:T(8,128)S(1)}, u32[]{:S(2)}, u32[]{:S(2)}) collective-permute-start(f32[48,1152]{1,0:T(8,128)} %refs_0_.3), channel_id=1, source_target_pairs={{0,8},{8,16},{16,24},{24,32},{32,40},{40,48},{48,56},{56,0},{1,9},... | collective-permute-start | bytes 663560 | tf_op jit(solution)/shard_map/ppermute | solution.py:18
  14.3 7.1 %collective-permute-start.1 = (f32[48,1152]{1,0:T(8,128)S(1)}, f32[48,1152]{1,0:T(8,128)S(1)}, u32[]{:S(2)}, u32[]{:S(2)}) collective-permute-start(f32[48,1152]{1,0:T(8,128)S(1)} %collective-permute-done.refs_1_), channel_id=1, source_target_pairs={{0,56},{8,0},{16,8},{24,16},{32,24},{40,32},{48,40},{56,48},{1,57}... | collective-permute-start | bytes 663560 | tf_op jit(solution)/shard_map/ppermute | solution.py:18
  17.9 7.2 %collective-permute-start.7 = (f32[48,1152]{1,0:T(8,128)S(1)}, f32[48,1152]{1,0:T(8,128)S(1)}, u32[]{:S(2)}, u32[]{:S(2)}) collective-permute-start(f32[48,1152]{1,0:T(8,128)S(1)} %collective-permute-done.6.refs_7_), channel_id=1, source_target_pairs={{0,8},{8,16},{16,24},{24,32},{32,40},{40,48},{48,56},{56,0},{1,9},... | collective-permute-start | bytes 663560 | tf_op jit(solution)/shard_map/ppermute | solution.py:18
  21.4 17.2 %collective-permute-start.2 = (f32[48,1152]{1,0:T(8,128)S(1)}, f32[48,1152]{1,0:T(8,128)S(1)}, u32[]{:S(2)}, u32[]{:S(2)}) collective-permute-start(f32[48,1152]{1,0:T(8,128)S(1)} %collective-permute-done.1.refs_2_), channel_id=1, source_target_pairs={{0,56},{8,0},{16,8},{24,16},{32,24},{40,32},{48,40},{56,48},{1,57}... | collective-permute-start | bytes 663560 | tf_op jit(solution)/shard_map/ppermute | solution.py:18
  25.1 19.5 %collective-permute-start.8 = (f32[48,1152]{1,0:T(8,128)S(1)}, f32[48,1152]{1,0:T(8,128)S(1)}, u32[]{:S(2)}, u32[]{:S(2)}) collective-permute-start(f32[48,1152]{1,0:T(8,128)S(1)} %collective-permute-done.7.refs_6_), channel_id=1, source_target_pairs={{0,8},{8,16},{16,24},{24,32},{32,40},{40,48},{48,56},{56,0},{1,9},... | collective-permute-start | bytes 663560 | tf_op jit(solution)/shard_map/ppermute | solution.py:18
  32.5 19.4 %collective-permute-start.10 = (f32[144,1152]{1,0:T(8,128)S(1)}, f32[144,1152]{1,0:T(8,128)S(1)}, u32[]{:S(2)}, u32[]{:S(2)}) collective-permute-start(f32[144,1152]{1,0:T(8,128)S(1)} %slice.28), channel_id=1, source_target_pairs={{0,192},{64,0},{128,64},{192,128},{1,193},{65,1},{129,65},{193,129... | collective-permute-start | bytes 1990664 | tf_op jit(solution)/shard_map/ppermute | solution.py:18
  36.2 16.8 %collective-permute-start.11 = (f32[144,1152]{1,0:T(8,128)S(1)}, f32[144,1152]{1,0:T(8,128)S(1)}, u32[]{:S(2)}, u32[]{:S(2)}) collective-permute-start(f32[144,1152]{1,0:T(8,128)S(1)} %slice.29), channel_id=1, source_target_pairs={{0,64},{64,128},{128,192},{192,0},{1,65},{65,129},{129,193},{193,1... | collective-permute-start | bytes 1990664 | tf_op jit(solution)/shard_map/ppermute | solution.py:18
  38.7 9.5 %collective-permute-start.5 = (f32[48,1152]{1,0:T(8,128)S(1)}, f32[48,1152]{1,0:T(8,128)S(1)}, u32[]{:S(2)}, u32[]{:S(2)}) collective-permute-start(f32[48,1152]{1,0:T(8,128)S(1)} %broadcast_add_fusion), channel_id=1, source_target_pairs={{0,56},{8,0},{16,8},{24,16},{32,24},{40,32},{48,40},{56,48},{1,57}... | collective-permute-start | bytes 663560 | tf_op jit(solution)/shard_map/ppermute | solution.py:18
  48.1 50.8 %copy-start = (f32[48,96,500]{2,1,0:T(8,128)S(1)}, f32[48,96,500]{2,1,0:T(8,128)}, u32[]{:S(2)}) copy-start(f32[48,96,500]{2,1,0:T(8,128)} %refs_10_.1) | copy-start | bytes 27648004
  51.6 5.1 %collective-permute-start.9 = (f32[192,864]{1,0:T(8,128)S(1)}, f32[192,864]{1,0:T(8,128)S(1)}, u32[]{:S(2)}, u32[]{:S(2)}) collective-permute-start(f32[192,864]{1,0:T(8,128)S(1)} %get-tuple-element.20), channel_id=1, source_target_pairs={{0,2},{2,0},{1,3},{3,1},{4,6},{6,4},{5,7},{7,5},{8,10},{10,8},{9,1... | collective-permute-start | bytes 1990664 | tf_op jit(solution)/shard_map/ppermute | solution.py:22
  55.0 1.7 %collective-permute-start.12 = (f32[192,288]{1,0:T(8,128)S(1)}, f32[192,288]{1,0:T(8,128)S(1)}, u32[]{:S(2)}, u32[]{:S(2)}) collective-permute-start(f32[192,288]{1,0:T(8,128)S(1)} %get-tuple-element.22), channel_id=1, source_target_pairs={{0,2},{2,0},{1,3},{3,1},{4,6},{6,4},{5,7},{7,5},{8,10},{10,8},{9,1... | collective-permute-start | bytes 663560 | tf_op jit(solution)/shard_map/ppermute | solution.py:22
  56.9 5.2 %collective-permute-start.13 = (f32[24,1152]{1,0:T(8,128)S(1)}, f32[24,1152]{1,0:T(8,128)S(1)}, u32[]{:S(2)}, u32[]{:S(2)}) collective-permute-start(f32[24,1152]{1,0:T(8,128)S(1)} %get-tuple-element.25), channel_id=1, source_target_pairs={{0,1},{1,4},{4,5},{5,0},{2,3},{3,6},{6,7},{7,2},{8,9},{9,12},{12,1... | collective-permute-start | bytes 331784 | tf_op jit(solution)/shard_map/ppermute | solution.py:18
  57.4 6.0 %collective-permute-start.14 = (f32[24,1152]{1,0:T(8,128)S(1)}, f32[24,1152]{1,0:T(8,128)S(1)}, u32[]{:S(2)}, u32[]{:S(2)}) collective-permute-start(f32[24,1152]{1,0:T(8,128)S(1)} %get-tuple-element.27), channel_id=1, source_target_pairs={{0,5},{1,0},{4,1},{5,4},{2,7},{3,2},{6,3},{7,6},{8,13},{9,8},{12,9... | collective-permute-start | bytes 331784 | tf_op jit(solution)/shard_map/ppermute | solution.py:18
  63.5 6.4 %collective-permute-start.15 = (f32[48,1152]{1,0:T(8,128)S(1)}, f32[48,1152]{1,0:T(8,128)S(1)}, u32[]{:S(2)}, u32[]{:S(2)}) collective-permute-start(f32[48,1152]{1,0:T(8,128)S(1)} %get-tuple-element.28), channel_id=1, source_target_pairs={{0,1},{1,4},{4,5},{5,0},{2,3},{3,6},{6,7},{7,2},{8,9},{9,12},{12,1... | collective-permute-start | bytes 663560 | tf_op jit(solution)/shard_map/ppermute | solution.py:18
  63.9 7.6 %collective-permute-start.16 = (f32[48,1152]{1,0:T(8,128)S(1)}, f32[48,1152]{1,0:T(8,128)S(1)}, u32[]{:S(2)}, u32[]{:S(2)}) collective-permute-start(f32[48,1152]{1,0:T(8,128)S(1)} %get-tuple-element.29), channel_id=1, source_target_pairs={{0,5},{1,0},{4,1},{5,4},{2,7},{3,2},{6,3},{7,6},{8,13},{9,8},{12,9... | collective-permute-start | bytes 663560 | tf_op jit(solution)/shard_map/ppermute | solution.py:18
  71.5 12.8 %collective-permute-start.17 = (f32[48,1152]{1,0:T(8,128)S(1)}, f32[48,1152]{1,0:T(8,128)S(1)}, u32[]{:S(2)}, u32[]{:S(2)}) collective-permute-start(f32[48,1152]{1,0:T(8,128)S(1)} %add_add_fusion), channel_id=1, source_target_pairs={{0,0},{2,34},{1,9},{3,43},{4,20},{6,54},{5,29},{7,63},{8,8},{10,42... | collective-permute-start | bytes 663560 | tf_op jit(solution)/shard_map/ppermute | solution.py:264
  84.2 7.1 %collective-permute-start.18 = (f32[48,1152]{1,0:T(8,128)S(1)}, f32[48,1152]{1,0:T(8,128)S(1)}, u32[]{:S(2)}, u32[]{:S(2)}) collective-permute-start(f32[48,1152]{1,0:T(8,128)S(1)} %collective-permute-done.17.refs_0_), channel_id=1, source_target_pairs={{0,5},{1,0},{4,1},{5,4},{2,7},{3,2},{6,3},{7,6},{8,13},{9,8},{12,9... | collective-permute-start | bytes 663560 | tf_op jit(solution)/shard_map/ppermute | solution.py:18
  84.4 7.1 %collective-permute-start.20 = (f32[48,1152]{1,0:T(8,128)S(1)}, f32[48,1152]{1,0:T(8,128)S(1)}, u32[]{:S(2)}, u32[]{:S(2)}) collective-permute-start(f32[48,1152]{1,0:T(8,128)S(1)} %collective-permute-done.17.refs_0_), channel_id=1, source_target_pairs={{0,1},{1,4},{4,5},{5,0},{2,3},{3,6},{6,7},{7,2},{8,9},{9,12},{12,1... | collective-permute-start | bytes 663560 | tf_op jit(solution)/shard_map/ppermute | solution.py:18
  87.5 10.5 %collective-permute-start.22 = (f32[48,1152]{1,0:T(8,128)S(1)}, f32[48,1152]{1,0:T(8,128)S(1)}, u32[]{:S(2)}, u32[]{:S(2)}) collective-permute-start(f32[48,1152]{1,0:T(8,128)S(1)} %collective-permute-done.17.refs_0_), channel_id=1, source_target_pairs={{0,2},{2,0},{1,3},{3,1},{4,6},{6,4},{5,7},{7,5},{8,10},{10,8},{9,1... | collective-permute-start | bytes 663560 | tf_op jit(solution)/shard_map/ppermute | solution.py:22
  91.4 6.0 %collective-permute-start.19 = (f32[24,1152]{1,0:T(8,128)S(1)}, f32[24,1152]{1,0:T(8,128)S(1)}, u32[]{:S(2)}, u32[]{:S(2)}) collective-permute-start(f32[24,1152]{1,0:T(8,128)S(1)} %slice.30), channel_id=1, source_target_pairs={{0,5},{1,0},{4,1},{5,4},{2,7},{3,2},{6,3},{7,6},{8,13},{9,8},{12,9... | collective-permute-start | bytes 331784 | tf_op jit(solution)/shard_map/ppermute | solution.py:18
  91.5 5.9 %collective-permute-start.21 = (f32[24,1152]{1,0:T(8,128)S(1)}, f32[24,1152]{1,0:T(8,128)S(1)}, u32[]{:S(2)}, u32[]{:S(2)}) collective-permute-start(f32[24,1152]{1,0:T(8,128)S(1)} %slice.31), channel_id=1, source_target_pairs={{0,1},{1,4},{4,5},{5,0},{2,3},{3,6},{6,7},{7,2},{8,9},{9,12},{12,1... | collective-permute-start | bytes 331784 | tf_op jit(solution)/shard_map/ppermute | solution.py:18
  94.8 4.1 %collective-permute-start.23 = (f32[48,1152]{1,0:T(8,128)S(1)}, f32[48,1152]{1,0:T(8,128)S(1)}, u32[]{:S(2)}, u32[]{:S(2)}) collective-permute-start(f32[48,1152]{1,0:T(8,128)S(1)} %collective-permute-done.18.refs_1_), channel_id=1, source_target_pairs={{0,2},{2,0},{1,3},{3,1},{4,6},{6,4},{5,7},{7,5},{8,10},{10,8},{9,1... | collective-permute-start | bytes 663560 | tf_op jit(solution)/shard_map/ppermute | solution.py:22
  94.8 4.1 %collective-permute-start.26 = (f32[48,1152]{1,0:T(8,128)S(1)}, f32[48,1152]{1,0:T(8,128)S(1)}, u32[]{:S(2)}, u32[]{:S(2)}) collective-permute-start(f32[48,1152]{1,0:T(8,128)S(1)} %collective-permute-done.20.refs_4_), channel_id=1, source_target_pairs={{0,2},{2,0},{1,3},{3,1},{4,6},{6,4},{5,7},{7,5},{8,10},{10,8},{9,1... | collective-permute-start | bytes 663560 | tf_op jit(solution)/shard_map/ppermute | solution.py:22
  97.4 1.3 collective-permute-start.24
  97.4 1.5 collective-permute-start.25
  104.5 39.1 %copy-start.3 = (f32[125,500]{0,1:T(8,128)S(1)}, f32[125,500]{0,1:T(8,128)}, u32[]{:S(2)}) copy-start(f32[125,500]{0,1:T(8,128)} %param.8) | copy-start | bytes 750004
  104.6 44.6 %copy-start.4 = (f32[125,96]{0,1:T(8,128)S(1)}, f32[125,96]{0,1:T(8,128)}, u32[]{:S(2)}) copy-start(f32[125,96]{0,1:T(8,128)} %param.9) | copy-start | bytes 144004
  125.9 5.5 %collective-permute-start.27 = (f32[48,128]{1,0:T(8,128)S(1)}, f32[48,128]{1,0:T(8,128)S(1)}, u32[]{:S(2)}, u32[]{:S(2)}) collective-permute-start(f32[48,128]{1,0:T(8,128)S(1)} %reduce_sum.9), channel_id=1, source_target_pairs={{0,128},{64,192},{128,0},{192,64},{1,129},{65,193},{129,1},{193,65... | collective-permute-start | bytes 73736 | tf_op jit(solution)/shard_map/ppermute | solution.py:18
  126.0 5.4 %collective-permute-start.28 = (f32[48,128]{1,0:T(8,128)S(1)}, f32[48,128]{1,0:T(8,128)S(1)}, u32[]{:S(2)}, u32[]{:S(2)}) collective-permute-start(f32[48,128]{1,0:T(8,128)S(1)} %reduce_sum.9), channel_id=1, source_target_pairs={{0,64},{64,128},{128,192},{192,0},{1,65},{65,129},{129,193},{193,1... | collective-permute-start | bytes 73736 | tf_op jit(solution)/shard_map/ppermute | solution.py:18
  127.0 4.4 %collective-permute-start.29 = (f32[48,128]{1,0:T(8,128)S(1)}, f32[48,128]{1,0:T(8,128)S(1)}, u32[]{:S(2)}, u32[]{:S(2)}) collective-permute-start(f32[48,128]{1,0:T(8,128)S(1)} %reduce_sum.9), channel_id=1, source_target_pairs={{0,192},{64,0},{128,64},{192,128},{1,193},{65,1},{129,65},{193,129... | collective-permute-start | bytes 73736 | tf_op jit(solution)/shard_map/ppermute | solution.py:18
  143.9 1.3 collective-permute-start.30
  145.2 5.6 %collective-permute-start.31 = (f32[104,125]{1,0:T(8,128)S(1)}, f32[104,125]{1,0:T(8,128)S(1)}, u32[]{:S(2)}, u32[]{:S(2)}) collective-permute-start(f32[104,125]{1,0:T(8,128)S(1)} %add.36.a_ref), channel_id=1, source_target_pairs={{0,1},{1,4},{4,5},{5,0},{2,3},{3,6},{6,7},{7,2},{8,9},{9,12},{12,1... | collective-permute-start | bytes 156008 | tf_op jit(solution)/shard_map/ppermute | solution.py:18
  148.2 5.7 %collective-permute-start.32 = (f32[104,125]{1,0:T(8,128)S(1)}, f32[104,125]{1,0:T(8,128)S(1)}, u32[]{:S(2)}, u32[]{:S(2)}) collective-permute-start(f32[104,125]{1,0:T(8,128)S(1)} %add.36.a_ref), channel_id=1, source_target_pairs={{0,4},{1,5},{4,0},{5,1},{2,6},{3,7},{6,2},{7,3},{8,12},{9,13},{12,... | collective-permute-start | bytes 156008 | tf_op jit(solution)/shard_map/ppermute | solution.py:18
  148.2 5.9 %collective-permute-start.33 = (f32[104,125]{1,0:T(8,128)S(1)}, f32[104,125]{1,0:T(8,128)S(1)}, u32[]{:S(2)}, u32[]{:S(2)}) collective-permute-start(f32[104,125]{1,0:T(8,128)S(1)} %add.36.a_ref), channel_id=1, source_target_pairs={{0,5},{1,0},{4,1},{5,4},{2,7},{3,2},{6,3},{7,6},{8,13},{9,8},{12,9... | collective-permute-start | bytes 156008 | tf_op jit(solution)/shard_map/ppermute | solution.py:18

commit v2 on v1

--- a/solution.py
+++ b/solution.py
@@ -9,9 +9,9 @@
 from jax.sharding import Mesh, PartitionSpec as P
 
 NY, NZ, NX = 4, 8, 4
+TURN = 2
 X = ("xh", "xl")
-HIGH = lax.Precision.HIGH
-HIGHEST = lax.Precision.HIGHEST
+SMALL = pltpu.CompilerParams(vmem_limit_bytes=8 * 2**20)
 
 
 def shift(value, axis, size, step):
@@ -22,14 +22,8 @@
     return lax.ppermute(value, "co", [(0, 1), (1, 0)])
 
 
-def ring_gather(block, axis, size, tie):
-    found = {0: block}
-    half = size // 2
-    for k in range(1, half):
-        found[k] = shift(found[k - 1], axis, size, -1)
-        found[size - k] = shift(found[(size - k + 1) % size], axis, size, 1)
-    found[half] = shift(found[half - 1] + tie, axis, size, -1)
-    return [found[k] for k in range(size)]
+def swap(value, axis, size, mask):
+    return lax.ppermute(value, axis, [(i, i ^ mask) for i in range(size)])
 
 
 def split(value):
@@ -49,44 +43,46 @@
     return total + lax.dot_general(rest, first, dims, preferred_element_type=jnp.float32)
 
 
-def pair_kernel(n_p, *refs):
-    p_refs, r_refs = refs[:n_p], refs[n_p:-6]
-    kept_ref, sent_ref, p_head, p_rest, r_head, r_rest = refs[-6:]
+def pair_kernel(n_p, fresh, *refs):
+    p_head, p_rest = refs[-2:]
+    p_refs = refs[:n_p]
+    if fresh:
+        r_refs, (kept_ref, sent_ref, r_head, r_rest) = refs[n_p:-6], refs[-6:-2]
+        start = 0
+        for ref in r_refs:
+            rows = ref.shape[0]
+            r_head[start : start + rows, :], r_rest[start : start + rows, :] = split(ref[...])
+            start += rows
+    else:
+        r_head, r_rest, kept_ref, sent_ref = refs[n_p:-2]
     _, _, x, core = position()
-    half = kept_ref.shape[0]
+    half, n_cols = kept_ref.shape
     for k, ref in enumerate(p_refs):
         rows = ref.shape[0]
         start = ((k // NX) ^ core) * half + ((k % NX - x) & (NX - 1)) * rows
         place = pl.ds(pl.multiple_of(start, 16), rows)
         p_head[place, :], p_rest[place, :] = split(ref[...])
-    start = 0
-    for ref in r_refs:
-        rows = ref.shape[0]
-        r_head[start : start + rows, :], r_rest[start : start + rows, :] = split(ref[...])
-        start += rows
-    for low in range(0, start, 256):
-        high = min(low + 256, start)
+    for low in range(0, n_cols, 256):
+        high = min(low + 256, n_cols)
         pieces = (r_head[low:high, :], r_rest[low:high, :])
         total = product((p_head[...], p_rest[...]), pieces, (((1,), (1,)), ((), ())))
         kept_ref[:, low:high] = total[:half]
         sent_ref[:, low:high] = total[half:]
 
 
-def pair_product(p_pieces, r_pieces):
+def pair_product(p_pieces, rows, fresh):
     depth = p_pieces[0].shape[1]
     n_rows = sum(p.shape[0] for p in p_pieces)
-    n_cols = sum(r.shape[0] for r in r_pieces)
-    vmem = pl.BlockSpec(memory_space=pltpu.VMEM)
+    n_cols = sum(r.shape[0] for r in rows) if fresh else rows[0].shape[0]
     shape = jax.ShapeDtypeStruct((n_rows // 2, n_cols), jnp.float32)
+    parts = jax.ShapeDtypeStruct((n_cols, depth), jnp.bfloat16)
     return pl.pallas_call(
-        functools.partial(pair_kernel, len(p_pieces)),
-        out_shape=(shape, shape),
-        in_specs=[vmem] * (len(p_pieces) + len(r_pieces)),
-        out_specs=(vmem, vmem),
-        scratch_shapes=[pltpu.VMEM((n, depth), jnp.bfloat16) for n in (n_rows, n_rows, n_cols, n_cols)],
-        compiler_params=pltpu.CompilerParams(vmem_limit_bytes=20 * 2**20),
+        functools.partial(pair_kernel, len(p_pieces), fresh),
+        out_shape=(shape, shape) + ((parts, parts) if fresh else ()),
+        scratch_shapes=[pltpu.VMEM((n_rows, depth), jnp.bfloat16)] * 2,
+        compiler_params=pltpu.CompilerParams(vmem_limit_bytes=16 * 2**20),
         cost_estimate=pl.CostEstimate(flops=1000, bytes_accessed=1000, transcendentals=0),
-    )(*p_pieces, *r_pieces)
+    )(*p_pieces, *rows)
 
 
 def join_kernel(*refs):
@@ -112,17 +108,32 @@
     before_out[half:] = before_ref[half:] + down_ref[...]
 
 
+def sides_kernel(own_ref, one_ref, two_ref, first_ref, second_ref):
+    total = own_ref[...] + one_ref[...] + two_ref[...]
+    lanes = first_ref.shape[1]
+    first_ref[...] = total[:, :lanes]
+    second_ref[...] = total[:, lanes:]
+
+
+def lanes_kernel(first_ref, second_ref, out_ref):
+    lanes = first_ref.shape[1]
+    out_ref[:, :lanes] = first_ref[...]
+    out_ref[:, lanes:] = second_ref[...]
+
+
 def sum_over_x(chunks):
     rows = chunks[0].shape[0] // NX
     lanes = sum(chunk.shape[1] for chunk in chunks[::2])
     whole, part = (jax.ShapeDtypeStruct((n, lanes), jnp.float32) for n in (rows, rows // 2))
-    small = pltpu.CompilerParams(vmem_limit_bytes=8 * 2**20)
     own, after, before, low, high = pl.pallas_call(
-        join_kernel, out_shape=(whole, whole, whole, part, part), compiler_params=small
+        join_kernel, out_shape=(whole, whole, whole, part, part), compiler_params=SMALL
     )(*chunks)
     up, down = shift(low, X, NX, 1), shift(high, X, NX, -1)
-    after, before = pl.pallas_call(add_kernel, out_shape=(whole, whole), compiler_params=small)(after, up, before, down)
-    return own + shift(after, X, NX, 1) + shift(before, X, NX, -1)
+    after, before = pl.pallas_call(add_kernel, out_shape=(whole, whole), compiler_params=SMALL)(after, up, before, down)
+    side = jax.ShapeDtypeStruct((rows, lanes // 2), jnp.float32)
+    return pl.pallas_call(sides_kernel, out_shape=(side, side), compiler_params=SMALL)(
+        own, shift(after, X, NX, 1), shift(before, X, NX, -1)
+    )
 
 
 def fock_kernel(sizes, nact, per_step, *refs):
@@ -139,8 +150,9 @@
         base = 0
         for ref in refs[at : at + size]:
             rows = ref.shape[0]
-            for j, dy in enumerate((0, 1, 3, 2)):
-                first = (((y + dy) & (NY - 1)) * NZ + zb) * n_t
+            for j, mask in enumerate((0, 1, 3, 2)):
+                turned = zb if j < 2 else (zb - TURN) & (NZ - 1)
+                first = ((y ^ mask) * NZ + turned) * n_t
                 for t in range(n_t):
                     place = pl.ds(pl.multiple_of((first + t) * naux + base, 8), rows)
                     low = (j * n_t + t) * nact
@@ -220,48 +232,59 @@
     nbas = gen_coeffs.shape[0]
     f32 = jnp.float32
     shape = jax.ShapeDtypeStruct
-    small = pltpu.CompilerParams(vmem_limit_bytes=8 * 2**20)
     grad, packed = pl.pallas_call(
-        grad_kernel, out_shape=(shape((nact, norb), f32), shape((nact + 8, nbas), f32)), compiler_params=small
+        grad_kernel, out_shape=(shape((nact, norb), f32), shape((nact + 8, nbas), f32)), compiler_params=SMALL
     )(tiles, gen_coeffs.T)
-    raw = pl.pallas_call(general_kernel, out_shape=shape((norb, nbas), f32), compiler_params=small)(grad, act_coeffs.T)
+    raw = pl.pallas_call(general_kernel, out_shape=shape((norb, nbas), f32), compiler_params=SMALL)(grad, act_coeffs.T)
     packed = packed + swap_core(packed)
-    others = [shift(packed, X, NX, s) for s in range(1, NX)]
+    others = [swap(packed, X, NX, mask) for mask in (1, 2, 3)]
     direction, active, general = pl.pallas_call(
         functools.partial(scale_kernel, math.sqrt(nact), math.sqrt(nact * norb * 2 * NX)),
         out_shape=(shape((nact, norb), f32), shape((nact, nbas), f32), shape((norb, nbas), f32)),
-        compiler_params=small,
+        compiler_params=SMALL,
     )(packed, *others, grad, raw)
     return direction, active.T, general.T
 
 
 def on_device(pair_coeffs, rdm, b_tensor, gen_coeffs, act_coeffs):
     naux, nact, norb = b_tensor.shape
-    rows_tu = rdm.shape[0]
-    nt = rows_tu // nact
     half = naux // 2
-    ahead, behind = shift(rdm, "y", NY, -1), shift(rdm, "y", NY, 1)
-    cut = rows_tu // 2
-    lower, upper = ahead[:cut], behind[cut:]
-    gathered = ring_gather(pair_coeffs, "z", NZ, 0.0 * (lower[0, 0] + upper[0, 0]))
-    across = [shift(lower, "y", NY, -1), shift(upper, "y", NY, 1)]
-
-    chunks = []
-    for pieces in ([rdm, ahead, behind], across):
-        kept, sent = pair_product(gathered, pieces)
-        chunks += [kept, swap_core(sent)]
-    total = sum_over_x(chunks)
-
-    def rank(zz, xx, cc):
-        return ((zz * 2 + xx // 2) * 2 + cc) * 2 + xx % 2
-
-    pairs = [
-        (rank(zz, xx, cc), rank((zz + xx + NX * cc) % NZ, xx, cc))
-        for zz in range(NZ)
-        for xx in range(NX)
-        for cc in range(2)
-    ]
-    returned = lax.ppermute(total, ("z", "xh", "co", "xl"), pairs)
+    rows = [rdm, swap(rdm, "y", NY, 1)]
+    near = {0: pair_coeffs}
+    far = {0: swap(pair_coeffs, "y", NY, 3)}
+    for k in range(1, NZ // 2):
+        for found in (near, far):
+            if found is near or k < 3:
+                found[k] = shift(found[k - 1], "z", NZ, -1)
+                found[NZ - k] = shift(found[(NZ - k + 1) % NZ], "z", NZ, 1)
+    near[4] = shift(near[3], "z", NZ, -1)
+    for k in (3, 5, 4):
+        far[k] = swap(near[k], "y", NY, 3)
+
+    kept, sent, *rows = pair_product([near[k] for k in range(NZ)], rows, True)
+    chunks = [kept, swap_core(sent)]
+    kept, sent = pair_product([far[(k + TURN) % NZ] for k in range(NZ)], rows, False)
+    chunks += [kept, swap_core(sent)]
+    first, second = sum_over_x(chunks)
+
+    def rank(yy, zz, xx, cc):
+        return (((yy * NZ + zz % NZ) * 2 + xx // 2) * 2 + cc) * 2 + xx % 2
+
+    def send_home(value, mask, turn):
+        pairs = [
+            (rank(yy, zz, xx, cc), rank(yy ^ mask, zz + xx + NX * cc + turn, xx, cc))
+            for yy in range(NY)
+            for zz in range(NZ)
+            for xx in range(NX)
+            for cc in range(2)
+        ]
+        return lax.ppermute(value, ("y", "z", "xh", "co", "xl"), pairs)
+
+    returned = pl.pallas_call(
+        lanes_kernel,
+        out_shape=jax.ShapeDtypeStruct((naux, 2 * first.shape[1]), first.dtype),
+        compiler_params=SMALL,
+    )(send_home(first, 0, 0), send_home(second, 3, TURN))
 
     after = shift(returned, X, NX, -1)
     before = shift(returned, X, NX, 1)
@@ -273,7 +296,7 @@
     lanes = 128 if norb > 128 else norb // NX
     tiles = fock_product(mine + theirs, b_tensor, lanes)
     piece = jnp.sum(lax.all_to_all(tiles, "z", split_axis=0, concat_axis=0, tiled=True), axis=0)
-    piece = (piece + shift(piece, "y", NY, 2)) + (shift(piece, "y", NY, 1) + shift(piece, "y", NY, -1))
+    piece = (piece + swap(piece, "y", NY, 2)) + (swap(piece, "y", NY, 1) + swap(piece, "y", NY, 3))
     tiles = lax.all_to_all(
         jnp.broadcast_to(piece[None], tiles.shape), "z", split_axis=0, concat_axis=0, tiled=True
     )

time: 156 us -> 155 us (level)
  starting transfers between devices: 52.1 us -> 61.6 us
  blocking collectives: 33.5 us -> 28.2 us
  waiting for transfers between devices: 53.2 us -> 48.8 us
    ppermute x1 -> x13, starting transfers between devices: 6.53 us -> 26.2 us  [the longest x11 18.3 us: swap(): return lax.ppermute(value, axis, [(i, i ^ mask) for i in range(size)])]
    ppermute x25 -> x19, waiting for transfers between devices: 43.2 us -> 27.2 us  [shift(): lax.ppermute(value, axis, [(i, (i + step) % size) for i in range(size)])]
    ppermute x1 -> x13, waiting for transfers between devices: 6.22 us -> 17.4 us  [the longest x11 11.5 us: swap(): return lax.ppermute(value, axis, [(i, i ^ mask) for i in range(size)])]
    ppermute x25 -> x19, starting transfers between devices: 44.1 us -> 33.7 us  [shift(): lax.ppermute(value, axis, [(i, (i + step) % size) for i in range(size)])]
    all_to_all x1, blocking collectives: 21.3 us -> 16 us  [on_device(): lax.all_to_all(tiles, 'z', split_axis=0, concat_axis=0, tiled=True)]
    unnamed x10, local copies, waits for them, and re-layouts: 0.02 us -> 2.27 us
    pallas_call x3 -> x5, Pallas kernels: 5.56 us -> 5.67 us  [the longest x2 5.42 us: pair_product(): pl.pallas_call(functools.partial(pair_kernel, len(p_pieces), fresh), out_...]
  transfers between devices with their start and end apart: 34 -> 40, of which waited for: 20 -> 25; matrix products, arithmetic and copies ran while one was open for 1% -> 0% of each run, Pallas kernels for 4% -> 2%
where the time goes in v2:
time: 155 us
  starting transfers between devices  61.6 us (40%)
  waiting for transfers between devices  48.8 us (31%)
  blocking collectives  28.2 us (18%)
  Pallas kernels  12.9 us (8%)
  local copies, waits for them, and re-layouts  2.31 us (1%)
    ppermute x19, starting transfers between devices, shift(): lax.ppermute(value, axis, [(i, (i + step) % size) for i in range(size)])  33.7 us
    ppermute x19, waiting for transfers between devices, shift(): lax.ppermute(value, axis, [(i, (i + step) % size) for i in range(size)])  27.2 us
    ppermute x11, starting transfers between devices, swap(): return lax.ppermute(value, axis, [(i, i ^ mask) for i in range(size)])  18.3 us
    all_to_all x1, blocking collectives, on_device(): lax.all_to_all(tiles, 'z', split_axis=0, concat_axis=0, tiled=True)  16 us
    all_to_all x1, blocking collectives, on_device(): lax.all_to_all(jnp.broadcast_to(piece[None], tiles.shape), 'z', split_axi...  12.2 us
    ppermute x11, waiting for transfers between devices, swap(): return lax.ppermute(value, axis, [(i, i ^ mask) for i in range(size)])  11.5 us
    ppermute x2, starting transfers between devices, send_home(): return lax.ppermute(value, ('y', 'z', 'xh', 'co', 'xl'), pairs)  7.93 us
    ppermute x2, waiting for transfers between devices, send_home(): return lax.ppermute(value, ('y', 'z', 'xh', 'co', 'xl'), pairs)  5.98 us
  transfers between devices with their start and end apart: 40, of which 25 were waited for; matrix products, arithmetic and copies ran while one was open for 0% of the time, Pallas kernels for 2%

profile of v2, /device:TPU:6, one launch (start us, length us, event | category | flops | bytes accessed | tf_op | source)
XLA Modules:
  0.0 154.7 jit_solution(7920559815304459861)
XLA Ops:
  0.6 1.7 %collective-permute-start.7 = (f32[288,1152]{1,0:T(8,128)}, f32[288,1152]{1,0:T(8,128)S(1)}, u32[]{:S(2)}, u32[]{:S(2)}) collective-permute-start(f32[288,1152]{1,0:T(8,128)} %refs_8_.1), channel_id=1, source_target_pairs={{0,64},{64,0},{128,192},{192,128},{1,65},{65,1},{129,193},{193,129... | collective-permute-start | bytes 3981320 | tf_op jit(solution)/shard_map/ppermute | solution.py:26
  2.3 5.9 %collective-permute-start = (f32[48,1152]{1,0:T(8,128)}, f32[48,1152]{1,0:T(8,128)S(1)}, u32[]{:S(2)}, u32[]{:S(2)}) collective-permute-start(f32[48,1152]{1,0:T(8,128)} %refs_0_.1), channel_id=1, source_target_pairs={{0,56},{8,0},{16,8},{24,16},{32,24},{40,32},{48,40},{56,48},{1,57}... | collective-permute-start | bytes 663560 | tf_op jit(solution)/shard_map/ppermute | solution.py:18
  8.2 4.7 %collective-permute-done.refs_1_ = f32[48,1152]{1,0:T(8,128)S(1)} collective-permute-done((f32[48,1152]{1,0:T(8,128)}, f32[48,1152]{1,0:T(8,128)S(1)}, u32[]{:S(2)}, u32[]{:S(2)}) %collective-permute-start) | collective-permute-done | bytes 221216 | tf_op jit(solution)/shard_map/ppermute | solution.py:18
  12.9 3.6 %collective-permute-start.1 = (f32[48,1152]{1,0:T(8,128)S(1)}, f32[48,1152]{1,0:T(8,128)S(1)}, u32[]{:S(2)}, u32[]{:S(2)}) collective-permute-start(f32[48,1152]{1,0:T(8,128)S(1)} %collective-permute-done.refs_1_), channel_id=1, source_target_pairs={{0,56},{8,0},{16,8},{24,16},{32,24},{40,32},{48,40},{56,48},{1,57}... | collective-permute-start | bytes 663560 | tf_op jit(solution)/shard_map/ppermute | solution.py:18
  16.5 2.2 %collective-permute-start.9 = (f32[48,1152]{1,0:T(8,128)}, f32[48,1152]{1,0:T(8,128)S(1)}, u32[]{:S(2)}, u32[]{:S(2)}) collective-permute-start(f32[48,1152]{1,0:T(8,128)} %refs_0_.1), channel_id=1, source_target_pairs={{0,192},{64,128},{128,64},{192,0},{1,193},{65,129},{129,65},{193,1... | collective-permute-start | bytes 663560 | tf_op jit(solution)/shard_map/ppermute | solution.py:26
  18.6 1.3 collective-permute-done.1.refs_2_
  20.0 3.7 %collective-permute-start.2 = (f32[48,1152]{1,0:T(8,128)S(1)}, f32[48,1152]{1,0:T(8,128)S(1)}, u32[]{:S(2)}, u32[]{:S(2)}) collective-permute-start(f32[48,1152]{1,0:T(8,128)S(1)} %collective-permute-done.1.refs_2_), channel_id=1, source_target_pairs={{0,56},{8,0},{16,8},{24,16},{32,24},{40,32},{48,40},{56,48},{1,57}... | collective-permute-start | bytes 663560 | tf_op jit(solution)/shard_map/ppermute | solution.py:18
  23.9 2.0 %collective-permute-start.15 = (f32[48,1152]{1,0:T(8,128)S(1)}, f32[48,1152]{1,0:T(8,128)S(1)}, u32[]{:S(2)}, u32[]{:S(2)}) collective-permute-start(f32[48,1152]{1,0:T(8,128)S(1)} %collective-permute-done.9.refs_6_), channel_id=1, source_target_pairs={{0,8},{8,16},{16,24},{24,32},{32,40},{40,48},{48,56},{56,0},{1,9},... | collective-permute-start | bytes 663560 | tf_op jit(solution)/shard_map/ppermute | solution.py:18
  26.4 3.0 %collective-permute-done.2.refs_3_ = f32[48,1152]{1,0:T(8,128)S(1)} collective-permute-done((f32[48,1152]{1,0:T(8,128)S(1)}, f32[48,1152]{1,0:T(8,128)S(1)}, u32[]{:S(2)}, u32[]{:S(2)}) %collective-permute-start.2) | collective-permute-done | bytes 221216 | tf_op jit(solution)/shard_map/ppermute | solution.py:18
  29.4 3.7 %collective-permute-start.3 = (f32[48,1152]{1,0:T(8,128)S(1)}, f32[48,1152]{1,0:T(8,128)S(1)}, u32[]{:S(2)}, u32[]{:S(2)}) collective-permute-start(f32[48,1152]{1,0:T(8,128)S(1)} %collective-permute-done.2.refs_3_), channel_id=1, source_target_pairs={{0,56},{8,0},{16,8},{24,16},{32,24},{40,32},{48,40},{56,48},{1,57}... | collective-permute-start | bytes 663560 | tf_op jit(solution)/shard_map/ppermute | solution.py:18
  33.1 1.0 collective-permute-done.10.refs_7_
  34.1 3.7 %collective-permute-start.11 = (f32[48,1152]{1,0:T(8,128)S(1)}, f32[48,1152]{1,0:T(8,128)S(1)}, u32[]{:S(2)}, u32[]{:S(2)}) collective-permute-start(f32[48,1152]{1,0:T(8,128)S(1)} %collective-permute-done.10.refs_7_), channel_id=1, source_target_pairs={{0,56},{8,0},{16,8},{24,16},{32,24},{40,32},{48,40},{56,48},{1,57}... | collective-permute-start | bytes 663560 | tf_op jit(solution)/shard_map/ppermute | solution.py:18
  37.8 2.3 %collective-permute-start.12 = (f32[48,1152]{1,0:T(8,128)S(1)}, f32[48,1152]{1,0:T(8,128)S(1)}, u32[]{:S(2)}, u32[]{:S(2)}) collective-permute-start(f32[48,1152]{1,0:T(8,128)S(1)} %collective-permute-done.2.refs_3_), channel_id=1, source_target_pairs={{0,192},{64,128},{128,64},{192,0},{1,193},{65,129},{129,65},{193,1... | collective-permute-start | bytes 663560 | tf_op jit(solution)/shard_map/ppermute | solution.py:26
  40.1 1.1 collective-permute-start.14
  41.1 2.2 %collective-permute-start.13 = (f32[48,1152]{1,0:T(8,128)S(1)}, f32[48,1152]{1,0:T(8,128)S(1)}, u32[]{:S(2)}, u32[]{:S(2)}) collective-permute-start(f32[48,1152]{1,0:T(8,128)S(1)} %collective-permute-done.3.refs_4_), channel_id=1, source_target_pairs={{0,192},{64,128},{128,64},{192,0},{1,193},{65,129},{129,65},{193,1... | collective-permute-start | bytes 663560 | tf_op jit(solution)/shard_map/ppermute | solution.py:26
  43.3 1.3 copy-done.1
  44.7 0.9 copy-done.3
  45.6 2.7 %shard_map.76 = (f32[192,576]{1,0:T(8,128)S(1)}, f32[192,576]{1,0:T(8,128)S(1)}, bf16[576,1152]{1,0:T(8,128)(2,1)S(1)}, bf16[576,1152]{1,0:T(8,128)(2,1)S(1)}) custom-call(f32[48,1152]{1,0:T(8,128)S(1)} %copy-done.3, f32[48,1152]{1,0:T(8,128)S(1)} %collective-permute-done.refs_1_, f32[48,1152]{1,0:T(8,128)S(1)} %collective-permute-done.1.refs_2_, ...), custom_call_target="tpu_custom_call" | custom-call | flops 1000 | bytes 1000 | tf_op jit(solution)/shard_map/pallas_call | solution.py:79
  48.4 2.1 %collective-permute-done.13.refs_2_ = f32[48,1152]{1,0:T(8,128)S(1)} collective-permute-done((f32[48,1152]{1,0:T(8,128)S(1)}, f32[48,1152]{1,0:T(8,128)S(1)}, u32[]{:S(2)}, u32[]{:S(2)}) %collective-permute-start.13) | collective-permute-done | bytes 221216 | tf_op jit(solution)/shard_map/ppermute | solution.py:26
  50.5 2.7 %shard_map.77 = (f32[192,576]{1,0:T(8,128)S(1)}, f32[192,576]{1,0:T(8,128)S(1)}) custom-call(f32[48,1152]{1,0:T(8,128)S(1)} %collective-permute-done.11.refs_0_, f32[48,1152]{1,0:T(8,128)S(1)} %collective-permute-done.12.refs_1_, f32[48,1152]{1,0:T(8,128)S(1)} %collective-permute-done.13.refs_2_, f32[48,1152]{1,0:T(8,128)S(1)} %collective-permute-done.14.refs_3_, ...), custom_call_target="tpu_custom_call" | custom-call | flops 1000 | bytes 1000 | tf_op jit(solution)/shard_map/pallas_call | solution.py:79
  53.8 1.4 collective-permute-done.17.refs_3_
  56.6 1.6 %collective-permute-start.19 = (f32[24,1152]{1,0:T(8,128)S(1)}, f32[24,1152]{1,0:T(8,128)S(1)}, u32[]{:S(2)}, u32[]{:S(2)}) collective-permute-start(f32[24,1152]{1,0:T(8,128)S(1)} %get-tuple-element.33), channel_id=1, source_target_pairs={{0,5},{1,0},{4,1},{5,4},{2,7},{3,2},{6,3},{7,6},{8,13},{9,8},{12,9... | collective-permute-start | bytes 331784 | tf_op jit(solution)/shard_map/ppermute | solution.py:18
  58.1 3.1 %collective-permute-done.18.up_ref = f32[24,1152]{1,0:T(8,128)S(1)} collective-permute-done((f32[24,1152]{1,0:T(8,128)S(1)}, f32[24,1152]{1,0:T(8,128)S(1)}, u32[]{:S(2)}, u32[]{:S(2)}) %collective-permute-start.18) | collective-permute-done | bytes 110624 | tf_op jit(solution)/shard_map/ppermute | solution.py:18
  61.2 1.4 collective-permute-done.19.down_ref
  63.0 1.7 %collective-permute-start.21 = (f32[48,1152]{1,0:T(8,128)S(1)}, f32[48,1152]{1,0:T(8,128)S(1)}, u32[]{:S(2)}, u32[]{:S(2)}) collective-permute-start(f32[48,1152]{1,0:T(8,128)S(1)} %get-tuple-element.35), channel_id=1, source_target_pairs={{0,5},{1,0},{4,1},{5,4},{2,7},{3,2},{6,3},{7,6},{8,13},{9,8},{12,9... | collective-permute-start | bytes 663560 | tf_op jit(solution)/shard_map/ppermute | solution.py:18
  64.8 4.3 %collective-permute-done.20.one_ref = f32[48,1152]{1,0:T(8,128)S(1)} collective-permute-done((f32[48,1152]{1,0:T(8,128)S(1)}, f32[48,1152]{1,0:T(8,128)S(1)}, u32[]{:S(2)}, u32[]{:S(2)}) %collective-permute-start.20) | collective-permute-done | bytes 221216 | tf_op jit(solution)/shard_map/ppermute | solution.py:18
  69.1 1.5 collective-permute-done.21.two_ref
  70.7 3.6 %collective-permute-start.22 = (f32[48,576]{1,0:T(8,128)S(1)}, f32[48,576]{1,0:T(8,128)S(1)}, u32[]{:S(2)}, u32[]{:S(2)}) collective-permute-start(f32[48,576]{1,0:T(8,128)S(1)} %get-tuple-element.36), channel_id=1, source_target_pairs={{0,0},{2,34},{1,9},{3,43},{4,20},{6,54},{5,29},{7,63},{8,8},{10,42... | collective-permute-start | bytes 331784 | tf_op jit(solution)/shard_map/ppermute | solution.py:281
  74.4 4.3 %collective-permute-start.23 = (f32[48,576]{1,0:T(8,128)S(1)}, f32[48,576]{1,0:T(8,128)S(1)}, u32[]{:S(2)}, u32[]{:S(2)}) collective-permute-start(f32[48,576]{1,0:T(8,128)S(1)} %get-tuple-element.37), channel_id=1, source_target_pairs={{0,208},{2,242},{1,217},{3,251},{4,228},{6,198},{5,237},{7,207},{8... | collective-permute-start | bytes 331784 | tf_op jit(solution)/shard_map/ppermute | solution.py:281
  78.7 3.6 %collective-permute-done.22.first_ref = f32[48,576]{1,0:T(8,128)S(1)} collective-permute-done((f32[48,576]{1,0:T(8,128)S(1)}, f32[48,576]{1,0:T(8,128)S(1)}, u32[]{:S(2)}, u32[]{:S(2)}) %collective-permute-start.22) | collective-permute-done | bytes 110624 | tf_op jit(solution)/shard_map/ppermute | solution.py:281
  82.3 2.4 %collective-permute-done.23.second_ref = f32[48,576]{1,0:T(8,128)S(1)} collective-permute-done((f32[48,576]{1,0:T(8,128)S(1)}, f32[48,576]{1,0:T(8,128)S(1)}, u32[]{:S(2)}, u32[]{:S(2)}) %collective-permute-start.23) | collective-permute-done | bytes 110624 | tf_op jit(solution)/shard_map/ppermute | solution.py:281
  84.8 3.2 %collective-permute-start.26 = (f32[48,1152]{1,0:T(8,128)S(1)}, f32[48,1152]{1,0:T(8,128)S(1)}, u32[]{:S(2)}, u32[]{:S(2)}) collective-permute-start(f32[48,1152]{1,0:T(8,128)S(1)} %shard_map.81.refs_0_), channel_id=1, source_target_pairs={{0,1},{1,4},{4,5},{5,0},{2,3},{3,6},{6,7},{7,2},{8,9},{9,12},{12,1... | collective-permute-start | bytes 663560 | tf_op jit(solution)/shard_map/ppermute | solution.py:18
  88.1 4.1 %collective-permute-done.24.refs_1_ = f32[48,1152]{1,0:T(8,128)S(1)} collective-permute-done((f32[48,1152]{1,0:T(8,128)S(1)}, f32[48,1152]{1,0:T(8,128)S(1)}, u32[]{:S(2)}, u32[]{:S(2)}) %collective-permute-start.24) | collective-permute-done | bytes 221216 | tf_op jit(solution)/shard_map/ppermute | solution.py:18
  92.5 3.3 %collective-permute-start.27 = (f32[24,1152]{1,0:T(8,128)S(1)}, f32[24,1152]{1,0:T(8,128)S(1)}, u32[]{:S(2)}, u32[]{:S(2)}) collective-permute-start(f32[24,1152]{1,0:T(8,128)S(1)} %slice.9), channel_id=1, source_target_pairs={{0,1},{1,4},{4,5},{5,0},{2,3},{3,6},{6,7},{7,2},{8,9},{9,12},{12,1... | collective-permute-start | bytes 331784 | tf_op jit(solution)/shard_map/ppermute | solution.py:18
  96.3 2.1 %collective-permute-done.25.refs_2_ = f32[24,1152]{1,0:T(8,128)S(1)} collective-permute-done((f32[24,1152]{1,0:T(8,128)S(1)}, f32[24,1152]{1,0:T(8,128)S(1)}, u32[]{:S(2)}, u32[]{:S(2)}) %collective-permute-start.25) | collective-permute-done | bytes 110624 | tf_op jit(solution)/shard_map/ppermute | solution.py:18
  99.0 0.8 collective-permute-done.30.refs_7_
  99.9 5.6 %shard_map.82 = f32[8,48,128]{2,1,0:T(8,128)S(1)} custom-call(f32[48,1152]{1,0:T(8,128)S(1)} %shard_map.81.refs_0_, f32[48,1152]{1,0:T(8,128)S(1)} %collective-permute-done.24.refs_1_, f32[24,1152]{1,0:T(8,128)S(1)} %collective-permute-done.25.refs_2_, f32[24,1152]{1,0:T(8,128)S(1)} %collective-permute-done.27.refs_3_, ...), custom_call_target="tpu_custom_call" | custom-call | tf_op jit(solution)/shard_map/pallas_call | solution.py:191
  105.6 16.0 %all_to_all.10 = f32[8,48,128]{2,1,0:T(8,128)S(1)} all-to-all(f32[8,48,128]{2,1,0:T(8,128)S(1)} %shard_map.82), channel_id=1, replica_groups=mesh['y'=4,'z'=8,'xh'=2,'co'=2,'xl'=2] {'z'}, dimensions={0} | all-to-all | bytes 393216 | tf_op jit(solution)/shard_map/all_to_all | solution.py:298
  121.6 0.7 collective-permute-start.33
  122.3 2.9 %collective-permute-start.34 = (f32[48,128]{1,0:T(8,128)S(1)}, f32[48,128]{1,0:T(8,128)S(1)}, u32[]{:S(2)}, u32[]{:S(2)}) collective-permute-start(f32[48,128]{1,0:T(8,128)S(1)} %reduce_sum.9), channel_id=1, source_target_pairs={{0,64},{64,0},{128,192},{192,128},{1,65},{65,1},{129,193},{193,129... | collective-permute-start | bytes 73736 | tf_op jit(solution)/shard_map/ppermute | solution.py:26
  125.8 1.2 collective-permute-done.33
  127.2 3.0 %collective-permute-done.35 = f32[48,128]{1,0:T(8,128)S(1)} collective-permute-done((f32[48,128]{1,0:T(8,128)S(1)}, f32[48,128]{1,0:T(8,128)S(1)}, u32[]{:S(2)}, u32[]{:S(2)}) %collective-permute-start.35) | collective-permute-done | bytes 24608 | tf_op jit(solution)/shard_map/ppermute | solution.py:26
  130.3 12.2 %all_to_all.11.tiles_ref = f32[8,48,128]{2,1,0:T(8,128)S(1)} all-to-all(f32[8,48,128]{2,1,0:T(8,128)S(1)} %broadcast_in_dim.2), channel_id=1, replica_groups=mesh['y'=4,'z'=8,'xh'=2,'co'=2,'xl'=2] {'z'}, dimensions={0} | all-to-all | bytes 393216 | tf_op jit(solution)/shard_map/all_to_all | solution.py:300
  142.8 1.2 collective-permute-done.36
  144.1 4.4 %collective-permute-start.38 = (f32[104,125]{1,0:T(8,128)S(1)}, f32[104,125]{1,0:T(8,128)S(1)}, u32[]{:S(2)}, u32[]{:S(2)}) collective-permute-start(f32[104,125]{1,0:T(8,128)S(1)} %add.15.a_ref), channel_id=1, source_target_pairs={{0,4},{1,5},{4,0},{5,1},{2,6},{3,7},{6,2},{7,3},{8,12},{9,13},{12,... | collective-permute-start | bytes 156008 | tf_op jit(solution)/shard_map/ppermute | solution.py:26
  149.2 2.3 %collective-permute-done.38.c_ref = f32[104,125]{1,0:T(8,128)S(1)} collective-permute-done((f32[104,125]{1,0:T(8,128)S(1)}, f32[104,125]{1,0:T(8,128)S(1)}, u32[]{:S(2)}, u32[]{:S(2)}) %collective-permute-start.38) | collective-permute-done | bytes 52032 | tf_op jit(solution)/shard_map/ppermute | solution.py:26
  151.5 2.4 %collective-permute-done.39.d_ref = f32[104,125]{1,0:T(8,128)S(1)} collective-permute-done((f32[104,125]{1,0:T(8,128)S(1)}, f32[104,125]{1,0:T(8,128)S(1)}, u32[]{:S(2)}, u32[]{:S(2)}) %collective-permute-start.39) | collective-permute-done | bytes 52032 | tf_op jit(solution)/shard_map/ppermute | solution.py:26
  153.9 0.8 shard_map.85
  (60 shorter events, 7.0 us)
Async XLA Ops:
  0.6 40.5 %collective-permute-start.7 = (f32[288,1152]{1,0:T(8,128)}, f32[288,1152]{1,0:T(8,128)S(1)}, u32[]{:S(2)}, u32[]{:S(2)}) collective-permute-start(f32[288,1152]{1,0:T(8,128)} %refs_8_.1), channel_id=1, source_target_pairs={{0,64},{64,0},{128,192},{192,128},{1,65},{65,1},{129,193},{193,129... | collective-permute-start | bytes 3981320 | tf_op jit(solution)/shard_map/ppermute | solution.py:26
  2.3 10.6 %collective-permute-start = (f32[48,1152]{1,0:T(8,128)}, f32[48,1152]{1,0:T(8,128)S(1)}, u32[]{:S(2)}, u32[]{:S(2)}) collective-permute-start(f32[48,1152]{1,0:T(8,128)} %refs_0_.1), channel_id=1, source_target_pairs={{0,56},{8,0},{16,8},{24,16},{32,24},{40,32},{48,40},{56,48},{1,57}... | collective-permute-start | bytes 663560 | tf_op jit(solution)/shard_map/ppermute | solution.py:18
  8.2 10.5 %collective-permute-start.4 = (f32[48,1152]{1,0:T(8,128)}, f32[48,1152]{1,0:T(8,128)S(1)}, u32[]{:S(2)}, u32[]{:S(2)}) collective-permute-start(f32[48,1152]{1,0:T(8,128)} %refs_0_.1), channel_id=1, source_target_pairs={{0,8},{8,16},{16,24},{24,32},{32,40},{40,48},{48,56},{56,0},{1,9},... | collective-permute-start | bytes 663560 | tf_op jit(solution)/shard_map/ppermute | solution.py:18
  12.9 7.1 %collective-permute-start.1 = (f32[48,1152]{1,0:T(8,128)S(1)}, f32[48,1152]{1,0:T(8,128)S(1)}, u32[]{:S(2)}, u32[]{:S(2)}) collective-permute-start(f32[48,1152]{1,0:T(8,128)S(1)} %collective-permute-done.refs_1_), channel_id=1, source_target_pairs={{0,56},{8,0},{16,8},{24,16},{32,24},{40,32},{48,40},{56,48},{1,57}... | collective-permute-start | bytes 663560 | tf_op jit(solution)/shard_map/ppermute | solution.py:18
  16.5 7.4 %collective-permute-start.9 = (f32[48,1152]{1,0:T(8,128)}, f32[48,1152]{1,0:T(8,128)S(1)}, u32[]{:S(2)}, u32[]{:S(2)}) collective-permute-start(f32[48,1152]{1,0:T(8,128)} %refs_0_.1), channel_id=1, source_target_pairs={{0,192},{64,128},{128,64},{192,0},{1,193},{65,129},{129,65},{193,1... | collective-permute-start | bytes 663560 | tf_op jit(solution)/shard_map/ppermute | solution.py:26
  18.6 7.7 %collective-permute-start.5 = (f32[48,1152]{1,0:T(8,128)S(1)}, f32[48,1152]{1,0:T(8,128)S(1)}, u32[]{:S(2)}, u32[]{:S(2)}) collective-permute-start(f32[48,1152]{1,0:T(8,128)S(1)} %collective-permute-done.4.refs_7_), channel_id=1, source_target_pairs={{0,8},{8,16},{16,24},{24,32},{32,40},{40,48},{48,56},{56,0},{1,9},... | collective-permute-start | bytes 663560 | tf_op jit(solution)/shard_map/ppermute | solution.py:18
  20.0 9.4 %collective-permute-start.2 = (f32[48,1152]{1,0:T(8,128)S(1)}, f32[48,1152]{1,0:T(8,128)S(1)}, u32[]{:S(2)}, u32[]{:S(2)}) collective-permute-start(f32[48,1152]{1,0:T(8,128)S(1)} %collective-permute-done.1.refs_2_), channel_id=1, source_target_pairs={{0,56},{8,0},{16,8},{24,16},{32,24},{40,32},{48,40},{56,48},{1,57}... | collective-permute-start | bytes 663560 | tf_op jit(solution)/shard_map/ppermute | solution.py:18
  23.8 10.3 %collective-permute-start.10 = (f32[48,1152]{1,0:T(8,128)S(1)}, f32[48,1152]{1,0:T(8,128)S(1)}, u32[]{:S(2)}, u32[]{:S(2)}) collective-permute-start(f32[48,1152]{1,0:T(8,128)S(1)} %collective-permute-done.9.refs_6_), channel_id=1, source_target_pairs={{0,56},{8,0},{16,8},{24,16},{32,24},{40,32},{48,40},{56,48},{1,57}... | collective-permute-start | bytes 663560 | tf_op jit(solution)/shard_map/ppermute | solution.py:18
  23.9 13.9 %collective-permute-start.15 = (f32[48,1152]{1,0:T(8,128)S(1)}, f32[48,1152]{1,0:T(8,128)S(1)}, u32[]{:S(2)}, u32[]{:S(2)}) collective-permute-start(f32[48,1152]{1,0:T(8,128)S(1)} %collective-permute-done.9.refs_6_), channel_id=1, source_target_pairs={{0,8},{8,16},{16,24},{24,32},{32,40},{40,48},{48,56},{56,0},{1,9},... | collective-permute-start | bytes 663560 | tf_op jit(solution)/shard_map/ppermute | solution.py:18
  26.4 11.4 %collective-permute-start.6 = (f32[48,1152]{1,0:T(8,128)S(1)}, f32[48,1152]{1,0:T(8,128)S(1)}, u32[]{:S(2)}, u32[]{:S(2)}) collective-permute-start(f32[48,1152]{1,0:T(8,128)S(1)} %collective-permute-done.5.refs_6_), channel_id=1, source_target_pairs={{0,8},{8,16},{16,24},{24,32},{32,40},{40,48},{48,56},{56,0},{1,9},... | collective-permute-start | bytes 663560 | tf_op jit(solution)/shard_map/ppermute | solution.py:18
  29.4 10.7 %collective-permute-start.3 = (f32[48,1152]{1,0:T(8,128)S(1)}, f32[48,1152]{1,0:T(8,128)S(1)}, u32[]{:S(2)}, u32[]{:S(2)}) collective-permute-start(f32[48,1152]{1,0:T(8,128)S(1)} %collective-permute-done.2.refs_3_), channel_id=1, source_target_pairs={{0,56},{8,0},{16,8},{24,16},{32,24},{40,32},{48,40},{56,48},{1,57}... | collective-permute-start | bytes 663560 | tf_op jit(solution)/shard_map/ppermute | solution.py:18
  34.1 14.2 %collective-permute-start.11 = (f32[48,1152]{1,0:T(8,128)S(1)}, f32[48,1152]{1,0:T(8,128)S(1)}, u32[]{:S(2)}, u32[]{:S(2)}) collective-permute-start(f32[48,1152]{1,0:T(8,128)S(1)} %collective-permute-done.10.refs_7_), channel_id=1, source_target_pairs={{0,56},{8,0},{16,8},{24,16},{32,24},{40,32},{48,40},{56,48},{1,57}... | collective-permute-start | bytes 663560 | tf_op jit(solution)/shard_map/ppermute | solution.py:18
  37.8 10.5 %collective-permute-start.16 = (f32[48,1152]{1,0:T(8,128)S(1)}, f32[48,1152]{1,0:T(8,128)S(1)}, u32[]{:S(2)}, u32[]{:S(2)}) collective-permute-start(f32[48,1152]{1,0:T(8,128)S(1)} %collective-permute-done.15.refs_5_), channel_id=1, source_target_pairs={{0,8},{8,16},{16,24},{24,32},{32,40},{40,48},{48,56},{56,0},{1,9},... | collective-permute-start | bytes 663560 | tf_op jit(solution)/shard_map/ppermute | solution.py:18
  37.8 10.5 %collective-permute-start.12 = (f32[48,1152]{1,0:T(8,128)S(1)}, f32[48,1152]{1,0:T(8,128)S(1)}, u32[]{:S(2)}, u32[]{:S(2)}) collective-permute-start(f32[48,1152]{1,0:T(8,128)S(1)} %collective-permute-done.2.refs_3_), channel_id=1, source_target_pairs={{0,192},{64,128},{128,64},{192,0},{1,193},{65,129},{129,65},{193,1... | collective-permute-start | bytes 663560 | tf_op jit(solution)/shard_map/ppermute | solution.py:26
  40.1 8.3 %collective-permute-start.14 = (f32[48,1152]{1,0:T(8,128)S(1)}, f32[48,1152]{1,0:T(8,128)S(1)}, u32[]{:S(2)}, u32[]{:S(2)}) collective-permute-start(f32[48,1152]{1,0:T(8,128)S(1)} %collective-permute-done.6.refs_5_), channel_id=1, source_target_pairs={{0,192},{64,128},{128,64},{192,0},{1,193},{65,129},{129,65},{193,1... | collective-permute-start | bytes 663560 | tf_op jit(solution)/shard_map/ppermute | solution.py:26
  41.1 9.3 %collective-permute-start.13 = (f32[48,1152]{1,0:T(8,128)S(1)}, f32[48,1152]{1,0:T(8,128)S(1)}, u32[]{:S(2)}, u32[]{:S(2)}) collective-permute-start(f32[48,1152]{1,0:T(8,128)S(1)} %collective-permute-done.3.refs_4_), channel_id=1, source_target_pairs={{0,192},{64,128},{128,64},{192,0},{1,193},{65,129},{129,65},{193,1... | collective-permute-start | bytes 663560 | tf_op jit(solution)/shard_map/ppermute | solution.py:26
  43.3 1.3 copy-start.1
  44.6 0.9 copy-start.3
  45.6 54.3 %copy-start = (f32[48,96,500]{2,1,0:T(8,128)S(1)}, f32[48,96,500]{2,1,0:T(8,128)}, u32[]{:S(2)}) copy-start(f32[48,96,500]{2,1,0:T(8,128)} %refs_10_.1) | copy-start | bytes 27648004
  53.2 2.0 %collective-permute-start.17 = (f32[192,576]{1,0:T(8,128)S(1)}, f32[192,576]{1,0:T(8,128)S(1)}, u32[]{:S(2)}, u32[]{:S(2)}) collective-permute-start(f32[192,576]{1,0:T(8,128)S(1)} %get-tuple-element.28), channel_id=1, source_target_pairs={{0,2},{2,0},{1,3},{3,1},{4,6},{6,4},{5,7},{7,5},{8,10},{10,8},{9,1... | collective-permute-start | bytes 1327112 | tf_op jit(solution)/shard_map/ppermute | solution.py:22
  53.3 2.6 %collective-permute-start.8 = (f32[192,576]{1,0:T(8,128)S(1)}, f32[192,576]{1,0:T(8,128)S(1)}, u32[]{:S(2)}, u32[]{:S(2)}) collective-permute-start(f32[192,576]{1,0:T(8,128)S(1)} %get-tuple-element.24), channel_id=1, source_target_pairs={{0,2},{2,0},{1,3},{3,1},{4,6},{6,4},{5,7},{7,5},{8,10},{10,8},{9,1... | collective-permute-start | bytes 1327112 | tf_op jit(solution)/shard_map/ppermute | solution.py:22
  56.0 5.2 %collective-permute-start.18 = (f32[24,1152]{1,0:T(8,128)S(1)}, f32[24,1152]{1,0:T(8,128)S(1)}, u32[]{:S(2)}, u32[]{:S(2)}) collective-permute-start(f32[24,1152]{1,0:T(8,128)S(1)} %get-tuple-element.31), channel_id=1, source_target_pairs={{0,1},{1,4},{4,5},{5,0},{2,3},{3,6},{6,7},{7,2},{8,9},{9,12},{12,1... | collective-permute-start | bytes 331784 | tf_op jit(solution)/shard_map/ppermute | solution.py:18
  56.6 6.0 %collective-permute-start.19 = (f32[24,1152]{1,0:T(8,128)S(1)}, f32[24,1152]{1,0:T(8,128)S(1)}, u32[]{:S(2)}, u32[]{:S(2)}) collective-permute-start(f32[24,1152]{1,0:T(8,128)S(1)} %get-tuple-element.33), channel_id=1, source_target_pairs={{0,5},{1,0},{4,1},{5,4},{2,7},{3,2},{6,3},{7,6},{8,13},{9,8},{12,9... | collective-permute-start | bytes 331784 | tf_op jit(solution)/shard_map/ppermute | solution.py:18
  62.7 6.4 %collective-permute-start.20 = (f32[48,1152]{1,0:T(8,128)S(1)}, f32[48,1152]{1,0:T(8,128)S(1)}, u32[]{:S(2)}, u32[]{:S(2)}) collective-permute-start(f32[48,1152]{1,0:T(8,128)S(1)} %get-tuple-element.34), channel_id=1, source_target_pairs={{0,1},{1,4},{4,5},{5,0},{2,3},{3,6},{6,7},{7,2},{8,9},{9,12},{12,1... | collective-permute-start | bytes 663560 | tf_op jit(solution)/shard_map/ppermute | solution.py:18
  63.0 7.6 %collective-permute-start.21 = (f32[48,1152]{1,0:T(8,128)S(1)}, f32[48,1152]{1,0:T(8,128)S(1)}, u32[]{:S(2)}, u32[]{:S(2)}) collective-permute-start(f32[48,1152]{1,0:T(8,128)S(1)} %get-tuple-element.35), channel_id=1, source_target_pairs={{0,5},{1,0},{4,1},{5,4},{2,7},{3,2},{6,3},{7,6},{8,13},{9,8},{12,9... | collective-permute-start | bytes 663560 | tf_op jit(solution)/shard_map/ppermute | solution.py:18
  70.7 11.5 %collective-permute-start.22 = (f32[48,576]{1,0:T(8,128)S(1)}, f32[48,576]{1,0:T(8,128)S(1)}, u32[]{:S(2)}, u32[]{:S(2)}) collective-permute-start(f32[48,576]{1,0:T(8,128)S(1)} %get-tuple-element.36), channel_id=1, source_target_pairs={{0,0},{2,34},{1,9},{3,43},{4,20},{6,54},{5,29},{7,63},{8,8},{10,42... | collective-permute-start | bytes 331784 | tf_op jit(solution)/shard_map/ppermute | solution.py:281
  74.4 10.3 %collective-permute-start.23 = (f32[48,576]{1,0:T(8,128)S(1)}, f32[48,576]{1,0:T(8,128)S(1)}, u32[]{:S(2)}, u32[]{:S(2)}) collective-permute-start(f32[48,576]{1,0:T(8,128)S(1)} %get-tuple-element.37), channel_id=1, source_target_pairs={{0,208},{2,242},{1,217},{3,251},{4,228},{6,198},{5,237},{7,207},{8... | collective-permute-start | bytes 331784 | tf_op jit(solution)/shard_map/ppermute | solution.py:281
  84.7 7.4 %collective-permute-start.24 = (f32[48,1152]{1,0:T(8,128)S(1)}, f32[48,1152]{1,0:T(8,128)S(1)}, u32[]{:S(2)}, u32[]{:S(2)}) collective-permute-start(f32[48,1152]{1,0:T(8,128)S(1)} %shard_map.81.refs_0_), channel_id=1, source_target_pairs={{0,5},{1,0},{4,1},{5,4},{2,7},{3,2},{6,3},{7,6},{8,13},{9,8},{12,9... | collective-permute-start | bytes 663560 | tf_op jit(solution)/shard_map/ppermute | solution.py:18
  84.8 7.7 %collective-permute-start.26 = (f32[48,1152]{1,0:T(8,128)S(1)}, f32[48,1152]{1,0:T(8,128)S(1)}, u32[]{:S(2)}, u32[]{:S(2)}) collective-permute-start(f32[48,1152]{1,0:T(8,128)S(1)} %shard_map.81.refs_0_), channel_id=1, source_target_pairs={{0,1},{1,4},{4,5},{5,0},{2,3},{3,6},{6,7},{7,2},{8,9},{9,12},{12,1... | collective-permute-start | bytes 663560 | tf_op jit(solution)/shard_map/ppermute | solution.py:18
  88.1 10.9 %collective-permute-start.28 = (f32[48,1152]{1,0:T(8,128)S(1)}, f32[48,1152]{1,0:T(8,128)S(1)}, u32[]{:S(2)}, u32[]{:S(2)}) collective-permute-start(f32[48,1152]{1,0:T(8,128)S(1)} %shard_map.81.refs_0_), channel_id=1, source_target_pairs={{0,2},{2,0},{1,3},{3,1},{4,6},{6,4},{5,7},{7,5},{8,10},{10,8},{9,1... | collective-permute-start | bytes 663560 | tf_op jit(solution)/shard_map/ppermute | solution.py:22
  92.2 6.3 %collective-permute-start.25 = (f32[24,1152]{1,0:T(8,128)S(1)}, f32[24,1152]{1,0:T(8,128)S(1)}, u32[]{:S(2)}, u32[]{:S(2)}) collective-permute-start(f32[24,1152]{1,0:T(8,128)S(1)} %slice.8), channel_id=1, source_target_pairs={{0,5},{1,0},{4,1},{5,4},{2,7},{3,2},{6,3},{7,6},{8,13},{9,8},{12,9... | collective-permute-start | bytes 331784 | tf_op jit(solution)/shard_map/ppermute | solution.py:18
  92.5 5.9 %collective-permute-start.27 = (f32[24,1152]{1,0:T(8,128)S(1)}, f32[24,1152]{1,0:T(8,128)S(1)}, u32[]{:S(2)}, u32[]{:S(2)}) collective-permute-start(f32[24,1152]{1,0:T(8,128)S(1)} %slice.9), channel_id=1, source_target_pairs={{0,1},{1,4},{4,5},{5,0},{2,3},{3,6},{6,7},{7,2},{8,9},{9,12},{12,1... | collective-permute-start | bytes 331784 | tf_op jit(solution)/shard_map/ppermute | solution.py:18
  95.8 4.1 %collective-permute-start.29 = (f32[48,1152]{1,0:T(8,128)S(1)}, f32[48,1152]{1,0:T(8,128)S(1)}, u32[]{:S(2)}, u32[]{:S(2)}) collective-permute-start(f32[48,1152]{1,0:T(8,128)S(1)} %collective-permute-done.24.refs_1_), channel_id=1, source_target_pairs={{0,2},{2,0},{1,3},{3,1},{4,6},{6,4},{5,7},{7,5},{8,10},{10,8},{9,1... | collective-permute-start | bytes 663560 | tf_op jit(solution)/shard_map/ppermute | solution.py:22
  95.8 4.1 %collective-permute-start.32 = (f32[48,1152]{1,0:T(8,128)S(1)}, f32[48,1152]{1,0:T(8,128)S(1)}, u32[]{:S(2)}, u32[]{:S(2)}) collective-permute-start(f32[48,1152]{1,0:T(8,128)S(1)} %collective-permute-done.26.refs_4_), channel_id=1, source_target_pairs={{0,2},{2,0},{1,3},{3,1},{4,6},{6,4},{5,7},{7,5},{8,10},{10,8},{9,1... | collective-permute-start | bytes 663560 | tf_op jit(solution)/shard_map/ppermute | solution.py:22
  98.4 1.3 collective-permute-start.30
  98.5 1.5 collective-permute-start.31
  105.6 36.9 %copy-start.2 = (f32[125,500]{0,1:T(8,128)S(1)}, f32[125,500]{0,1:T(8,128)}, u32[]{:S(2)}) copy-start(f32[125,500]{0,1:T(8,128)} %param.8) | copy-start | bytes 750004
  105.6 43.2 %copy-start.4 = (f32[125,96]{0,1:T(8,128)S(1)}, f32[125,96]{0,1:T(8,128)}, u32[]{:S(2)}) copy-start(f32[125,96]{0,1:T(8,128)} %param.9) | copy-start | bytes 144004
  121.6 5.4 %collective-permute-start.33 = (f32[48,128]{1,0:T(8,128)S(1)}, f32[48,128]{1,0:T(8,128)S(1)}, u32[]{:S(2)}, u32[]{:S(2)}) collective-permute-start(f32[48,128]{1,0:T(8,128)S(1)} %reduce_sum.9), channel_id=1, source_target_pairs={{0,128},{64,192},{128,0},{192,64},{1,129},{65,193},{129,1},{193,65... | collective-permute-start | bytes 73736 | tf_op jit(solution)/shard_map/ppermute | solution.py:26
  122.3 4.9 %collective-permute-start.34 = (f32[48,128]{1,0:T(8,128)S(1)}, f32[48,128]{1,0:T(8,128)S(1)}, u32[]{:S(2)}, u32[]{:S(2)}) collective-permute-start(f32[48,128]{1,0:T(8,128)S(1)} %reduce_sum.9), channel_id=1, source_target_pairs={{0,64},{64,0},{128,192},{192,128},{1,65},{65,1},{129,193},{193,129... | collective-permute-start | bytes 73736 | tf_op jit(solution)/shard_map/ppermute | solution.py:26
  125.2 5.0 %collective-permute-start.35 = (f32[48,128]{1,0:T(8,128)S(1)}, f32[48,128]{1,0:T(8,128)S(1)}, u32[]{:S(2)}, u32[]{:S(2)}) collective-permute-start(f32[48,128]{1,0:T(8,128)S(1)} %reduce_sum.9), channel_id=1, source_target_pairs={{0,192},{64,128},{128,64},{192,0},{1,193},{65,129},{129,65},{193,1... | collective-permute-start | bytes 73736 | tf_op jit(solution)/shard_map/ppermute | solution.py:26
  142.7 1.3 collective-permute-start.36
  144.0 5.1 %collective-permute-start.37 = (f32[104,125]{1,0:T(8,128)S(1)}, f32[104,125]{1,0:T(8,128)S(1)}, u32[]{:S(2)}, u32[]{:S(2)}) collective-permute-start(f32[104,125]{1,0:T(8,128)S(1)} %add.15.a_ref), channel_id=1, source_target_pairs={{0,1},{1,0},{4,5},{5,4},{2,3},{3,2},{6,7},{7,6},{8,9},{9,8},{12,13... | collective-permute-start | bytes 156008 | tf_op jit(solution)/shard_map/ppermute | solution.py:26
  144.1 7.4 %collective-permute-start.38 = (f32[104,125]{1,0:T(8,128)S(1)}, f32[104,125]{1,0:T(8,128)S(1)}, u32[]{:S(2)}, u32[]{:S(2)}) collective-permute-start(f32[104,125]{1,0:T(8,128)S(1)} %add.15.a_ref), channel_id=1, source_target_pairs={{0,4},{1,5},{4,0},{5,1},{2,6},{3,7},{6,2},{7,3},{8,12},{9,13},{12,... | collective-permute-start | bytes 156008 | tf_op jit(solution)/shard_map/ppermute | solution.py:26
  148.5 5.3 %collective-permute-start.39 = (f32[104,125]{1,0:T(8,128)S(1)}, f32[104,125]{1,0:T(8,128)S(1)}, u32[]{:S(2)}, u32[]{:S(2)}) collective-permute-start(f32[104,125]{1,0:T(8,128)S(1)} %add.15.a_ref), channel_id=1, source_target_pairs={{0,5},{1,4},{4,1},{5,0},{2,7},{3,6},{6,3},{7,2},{8,13},{9,12},{12,... | collective-permute-start | bytes 156008 | tf_op jit(solution)/shard_map/ppermute | solution.py:26

commit v3 on v2

--- a/solution.py
+++ b/solution.py
@@ -257,7 +257,7 @@
             if found is near or k < 3:
                 found[k] = shift(found[k - 1], "z", NZ, -1)
                 found[NZ - k] = shift(found[(NZ - k + 1) % NZ], "z", NZ, 1)
-    near[4] = shift(near[3], "z", NZ, -1)
+    near[4] = shift(near[2], "z", NZ, -2)
     for k in (3, 5, 4):
         far[k] = swap(near[k], "y", NY, 3)
 

time: 155 us -> 159 us (1.026)
  waiting for transfers between devices: 48.8 us -> 57.4 us
  starting transfers between devices: 61.6 us -> 57.6 us
    ppermute x19, waiting for transfers between devices: 27.2 us -> 35 us  [shift(): lax.ppermute(value, axis, [(i, (i + step) % size) for i in range(size)])]
    ppermute x19, starting transfers between devices: 33.7 us -> 29 us  [shift(): lax.ppermute(value, axis, [(i, (i + step) % size) for i in range(size)])]
    ppermute x2, waiting for transfers between devices: 5.98 us -> 7.82 us  [send_home(): return lax.ppermute(value, ('y', 'z', 'xh', 'co', 'xl'), pairs)]
where the time goes in v3:
time: 159 us
  starting transfers between devices  57.6 us (36%)
  waiting for transfers between devices  57.4 us (36%)
  blocking collectives  27.5 us (17%)
  Pallas kernels  12.9 us (8%)
  local copies, waits for them, and re-layouts  2.31 us (1%)
    ppermute x19, waiting for transfers between devices, shift(): lax.ppermute(value, axis, [(i, (i + step) % size) for i in range(size)])  35 us
    ppermute x19, starting transfers between devices, shift(): lax.ppermute(value, axis, [(i, (i + step) % size) for i in range(size)])  29 us
    ppermute x11, starting transfers between devices, swap(): return lax.ppermute(value, axis, [(i, i ^ mask) for i in range(size)])  18.2 us
    all_to_all x1, blocking collectives, on_device(): lax.all_to_all(tiles, 'z', split_axis=0, concat_axis=0, tiled=True)  15.3 us
    all_to_all x1, blocking collectives, on_device(): lax.all_to_all(jnp.broadcast_to(piece[None], tiles.shape), 'z', split_axi...  12.2 us
    ppermute x11, waiting for transfers between devices, swap(): return lax.ppermute(value, axis, [(i, i ^ mask) for i in range(size)])  10.3 us
    ppermute x2, starting transfers between devices, send_home(): return lax.ppermute(value, ('y', 'z', 'xh', 'co', 'xl'), pairs)  8.63 us
    ppermute x2, waiting for transfers between devices, send_home(): return lax.ppermute(value, ('y', 'z', 'xh', 'co', 'xl'), pairs)  7.82 us
  transfers between devices with their start and end apart: 40, of which 25 were waited for; matrix products, arithmetic and copies ran while one was open for 0% of the time, Pallas kernels for 2%

profile of v3, /device:TPU:6, one launch (start us, length us, event | category | flops | bytes accessed | tf_op | source)
XLA Modules:
  0.0 158.5 jit_solution(11354842075602172819)
XLA Ops:
  0.6 1.7 %collective-permute-start.7 = (f32[288,1152]{1,0:T(8,128)}, f32[288,1152]{1,0:T(8,128)S(1)}, u32[]{:S(2)}, u32[]{:S(2)}) collective-permute-start(f32[288,1152]{1,0:T(8,128)} %refs_8_.1), channel_id=1, source_target_pairs={{0,64},{64,0},{128,192},{192,128},{1,65},{65,1},{129,193},{193,129... | collective-permute-start | bytes 3981320 | tf_op jit(solution)/shard_map/ppermute | solution.py:26
  2.3 5.9 %collective-permute-start = (f32[48,1152]{1,0:T(8,128)}, f32[48,1152]{1,0:T(8,128)S(1)}, u32[]{:S(2)}, u32[]{:S(2)}) collective-permute-start(f32[48,1152]{1,0:T(8,128)} %refs_0_.1), channel_id=1, source_target_pairs={{0,56},{8,0},{16,8},{24,16},{32,24},{40,32},{48,40},{56,48},{1,57}... | collective-permute-start | bytes 663560 | tf_op jit(solution)/shard_map/ppermute | solution.py:18
  8.2 2.2 %collective-permute-start.9 = (f32[48,1152]{1,0:T(8,128)}, f32[48,1152]{1,0:T(8,128)S(1)}, u32[]{:S(2)}, u32[]{:S(2)}) collective-permute-start(f32[48,1152]{1,0:T(8,128)} %refs_0_.1), channel_id=1, source_target_pairs={{0,192},{64,128},{128,64},{192,0},{1,193},{65,129},{129,65},{193,1... | collective-permute-start | bytes 663560 | tf_op jit(solution)/shard_map/ppermute | solution.py:26
  10.3 2.5 %collective-permute-done.refs_1_ = f32[48,1152]{1,0:T(8,128)S(1)} collective-permute-done((f32[48,1152]{1,0:T(8,128)}, f32[48,1152]{1,0:T(8,128)S(1)}, u32[]{:S(2)}, u32[]{:S(2)}) %collective-permute-start) | collective-permute-done | bytes 221216 | tf_op jit(solution)/shard_map/ppermute | solution.py:18
  12.9 3.6 %collective-permute-start.1 = (f32[48,1152]{1,0:T(8,128)S(1)}, f32[48,1152]{1,0:T(8,128)S(1)}, u32[]{:S(2)}, u32[]{:S(2)}) collective-permute-start(f32[48,1152]{1,0:T(8,128)S(1)} %collective-permute-done.refs_1_), channel_id=1, source_target_pairs={{0,56},{8,0},{16,8},{24,16},{32,24},{40,32},{48,40},{56,48},{1,57}... | collective-permute-start | bytes 663560 | tf_op jit(solution)/shard_map/ppermute | solution.py:18
  16.5 3.2 %collective-permute-start.10 = (f32[48,1152]{1,0:T(8,128)S(1)}, f32[48,1152]{1,0:T(8,128)S(1)}, u32[]{:S(2)}, u32[]{:S(2)}) collective-permute-start(f32[48,1152]{1,0:T(8,128)S(1)} %collective-permute-done.9.refs_6_), channel_id=1, source_target_pairs={{0,56},{8,0},{16,8},{24,16},{32,24},{40,32},{48,40},{56,48},{1,57}... | collective-permute-start | bytes 663560 | tf_op jit(solution)/shard_map/ppermute | solution.py:18
  19.7 2.3 %collective-permute-done.1.refs_2_ = f32[48,1152]{1,0:T(8,128)S(1)} collective-permute-done((f32[48,1152]{1,0:T(8,128)S(1)}, f32[48,1152]{1,0:T(8,128)S(1)}, u32[]{:S(2)}, u32[]{:S(2)}) %collective-permute-start.1) | collective-permute-done | bytes 221216 | tf_op jit(solution)/shard_map/ppermute | solution.py:18
  22.0 3.7 %collective-permute-start.2 = (f32[48,1152]{1,0:T(8,128)S(1)}, f32[48,1152]{1,0:T(8,128)S(1)}, u32[]{:S(2)}, u32[]{:S(2)}) collective-permute-start(f32[48,1152]{1,0:T(8,128)S(1)} %collective-permute-done.1.refs_2_), channel_id=1, source_target_pairs={{0,56},{8,0},{16,8},{24,16},{32,24},{40,32},{48,40},{56,48},{1,57}... | collective-permute-start | bytes 663560 | tf_op jit(solution)/shard_map/ppermute | solution.py:18
  25.9 0.8 collective-permute-done.10.refs_7_
  27.2 2.2 %collective-permute-done.15.refs_5_ = f32[48,1152]{1,0:T(8,128)S(1)} collective-permute-done((f32[48,1152]{1,0:T(8,128)S(1)}, f32[48,1152]{1,0:T(8,128)S(1)}, u32[]{:S(2)}, u32[]{:S(2)}) %collective-permute-start.15) | collective-permute-done | bytes 221216 | tf_op jit(solution)/shard_map/ppermute | solution.py:18
  29.3 1.1 collective-permute-start.11
  30.4 4.2 %collective-permute-done.2.refs_3_ = f32[48,1152]{1,0:T(8,128)S(1)} collective-permute-done((f32[48,1152]{1,0:T(8,128)S(1)}, f32[48,1152]{1,0:T(8,128)S(1)}, u32[]{:S(2)}, u32[]{:S(2)}) %collective-permute-start.2) | collective-permute-done | bytes 221216 | tf_op jit(solution)/shard_map/ppermute | solution.py:18
  34.6 6.4 %collective-permute-done.3.refs_4_ = f32[48,1152]{1,0:T(8,128)S(1)} collective-permute-done((f32[48,1152]{1,0:T(8,128)S(1)}, f32[48,1152]{1,0:T(8,128)S(1)}, u32[]{:S(2)}, u32[]{:S(2)}) %collective-permute-start.3) | collective-permute-done | bytes 221216 | tf_op jit(solution)/shard_map/ppermute | solution.py:18
  41.1 2.2 %collective-permute-start.12 = (f32[48,1152]{1,0:T(8,128)S(1)}, f32[48,1152]{1,0:T(8,128)S(1)}, u32[]{:S(2)}, u32[]{:S(2)}) collective-permute-start(f32[48,1152]{1,0:T(8,128)S(1)} %collective-permute-done.2.refs_3_), channel_id=1, source_target_pairs={{0,192},{64,128},{128,64},{192,0},{1,193},{65,129},{129,65},{193,1... | collective-permute-start | bytes 663560 | tf_op jit(solution)/shard_map/ppermute | solution.py:26
  43.3 1.1 collective-permute-start.13
  44.3 2.2 %collective-permute-start.14 = (f32[48,1152]{1,0:T(8,128)S(1)}, f32[48,1152]{1,0:T(8,128)S(1)}, u32[]{:S(2)}, u32[]{:S(2)}) collective-permute-start(f32[48,1152]{1,0:T(8,128)S(1)} %collective-permute-done.6.refs_5_), channel_id=1, source_target_pairs={{0,192},{64,128},{128,64},{192,0},{1,193},{65,129},{129,65},{193,1... | collective-permute-start | bytes 663560 | tf_op jit(solution)/shard_map/ppermute | solution.py:26
  46.5 1.3 copy-done.1
  47.8 0.9 copy-done.3
  48.8 2.7 %shard_map.76 = (f32[192,576]{1,0:T(8,128)S(1)}, f32[192,576]{1,0:T(8,128)S(1)}, bf16[576,1152]{1,0:T(8,128)(2,1)S(1)}, bf16[576,1152]{1,0:T(8,128)(2,1)S(1)}) custom-call(f32[48,1152]{1,0:T(8,128)S(1)} %copy-done.3, f32[48,1152]{1,0:T(8,128)S(1)} %collective-permute-done.refs_1_, f32[48,1152]{1,0:T(8,128)S(1)} %collective-permute-done.1.refs_2_, ...), custom_call_target="tpu_custom_call" | custom-call | flops 1000 | bytes 1000 | tf_op jit(solution)/shard_map/pallas_call | solution.py:79
  51.5 1.9 %collective-permute-done.14.refs_3_ = f32[48,1152]{1,0:T(8,128)S(1)} collective-permute-done((f32[48,1152]{1,0:T(8,128)S(1)}, f32[48,1152]{1,0:T(8,128)S(1)}, u32[]{:S(2)}, u32[]{:S(2)}) %collective-permute-start.14) | collective-permute-done | bytes 221216 | tf_op jit(solution)/shard_map/ppermute | solution.py:26
  53.4 2.7 %shard_map.77 = (f32[192,576]{1,0:T(8,128)S(1)}, f32[192,576]{1,0:T(8,128)S(1)}) custom-call(f32[48,1152]{1,0:T(8,128)S(1)} %collective-permute-done.11.refs_0_, f32[48,1152]{1,0:T(8,128)S(1)} %collective-permute-done.12.refs_1_, f32[48,1152]{1,0:T(8,128)S(1)} %collective-permute-done.13.refs_2_, f32[48,1152]{1,0:T(8,128)S(1)} %collective-permute-done.14.refs_3_, ...), custom_call_target="tpu_custom_call" | custom-call | flops 1000 | bytes 1000 | tf_op jit(solution)/shard_map/pallas_call | solution.py:79
  56.7 1.4 collective-permute-done.17.refs_3_
  59.5 1.5 collective-permute-start.19
  61.1 3.1 %collective-permute-done.18.up_ref = f32[24,1152]{1,0:T(8,128)S(1)} collective-permute-done((f32[24,1152]{1,0:T(8,128)S(1)}, f32[24,1152]{1,0:T(8,128)S(1)}, u32[]{:S(2)}, u32[]{:S(2)}) %collective-permute-start.18) | collective-permute-done | bytes 110624 | tf_op jit(solution)/shard_map/ppermute | solution.py:18
  64.1 1.4 collective-permute-done.19.down_ref
  66.0 1.7 %collective-permute-start.21 = (f32[48,1152]{1,0:T(8,128)S(1)}, f32[48,1152]{1,0:T(8,128)S(1)}, u32[]{:S(2)}, u32[]{:S(2)}) collective-permute-start(f32[48,1152]{1,0:T(8,128)S(1)} %get-tuple-element.35), channel_id=1, source_target_pairs={{0,5},{1,0},{4,1},{5,4},{2,7},{3,2},{6,3},{7,6},{8,13},{9,8},{12,9... | collective-permute-start | bytes 663560 | tf_op jit(solution)/shard_map/ppermute | solution.py:18
  67.7 4.3 %collective-permute-done.20.one_ref = f32[48,1152]{1,0:T(8,128)S(1)} collective-permute-done((f32[48,1152]{1,0:T(8,128)S(1)}, f32[48,1152]{1,0:T(8,128)S(1)}, u32[]{:S(2)}, u32[]{:S(2)}) %collective-permute-start.20) | collective-permute-done | bytes 221216 | tf_op jit(solution)/shard_map/ppermute | solution.py:18
  72.0 1.5 collective-permute-done.21.two_ref
  73.6 3.8 %collective-permute-start.22 = (f32[48,576]{1,0:T(8,128)S(1)}, f32[48,576]{1,0:T(8,128)S(1)}, u32[]{:S(2)}, u32[]{:S(2)}) collective-permute-start(f32[48,576]{1,0:T(8,128)S(1)} %get-tuple-element.36), channel_id=1, source_target_pairs={{0,0},{2,34},{1,9},{3,43},{4,20},{6,54},{5,29},{7,63},{8,8},{10,42... | collective-permute-start | bytes 331784 | tf_op jit(solution)/shard_map/ppermute | solution.py:281
  77.4 4.9 %collective-permute-start.23 = (f32[48,576]{1,0:T(8,128)S(1)}, f32[48,576]{1,0:T(8,128)S(1)}, u32[]{:S(2)}, u32[]{:S(2)}) collective-permute-start(f32[48,576]{1,0:T(8,128)S(1)} %get-tuple-element.37), channel_id=1, source_target_pairs={{0,208},{2,242},{1,217},{3,251},{4,228},{6,198},{5,237},{7,207},{8... | collective-permute-start | bytes 331784 | tf_op jit(solution)/shard_map/ppermute | solution.py:281
  82.3 3.6 %collective-permute-done.22.first_ref = f32[48,576]{1,0:T(8,128)S(1)} collective-permute-done((f32[48,576]{1,0:T(8,128)S(1)}, f32[48,576]{1,0:T(8,128)S(1)}, u32[]{:S(2)}, u32[]{:S(2)}) %collective-permute-start.22) | collective-permute-done | bytes 110624 | tf_op jit(solution)/shard_map/ppermute | solution.py:281
  85.9 4.2 %collective-permute-done.23.second_ref = f32[48,576]{1,0:T(8,128)S(1)} collective-permute-done((f32[48,576]{1,0:T(8,128)S(1)}, f32[48,576]{1,0:T(8,128)S(1)}, u32[]{:S(2)}, u32[]{:S(2)}) %collective-permute-start.23) | collective-permute-done | bytes 110624 | tf_op jit(solution)/shard_map/ppermute | solution.py:281
  90.3 3.2 %collective-permute-start.26 = (f32[48,1152]{1,0:T(8,128)S(1)}, f32[48,1152]{1,0:T(8,128)S(1)}, u32[]{:S(2)}, u32[]{:S(2)}) collective-permute-start(f32[48,1152]{1,0:T(8,128)S(1)} %shard_map.81.refs_0_), channel_id=1, source_target_pairs={{0,1},{1,4},{4,5},{5,0},{2,3},{3,6},{6,7},{7,2},{8,9},{9,12},{12,1... | collective-permute-start | bytes 663560 | tf_op jit(solution)/shard_map/ppermute | solution.py:18
  93.5 3.9 %collective-permute-done.24.refs_1_ = f32[48,1152]{1,0:T(8,128)S(1)} collective-permute-done((f32[48,1152]{1,0:T(8,128)S(1)}, f32[48,1152]{1,0:T(8,128)S(1)}, u32[]{:S(2)}, u32[]{:S(2)}) %collective-permute-start.24) | collective-permute-done | bytes 221216 | tf_op jit(solution)/shard_map/ppermute | solution.py:18
  97.8 3.3 %collective-permute-start.27 = (f32[24,1152]{1,0:T(8,128)S(1)}, f32[24,1152]{1,0:T(8,128)S(1)}, u32[]{:S(2)}, u32[]{:S(2)}) collective-permute-start(f32[24,1152]{1,0:T(8,128)S(1)} %slice.9), channel_id=1, source_target_pairs={{0,1},{1,4},{4,5},{5,0},{2,3},{3,6},{6,7},{7,2},{8,9},{9,12},{12,1... | collective-permute-start | bytes 331784 | tf_op jit(solution)/shard_map/ppermute | solution.py:18
  101.6 2.1 %collective-permute-done.25.refs_2_ = f32[24,1152]{1,0:T(8,128)S(1)} collective-permute-done((f32[24,1152]{1,0:T(8,128)S(1)}, f32[24,1152]{1,0:T(8,128)S(1)}, u32[]{:S(2)}, u32[]{:S(2)}) %collective-permute-start.25) | collective-permute-done | bytes 110624 | tf_op jit(solution)/shard_map/ppermute | solution.py:18
  105.2 5.6 %shard_map.82 = f32[8,48,128]{2,1,0:T(8,128)S(1)} custom-call(f32[48,1152]{1,0:T(8,128)S(1)} %shard_map.81.refs_0_, f32[48,1152]{1,0:T(8,128)S(1)} %collective-permute-done.24.refs_1_, f32[24,1152]{1,0:T(8,128)S(1)} %collective-permute-done.25.refs_2_, f32[24,1152]{1,0:T(8,128)S(1)} %collective-permute-done.27.refs_3_, ...), custom_call_target="tpu_custom_call" | custom-call | tf_op jit(solution)/shard_map/pallas_call | solution.py:191
  110.8 15.3 %all_to_all.10 = f32[8,48,128]{2,1,0:T(8,128)S(1)} all-to-all(f32[8,48,128]{2,1,0:T(8,128)S(1)} %shard_map.82), channel_id=1, replica_groups=mesh['y'=4,'z'=8,'xh'=2,'co'=2,'xl'=2] {'z'}, dimensions={0} | all-to-all | bytes 393216 | tf_op jit(solution)/shard_map/all_to_all | solution.py:298
  126.5 2.6 %collective-permute-start.34 = (f32[48,128]{1,0:T(8,128)S(1)}, f32[48,128]{1,0:T(8,128)S(1)}, u32[]{:S(2)}, u32[]{:S(2)}) collective-permute-start(f32[48,128]{1,0:T(8,128)S(1)} %reduce_sum.9), channel_id=1, source_target_pairs={{0,64},{64,0},{128,192},{192,128},{1,65},{65,1},{129,193},{193,129... | collective-permute-start | bytes 73736 | tf_op jit(solution)/shard_map/ppermute | solution.py:26
  129.0 1.3 collective-permute-start.35
  130.3 1.3 collective-permute-done.33
  131.7 2.4 %collective-permute-done.35 = f32[48,128]{1,0:T(8,128)S(1)} collective-permute-done((f32[48,128]{1,0:T(8,128)S(1)}, f32[48,128]{1,0:T(8,128)S(1)}, u32[]{:S(2)}, u32[]{:S(2)}) %collective-permute-start.35) | collective-permute-done | bytes 24608 | tf_op jit(solution)/shard_map/ppermute | solution.py:26
  134.1 12.2 %all_to_all.11.tiles_ref = f32[8,48,128]{2,1,0:T(8,128)S(1)} all-to-all(f32[8,48,128]{2,1,0:T(8,128)S(1)} %broadcast_in_dim.2), channel_id=1, replica_groups=mesh['y'=4,'z'=8,'xh'=2,'co'=2,'xl'=2] {'z'}, dimensions={0} | all-to-all | bytes 393216 | tf_op jit(solution)/shard_map/all_to_all | solution.py:300
  146.6 1.2 collective-permute-done.36
  148.0 4.4 %collective-permute-start.38 = (f32[104,125]{1,0:T(8,128)S(1)}, f32[104,125]{1,0:T(8,128)S(1)}, u32[]{:S(2)}, u32[]{:S(2)}) collective-permute-start(f32[104,125]{1,0:T(8,128)S(1)} %add.15.a_ref), channel_id=1, source_target_pairs={{0,4},{1,5},{4,0},{5,1},{2,6},{3,7},{6,2},{7,3},{8,12},{9,13},{12,... | collective-permute-start | bytes 156008 | tf_op jit(solution)/shard_map/ppermute | solution.py:26
  153.0 2.3 %collective-permute-done.38.c_ref = f32[104,125]{1,0:T(8,128)S(1)} collective-permute-done((f32[104,125]{1,0:T(8,128)S(1)}, f32[104,125]{1,0:T(8,128)S(1)}, u32[]{:S(2)}, u32[]{:S(2)}) %collective-permute-start.38) | collective-permute-done | bytes 52032 | tf_op jit(solution)/shard_map/ppermute | solution.py:26
  155.3 2.4 %collective-permute-done.39.d_ref = f32[104,125]{1,0:T(8,128)S(1)} collective-permute-done((f32[104,125]{1,0:T(8,128)S(1)}, f32[104,125]{1,0:T(8,128)S(1)}, u32[]{:S(2)}, u32[]{:S(2)}) %collective-permute-start.39) | collective-permute-done | bytes 52032 | tf_op jit(solution)/shard_map/ppermute | solution.py:26
  157.7 0.8 shard_map.85
  (60 shorter events, 7.1 us)
Async XLA Ops:
  0.6 43.7 %collective-permute-start.7 = (f32[288,1152]{1,0:T(8,128)}, f32[288,1152]{1,0:T(8,128)S(1)}, u32[]{:S(2)}, u32[]{:S(2)}) collective-permute-start(f32[288,1152]{1,0:T(8,128)} %refs_8_.1), channel_id=1, source_target_pairs={{0,64},{64,0},{128,192},{192,128},{1,65},{65,1},{129,193},{193,129... | collective-permute-start | bytes 3981320 | tf_op jit(solution)/shard_map/ppermute | solution.py:26
  2.3 10.6 %collective-permute-start = (f32[48,1152]{1,0:T(8,128)}, f32[48,1152]{1,0:T(8,128)S(1)}, u32[]{:S(2)}, u32[]{:S(2)}) collective-permute-start(f32[48,1152]{1,0:T(8,128)} %refs_0_.1), channel_id=1, source_target_pairs={{0,56},{8,0},{16,8},{24,16},{32,24},{40,32},{48,40},{56,48},{1,57}... | collective-permute-start | bytes 663560 | tf_op jit(solution)/shard_map/ppermute | solution.py:18
  8.2 8.3 %collective-permute-start.4 = (f32[48,1152]{1,0:T(8,128)}, f32[48,1152]{1,0:T(8,128)S(1)}, u32[]{:S(2)}, u32[]{:S(2)}) collective-permute-start(f32[48,1152]{1,0:T(8,128)} %refs_0_.1), channel_id=1, source_target_pairs={{0,8},{8,16},{16,24},{24,32},{32,40},{40,48},{48,56},{56,0},{1,9},... | collective-permute-start | bytes 663560 | tf_op jit(solution)/shard_map/ppermute | solution.py:18
  8.2 8.3 %collective-permute-start.9 = (f32[48,1152]{1,0:T(8,128)}, f32[48,1152]{1,0:T(8,128)S(1)}, u32[]{:S(2)}, u32[]{:S(2)}) collective-permute-start(f32[48,1152]{1,0:T(8,128)} %refs_0_.1), channel_id=1, source_target_pairs={{0,192},{64,128},{128,64},{192,0},{1,193},{65,129},{129,65},{193,1... | collective-permute-start | bytes 663560 | tf_op jit(solution)/shard_map/ppermute | solution.py:26
  12.9 9.1 %collective-permute-start.1 = (f32[48,1152]{1,0:T(8,128)S(1)}, f32[48,1152]{1,0:T(8,128)S(1)}, u32[]{:S(2)}, u32[]{:S(2)}) collective-permute-start(f32[48,1152]{1,0:T(8,128)S(1)} %collective-permute-done.refs_1_), channel_id=1, source_target_pairs={{0,56},{8,0},{16,8},{24,16},{32,24},{40,32},{48,40},{56,48},{1,57}... | collective-permute-start | bytes 663560 | tf_op jit(solution)/shard_map/ppermute | solution.py:18
  16.5 9.4 %collective-permute-start.5 = (f32[48,1152]{1,0:T(8,128)S(1)}, f32[48,1152]{1,0:T(8,128)S(1)}, u32[]{:S(2)}, u32[]{:S(2)}) collective-permute-start(f32[48,1152]{1,0:T(8,128)S(1)} %collective-permute-done.4.refs_7_), channel_id=1, source_target_pairs={{0,8},{8,16},{16,24},{24,32},{32,40},{40,48},{48,56},{56,0},{1,9},... | collective-permute-start | bytes 663560 | tf_op jit(solution)/shard_map/ppermute | solution.py:18
  16.5 10.3 %collective-permute-start.10 = (f32[48,1152]{1,0:T(8,128)S(1)}, f32[48,1152]{1,0:T(8,128)S(1)}, u32[]{:S(2)}, u32[]{:S(2)}) collective-permute-start(f32[48,1152]{1,0:T(8,128)S(1)} %collective-permute-done.9.refs_6_), channel_id=1, source_target_pairs={{0,56},{8,0},{16,8},{24,16},{32,24},{40,32},{48,40},{56,48},{1,57}... | collective-permute-start | bytes 663560 | tf_op jit(solution)/shard_map/ppermute | solution.py:18
  19.7 9.6 %collective-permute-start.15 = (f32[48,1152]{1,0:T(8,128)S(1)}, f32[48,1152]{1,0:T(8,128)S(1)}, u32[]{:S(2)}, u32[]{:S(2)}) collective-permute-start(f32[48,1152]{1,0:T(8,128)S(1)} %collective-permute-done.9.refs_6_), channel_id=1, source_target_pairs={{0,8},{8,16},{16,24},{24,32},{32,40},{40,48},{48,56},{56,0},{1,9},... | collective-permute-start | bytes 663560 | tf_op jit(solution)/shard_map/ppermute | solution.py:18
  22.0 12.6 %collective-permute-start.2 = (f32[48,1152]{1,0:T(8,128)S(1)}, f32[48,1152]{1,0:T(8,128)S(1)}, u32[]{:S(2)}, u32[]{:S(2)}) collective-permute-start(f32[48,1152]{1,0:T(8,128)S(1)} %collective-permute-done.1.refs_2_), channel_id=1, source_target_pairs={{0,56},{8,0},{16,8},{24,16},{32,24},{40,32},{48,40},{56,48},{1,57}... | collective-permute-start | bytes 663560 | tf_op jit(solution)/shard_map/ppermute | solution.py:18
  25.9 15.2 %collective-permute-start.3 = (f32[48,1152]{1,0:T(8,128)S(1)}, f32[48,1152]{1,0:T(8,128)S(1)}, u32[]{:S(2)}, u32[]{:S(2)}) collective-permute-start(f32[48,1152]{1,0:T(8,128)S(1)} %collective-permute-done.1.refs_2_), channel_id=1, source_target_pairs={{0,48},{8,56},{16,0},{24,8},{32,16},{40,24},{48,32},{56,40},{1,49}... | collective-permute-start | bytes 663560 | tf_op jit(solution)/shard_map/ppermute | solution.py:18
  26.7 16.5 %collective-permute-start.6 = (f32[48,1152]{1,0:T(8,128)S(1)}, f32[48,1152]{1,0:T(8,128)S(1)}, u32[]{:S(2)}, u32[]{:S(2)}) collective-permute-start(f32[48,1152]{1,0:T(8,128)S(1)} %collective-permute-done.5.refs_6_), channel_id=1, source_target_pairs={{0,8},{8,16},{16,24},{24,32},{32,40},{40,48},{48,56},{56,0},{1,9},... | collective-permute-start | bytes 663560 | tf_op jit(solution)/shard_map/ppermute | solution.py:18
  29.3 22.2 %collective-permute-start.11 = (f32[48,1152]{1,0:T(8,128)S(1)}, f32[48,1152]{1,0:T(8,128)S(1)}, u32[]{:S(2)}, u32[]{:S(2)}) collective-permute-start(f32[48,1152]{1,0:T(8,128)S(1)} %collective-permute-done.10.refs_7_), channel_id=1, source_target_pairs={{0,56},{8,0},{16,8},{24,16},{32,24},{40,32},{48,40},{56,48},{1,57}... | collective-permute-start | bytes 663560 | tf_op jit(solution)/shard_map/ppermute | solution.py:18
  34.6 16.9 %collective-permute-start.16 = (f32[48,1152]{1,0:T(8,128)S(1)}, f32[48,1152]{1,0:T(8,128)S(1)}, u32[]{:S(2)}, u32[]{:S(2)}) collective-permute-start(f32[48,1152]{1,0:T(8,128)S(1)} %collective-permute-done.15.refs_5_), channel_id=1, source_target_pairs={{0,8},{8,16},{16,24},{24,32},{32,40},{40,48},{48,56},{56,0},{1,9},... | collective-permute-start | bytes 663560 | tf_op jit(solution)/shard_map/ppermute | solution.py:18
  41.1 10.4 %collective-permute-start.12 = (f32[48,1152]{1,0:T(8,128)S(1)}, f32[48,1152]{1,0:T(8,128)S(1)}, u32[]{:S(2)}, u32[]{:S(2)}) collective-permute-start(f32[48,1152]{1,0:T(8,128)S(1)} %collective-permute-done.2.refs_3_), channel_id=1, source_target_pairs={{0,192},{64,128},{128,64},{192,0},{1,193},{65,129},{129,65},{193,1... | collective-permute-start | bytes 663560 | tf_op jit(solution)/shard_map/ppermute | solution.py:26
  43.3 8.3 %collective-permute-start.13 = (f32[48,1152]{1,0:T(8,128)S(1)}, f32[48,1152]{1,0:T(8,128)S(1)}, u32[]{:S(2)}, u32[]{:S(2)}) collective-permute-start(f32[48,1152]{1,0:T(8,128)S(1)} %collective-permute-done.3.refs_4_), channel_id=1, source_target_pairs={{0,192},{64,128},{128,64},{192,0},{1,193},{65,129},{129,65},{193,1... | collective-permute-start | bytes 663560 | tf_op jit(solution)/shard_map/ppermute | solution.py:26
  44.3 9.1 %collective-permute-start.14 = (f32[48,1152]{1,0:T(8,128)S(1)}, f32[48,1152]{1,0:T(8,128)S(1)}, u32[]{:S(2)}, u32[]{:S(2)}) collective-permute-start(f32[48,1152]{1,0:T(8,128)S(1)} %collective-permute-done.6.refs_5_), channel_id=1, source_target_pairs={{0,192},{64,128},{128,64},{192,0},{1,193},{65,129},{129,65},{193,1... | collective-permute-start | bytes 663560 | tf_op jit(solution)/shard_map/ppermute | solution.py:26
  46.5 1.3 copy-start.1
  47.8 0.9 copy-start.3
  48.8 56.4 %copy-start = (f32[48,96,500]{2,1,0:T(8,128)S(1)}, f32[48,96,500]{2,1,0:T(8,128)}, u32[]{:S(2)}) copy-start(f32[48,96,500]{2,1,0:T(8,128)} %refs_10_.1) | copy-start | bytes 27648004
  56.1 2.0 %collective-permute-start.17 = (f32[192,576]{1,0:T(8,128)S(1)}, f32[192,576]{1,0:T(8,128)S(1)}, u32[]{:S(2)}, u32[]{:S(2)}) collective-permute-start(f32[192,576]{1,0:T(8,128)S(1)} %get-tuple-element.28), channel_id=1, source_target_pairs={{0,2},{2,0},{1,3},{3,1},{4,6},{6,4},{5,7},{7,5},{8,10},{10,8},{9,1... | collective-permute-start | bytes 1327112 | tf_op jit(solution)/shard_map/ppermute | solution.py:22
  56.2 2.6 %collective-permute-start.8 = (f32[192,576]{1,0:T(8,128)S(1)}, f32[192,576]{1,0:T(8,128)S(1)}, u32[]{:S(2)}, u32[]{:S(2)}) collective-permute-start(f32[192,576]{1,0:T(8,128)S(1)} %get-tuple-element.24), channel_id=1, source_target_pairs={{0,2},{2,0},{1,3},{3,1},{4,6},{6,4},{5,7},{7,5},{8,10},{10,8},{9,1... | collective-permute-start | bytes 1327112 | tf_op jit(solution)/shard_map/ppermute | solution.py:22
  59.0 5.2 %collective-permute-start.18 = (f32[24,1152]{1,0:T(8,128)S(1)}, f32[24,1152]{1,0:T(8,128)S(1)}, u32[]{:S(2)}, u32[]{:S(2)}) collective-permute-start(f32[24,1152]{1,0:T(8,128)S(1)} %get-tuple-element.31), channel_id=1, source_target_pairs={{0,1},{1,4},{4,5},{5,0},{2,3},{3,6},{6,7},{7,2},{8,9},{9,12},{12,1... | collective-permute-start | bytes 331784 | tf_op jit(solution)/shard_map/ppermute | solution.py:18
  59.5 6.0 %collective-permute-start.19 = (f32[24,1152]{1,0:T(8,128)S(1)}, f32[24,1152]{1,0:T(8,128)S(1)}, u32[]{:S(2)}, u32[]{:S(2)}) collective-permute-start(f32[24,1152]{1,0:T(8,128)S(1)} %get-tuple-element.33), channel_id=1, source_target_pairs={{0,5},{1,0},{4,1},{5,4},{2,7},{3,2},{6,3},{7,6},{8,13},{9,8},{12,9... | collective-permute-start | bytes 331784 | tf_op jit(solution)/shard_map/ppermute | solution.py:18
  65.6 6.4 %collective-permute-start.20 = (f32[48,1152]{1,0:T(8,128)S(1)}, f32[48,1152]{1,0:T(8,128)S(1)}, u32[]{:S(2)}, u32[]{:S(2)}) collective-permute-start(f32[48,1152]{1,0:T(8,128)S(1)} %get-tuple-element.34), channel_id=1, source_target_pairs={{0,1},{1,4},{4,5},{5,0},{2,3},{3,6},{6,7},{7,2},{8,9},{9,12},{12,1... | collective-permute-start | bytes 663560 | tf_op jit(solution)/shard_map/ppermute | solution.py:18
  66.0 7.6 %collective-permute-start.21 = (f32[48,1152]{1,0:T(8,128)S(1)}, f32[48,1152]{1,0:T(8,128)S(1)}, u32[]{:S(2)}, u32[]{:S(2)}) collective-permute-start(f32[48,1152]{1,0:T(8,128)S(1)} %get-tuple-element.35), channel_id=1, source_target_pairs={{0,5},{1,0},{4,1},{5,4},{2,7},{3,2},{6,3},{7,6},{8,13},{9,8},{12,9... | collective-permute-start | bytes 663560 | tf_op jit(solution)/shard_map/ppermute | solution.py:18
  73.6 12.2 %collective-permute-start.22 = (f32[48,576]{1,0:T(8,128)S(1)}, f32[48,576]{1,0:T(8,128)S(1)}, u32[]{:S(2)}, u32[]{:S(2)}) collective-permute-start(f32[48,576]{1,0:T(8,128)S(1)} %get-tuple-element.36), channel_id=1, source_target_pairs={{0,0},{2,34},{1,9},{3,43},{4,20},{6,54},{5,29},{7,63},{8,8},{10,42... | collective-permute-start | bytes 331784 | tf_op jit(solution)/shard_map/ppermute | solution.py:281
  77.4 12.7 %collective-permute-start.23 = (f32[48,576]{1,0:T(8,128)S(1)}, f32[48,576]{1,0:T(8,128)S(1)}, u32[]{:S(2)}, u32[]{:S(2)}) collective-permute-start(f32[48,576]{1,0:T(8,128)S(1)} %get-tuple-element.37), channel_id=1, source_target_pairs={{0,208},{2,242},{1,217},{3,251},{4,228},{6,198},{5,237},{7,207},{8... | collective-permute-start | bytes 331784 | tf_op jit(solution)/shard_map/ppermute | solution.py:281
  90.2 7.2 %collective-permute-start.24 = (f32[48,1152]{1,0:T(8,128)S(1)}, f32[48,1152]{1,0:T(8,128)S(1)}, u32[]{:S(2)}, u32[]{:S(2)}) collective-permute-start(f32[48,1152]{1,0:T(8,128)S(1)} %shard_map.81.refs_0_), channel_id=1, source_target_pairs={{0,5},{1,0},{4,1},{5,4},{2,7},{3,2},{6,3},{7,6},{8,13},{9,8},{12,9... | collective-permute-start | bytes 663560 | tf_op jit(solution)/shard_map/ppermute | solution.py:18
  90.3 7.5 %collective-permute-start.26 = (f32[48,1152]{1,0:T(8,128)S(1)}, f32[48,1152]{1,0:T(8,128)S(1)}, u32[]{:S(2)}, u32[]{:S(2)}) collective-permute-start(f32[48,1152]{1,0:T(8,128)S(1)} %shard_map.81.refs_0_), channel_id=1, source_target_pairs={{0,1},{1,4},{4,5},{5,0},{2,3},{3,6},{6,7},{7,2},{8,9},{9,12},{12,1... | collective-permute-start | bytes 663560 | tf_op jit(solution)/shard_map/ppermute | solution.py:18
  93.5 10.7 %collective-permute-start.28 = (f32[48,1152]{1,0:T(8,128)S(1)}, f32[48,1152]{1,0:T(8,128)S(1)}, u32[]{:S(2)}, u32[]{:S(2)}) collective-permute-start(f32[48,1152]{1,0:T(8,128)S(1)} %shard_map.81.refs_0_), channel_id=1, source_target_pairs={{0,2},{2,0},{1,3},{3,1},{4,6},{6,4},{5,7},{7,5},{8,10},{10,8},{9,1... | collective-permute-start | bytes 663560 | tf_op jit(solution)/shard_map/ppermute | solution.py:22
  97.4 6.3 %collective-permute-start.25 = (f32[24,1152]{1,0:T(8,128)S(1)}, f32[24,1152]{1,0:T(8,128)S(1)}, u32[]{:S(2)}, u32[]{:S(2)}) collective-permute-start(f32[24,1152]{1,0:T(8,128)S(1)} %slice.8), channel_id=1, source_target_pairs={{0,5},{1,0},{4,1},{5,4},{2,7},{3,2},{6,3},{7,6},{8,13},{9,8},{12,9... | collective-permute-start | bytes 331784 | tf_op jit(solution)/shard_map/ppermute | solution.py:18
  97.8 5.9 %collective-permute-start.27 = (f32[24,1152]{1,0:T(8,128)S(1)}, f32[24,1152]{1,0:T(8,128)S(1)}, u32[]{:S(2)}, u32[]{:S(2)}) collective-permute-start(f32[24,1152]{1,0:T(8,128)S(1)} %slice.9), channel_id=1, source_target_pairs={{0,1},{1,4},{4,5},{5,0},{2,3},{3,6},{6,7},{7,2},{8,9},{9,12},{12,1... | collective-permute-start | bytes 331784 | tf_op jit(solution)/shard_map/ppermute | solution.py:18
  101.1 4.1 %collective-permute-start.29 = (f32[48,1152]{1,0:T(8,128)S(1)}, f32[48,1152]{1,0:T(8,128)S(1)}, u32[]{:S(2)}, u32[]{:S(2)}) collective-permute-start(f32[48,1152]{1,0:T(8,128)S(1)} %collective-permute-done.24.refs_1_), channel_id=1, source_target_pairs={{0,2},{2,0},{1,3},{3,1},{4,6},{6,4},{5,7},{7,5},{8,10},{10,8},{9,1... | collective-permute-start | bytes 663560 | tf_op jit(solution)/shard_map/ppermute | solution.py:22
  101.1 4.1 %collective-permute-start.32 = (f32[48,1152]{1,0:T(8,128)S(1)}, f32[48,1152]{1,0:T(8,128)S(1)}, u32[]{:S(2)}, u32[]{:S(2)}) collective-permute-start(f32[48,1152]{1,0:T(8,128)S(1)} %collective-permute-done.26.refs_4_), channel_id=1, source_target_pairs={{0,2},{2,0},{1,3},{3,1},{4,6},{6,4},{5,7},{7,5},{8,10},{10,8},{9,1... | collective-permute-start | bytes 663560 | tf_op jit(solution)/shard_map/ppermute | solution.py:22
  103.7 1.3 collective-permute-start.30
  103.7 1.5 collective-permute-start.31
  110.8 35.4 %copy-start.2 = (f32[125,500]{0,1:T(8,128)S(1)}, f32[125,500]{0,1:T(8,128)}, u32[]{:S(2)}) copy-start(f32[125,500]{0,1:T(8,128)} %param.8) | copy-start | bytes 750004
  110.8 41.8 %copy-start.4 = (f32[125,96]{0,1:T(8,128)S(1)}, f32[125,96]{0,1:T(8,128)}, u32[]{:S(2)}) copy-start(f32[125,96]{0,1:T(8,128)} %param.9) | copy-start | bytes 144004
  126.2 5.5 %collective-permute-start.33 = (f32[48,128]{1,0:T(8,128)S(1)}, f32[48,128]{1,0:T(8,128)S(1)}, u32[]{:S(2)}, u32[]{:S(2)}) collective-permute-start(f32[48,128]{1,0:T(8,128)S(1)} %reduce_sum.9), channel_id=1, source_target_pairs={{0,128},{64,192},{128,0},{192,64},{1,129},{65,193},{129,1},{193,65... | collective-permute-start | bytes 73736 | tf_op jit(solution)/shard_map/ppermute | solution.py:26
  126.5 5.2 %collective-permute-start.34 = (f32[48,128]{1,0:T(8,128)S(1)}, f32[48,128]{1,0:T(8,128)S(1)}, u32[]{:S(2)}, u32[]{:S(2)}) collective-permute-start(f32[48,128]{1,0:T(8,128)S(1)} %reduce_sum.9), channel_id=1, source_target_pairs={{0,64},{64,0},{128,192},{192,128},{1,65},{65,1},{129,193},{193,129... | collective-permute-start | bytes 73736 | tf_op jit(solution)/shard_map/ppermute | solution.py:26
  129.0 5.0 %collective-permute-start.35 = (f32[48,128]{1,0:T(8,128)S(1)}, f32[48,128]{1,0:T(8,128)S(1)}, u32[]{:S(2)}, u32[]{:S(2)}) collective-permute-start(f32[48,128]{1,0:T(8,128)S(1)} %reduce_sum.9), channel_id=1, source_target_pairs={{0,192},{64,128},{128,64},{192,0},{1,193},{65,129},{129,65},{193,1... | collective-permute-start | bytes 73736 | tf_op jit(solution)/shard_map/ppermute | solution.py:26
  146.5 1.3 collective-permute-start.36
  147.9 5.1 %collective-permute-start.37 = (f32[104,125]{1,0:T(8,128)S(1)}, f32[104,125]{1,0:T(8,128)S(1)}, u32[]{:S(2)}, u32[]{:S(2)}) collective-permute-start(f32[104,125]{1,0:T(8,128)S(1)} %add.15.a_ref), channel_id=1, source_target_pairs={{0,1},{1,0},{4,5},{5,4},{2,3},{3,2},{6,7},{7,6},{8,9},{9,8},{12,13... | collective-permute-start | bytes 156008 | tf_op jit(solution)/shard_map/ppermute | solution.py:26
  148.0 7.4 %collective-permute-start.38 = (f32[104,125]{1,0:T(8,128)S(1)}, f32[104,125]{1,0:T(8,128)S(1)}, u32[]{:S(2)}, u32[]{:S(2)}) collective-permute-start(f32[104,125]{1,0:T(8,128)S(1)} %add.15.a_ref), channel_id=1, source_target_pairs={{0,4},{1,5},{4,0},{5,1},{2,6},{3,7},{6,2},{7,3},{8,12},{9,13},{12,... | collective-permute-start | bytes 156008 | tf_op jit(solution)/shard_map/ppermute | solution.py:26
  152.4 5.3 %collective-permute-start.39 = (f32[104,125]{1,0:T(8,128)S(1)}, f32[104,125]{1,0:T(8,128)S(1)}, u32[]{:S(2)}, u32[]{:S(2)}) collective-permute-start(f32[104,125]{1,0:T(8,128)S(1)} %add.15.a_ref), channel_id=1, source_target_pairs={{0,5},{1,4},{4,1},{5,0},{2,7},{3,6},{6,3},{7,2},{8,13},{9,12},{12,... | collective-permute-start | bytes 156008 | tf_op jit(solution)/shard_map/ppermute | solution.py:26

commit v4 on v2

--- a/solution.py
+++ b/solution.py
@@ -81,7 +81,11 @@
         out_shape=(shape, shape) + ((parts, parts) if fresh else ()),
         scratch_shapes=[pltpu.VMEM((n_rows, depth), jnp.bfloat16)] * 2,
         compiler_params=pltpu.CompilerParams(vmem_limit_bytes=16 * 2**20),
-        cost_estimate=pl.CostEstimate(flops=1000, bytes_accessed=1000, transcendentals=0),
+        cost_estimate=pl.CostEstimate(
+            flops=1000 if fresh else 6 * n_rows * n_cols * depth,
+            bytes_accessed=1000 if fresh else 4 * (n_rows + n_cols) * depth,
+            transcendentals=0,
+        ),
     )(*p_pieces, *rows)
 
 
@@ -163,10 +167,11 @@
 
     def step(i, carry):
         total = acc_ref[...]
-        for j in range(per_step):
+        for j in range(0, per_step, 2):
             q = i * per_step + j
-            head, rest = split(sorted_ref[pl.ds(q, nact, stride=naux), :])
-            b_head, b_rest = split(b_ref[q])
+            left = [sorted_ref[pl.ds(q + side, nact, stride=naux), :] for side in range(2)]
+            head, rest = split(jnp.concatenate(left, axis=1))
+            b_head, b_rest = split(b_ref[pl.ds(q, 2)].reshape(2 * nact, b_ref.shape[2]))
             both = jnp.dot(jnp.concatenate([head, rest]), b_head, preferred_element_type=jnp.float32)
             total += jnp.dot(head, b_rest, preferred_element_type=jnp.float32) + both[:nact] + both[nact:]
         acc_ref[...] = total

time: 155 us -> 154 us (level)
  no operation moved by 1% of the time
where the time goes in v4:
time: 154 us
  starting transfers between devices  61.6 us (40%)
  waiting for transfers between devices  48.9 us (32%)
  blocking collectives  28.2 us (18%)
  Pallas kernels  12.1 us (8%)
  local copies, waits for them, and re-layouts  2.31 us (2%)
    ppermute x19, starting transfers between devices, shift(): lax.ppermute(value, axis, [(i, (i + step) % size) for i in range(size)])  33.7 us
    ppermute x19, waiting for transfers between devices, shift(): lax.ppermute(value, axis, [(i, (i + step) % size) for i in range(size)])  27.2 us
    ppermute x11, starting transfers between devices, swap(): return lax.ppermute(value, axis, [(i, i ^ mask) for i in range(size)])  18.3 us
    all_to_all x1, blocking collectives, on_device(): lax.all_to_all(tiles, 'z', split_axis=0, concat_axis=0, tiled=True)  16 us
    all_to_all x1, blocking collectives, on_device(): lax.all_to_all(jnp.broadcast_to(piece[None], tiles.shape), 'z', split_axi...  12.2 us
    ppermute x11, waiting for transfers between devices, swap(): return lax.ppermute(value, axis, [(i, i ^ mask) for i in range(size)])  11.5 us
    ppermute x2, starting transfers between devices, send_home(): return lax.ppermute(value, ('y', 'z', 'xh', 'co', 'xl'), pairs)  7.93 us
    ppermute x2, waiting for transfers between devices, send_home(): return lax.ppermute(value, ('y', 'z', 'xh', 'co', 'xl'), pairs)  5.98 us
  transfers between devices with their start and end apart: 40, of which 25 were waited for; matrix products, arithmetic and copies ran while one was open for 0% of the time, Pallas kernels for 2%

profile of v4, /device:TPU:6, one launch (start us, length us, event | category | flops | bytes accessed | tf_op | source)
XLA Modules:
  0.0 153.9 jit_solution(9256314649630617355)
XLA Ops:
  0.6 1.7 %collective-permute-start.7 = (f32[288,1152]{1,0:T(8,128)}, f32[288,1152]{1,0:T(8,128)S(1)}, u32[]{:S(2)}, u32[]{:S(2)}) collective-permute-start(f32[288,1152]{1,0:T(8,128)} %refs_8_.1), channel_id=1, source_target_pairs={{0,64},{64,0},{128,192},{192,128},{1,65},{65,1},{129,193},{193,129... | collective-permute-start | bytes 3981320 | tf_op jit(solution)/shard_map/ppermute | solution.py:26
  2.3 5.9 %collective-permute-start = (f32[48,1152]{1,0:T(8,128)}, f32[48,1152]{1,0:T(8,128)S(1)}, u32[]{:S(2)}, u32[]{:S(2)}) collective-permute-start(f32[48,1152]{1,0:T(8,128)} %refs_0_.1), channel_id=1, source_target_pairs={{0,56},{8,0},{16,8},{24,16},{32,24},{40,32},{48,40},{56,48},{1,57}... | collective-permute-start | bytes 663560 | tf_op jit(solution)/shard_map/ppermute | solution.py:18
  8.2 4.7 %collective-permute-done.refs_1_ = f32[48,1152]{1,0:T(8,128)S(1)} collective-permute-done((f32[48,1152]{1,0:T(8,128)}, f32[48,1152]{1,0:T(8,128)S(1)}, u32[]{:S(2)}, u32[]{:S(2)}) %collective-permute-start) | collective-permute-done | bytes 221216 | tf_op jit(solution)/shard_map/ppermute | solution.py:18
  12.9 3.6 %collective-permute-start.1 = (f32[48,1152]{1,0:T(8,128)S(1)}, f32[48,1152]{1,0:T(8,128)S(1)}, u32[]{:S(2)}, u32[]{:S(2)}) collective-permute-start(f32[48,1152]{1,0:T(8,128)S(1)} %collective-permute-done.refs_1_), channel_id=1, source_target_pairs={{0,56},{8,0},{16,8},{24,16},{32,24},{40,32},{48,40},{56,48},{1,57}... | collective-permute-start | bytes 663560 | tf_op jit(solution)/shard_map/ppermute | solution.py:18
  16.5 2.2 %collective-permute-start.9 = (f32[48,1152]{1,0:T(8,128)}, f32[48,1152]{1,0:T(8,128)S(1)}, u32[]{:S(2)}, u32[]{:S(2)}) collective-permute-start(f32[48,1152]{1,0:T(8,128)} %refs_0_.1), channel_id=1, source_target_pairs={{0,192},{64,128},{128,64},{192,0},{1,193},{65,129},{129,65},{193,1... | collective-permute-start | bytes 663560 | tf_op jit(solution)/shard_map/ppermute | solution.py:26
  18.6 1.3 collective-permute-done.1.refs_2_
  20.0 3.7 %collective-permute-start.2 = (f32[48,1152]{1,0:T(8,128)S(1)}, f32[48,1152]{1,0:T(8,128)S(1)}, u32[]{:S(2)}, u32[]{:S(2)}) collective-permute-start(f32[48,1152]{1,0:T(8,128)S(1)} %collective-permute-done.1.refs_2_), channel_id=1, source_target_pairs={{0,56},{8,0},{16,8},{24,16},{32,24},{40,32},{48,40},{56,48},{1,57}... | collective-permute-start | bytes 663560 | tf_op jit(solution)/shard_map/ppermute | solution.py:18
  23.9 2.0 %collective-permute-start.15 = (f32[48,1152]{1,0:T(8,128)S(1)}, f32[48,1152]{1,0:T(8,128)S(1)}, u32[]{:S(2)}, u32[]{:S(2)}) collective-permute-start(f32[48,1152]{1,0:T(8,128)S(1)} %collective-permute-done.9.refs_6_), channel_id=1, source_target_pairs={{0,8},{8,16},{16,24},{24,32},{32,40},{40,48},{48,56},{56,0},{1,9},... | collective-permute-start | bytes 663560 | tf_op jit(solution)/shard_map/ppermute | solution.py:18
  26.4 3.0 %collective-permute-done.2.refs_3_ = f32[48,1152]{1,0:T(8,128)S(1)} collective-permute-done((f32[48,1152]{1,0:T(8,128)S(1)}, f32[48,1152]{1,0:T(8,128)S(1)}, u32[]{:S(2)}, u32[]{:S(2)}) %collective-permute-start.2) | collective-permute-done | bytes 221216 | tf_op jit(solution)/shard_map/ppermute | solution.py:18
  29.4 3.7 %collective-permute-start.3 = (f32[48,1152]{1,0:T(8,128)S(1)}, f32[48,1152]{1,0:T(8,128)S(1)}, u32[]{:S(2)}, u32[]{:S(2)}) collective-permute-start(f32[48,1152]{1,0:T(8,128)S(1)} %collective-permute-done.2.refs_3_), channel_id=1, source_target_pairs={{0,56},{8,0},{16,8},{24,16},{32,24},{40,32},{48,40},{56,48},{1,57}... | collective-permute-start | bytes 663560 | tf_op jit(solution)/shard_map/ppermute | solution.py:18
  33.1 1.0 collective-permute-done.10.refs_7_
  34.1 3.7 %collective-permute-start.11 = (f32[48,1152]{1,0:T(8,128)S(1)}, f32[48,1152]{1,0:T(8,128)S(1)}, u32[]{:S(2)}, u32[]{:S(2)}) collective-permute-start(f32[48,1152]{1,0:T(8,128)S(1)} %collective-permute-done.10.refs_7_), channel_id=1, source_target_pairs={{0,56},{8,0},{16,8},{24,16},{32,24},{40,32},{48,40},{56,48},{1,57}... | collective-permute-start | bytes 663560 | tf_op jit(solution)/shard_map/ppermute | solution.py:18
  37.8 2.3 %collective-permute-start.12 = (f32[48,1152]{1,0:T(8,128)S(1)}, f32[48,1152]{1,0:T(8,128)S(1)}, u32[]{:S(2)}, u32[]{:S(2)}) collective-permute-start(f32[48,1152]{1,0:T(8,128)S(1)} %collective-permute-done.2.refs_3_), channel_id=1, source_target_pairs={{0,192},{64,128},{128,64},{192,0},{1,193},{65,129},{129,65},{193,1... | collective-permute-start | bytes 663560 | tf_op jit(solution)/shard_map/ppermute | solution.py:26
  40.1 1.1 collective-permute-start.14
  41.1 2.2 %collective-permute-start.13 = (f32[48,1152]{1,0:T(8,128)S(1)}, f32[48,1152]{1,0:T(8,128)S(1)}, u32[]{:S(2)}, u32[]{:S(2)}) collective-permute-start(f32[48,1152]{1,0:T(8,128)S(1)} %collective-permute-done.3.refs_4_), channel_id=1, source_target_pairs={{0,192},{64,128},{128,64},{192,0},{1,193},{65,129},{129,65},{193,1... | collective-permute-start | bytes 663560 | tf_op jit(solution)/shard_map/ppermute | solution.py:26
  43.3 1.3 copy-done.1
  44.7 0.9 copy-done.3
  45.6 2.7 %shard_map.76 = (f32[192,576]{1,0:T(8,128)S(1)}, f32[192,576]{1,0:T(8,128)S(1)}, bf16[576,1152]{1,0:T(8,128)(2,1)S(1)}, bf16[576,1152]{1,0:T(8,128)(2,1)S(1)}) custom-call(f32[48,1152]{1,0:T(8,128)S(1)} %copy-done.3, f32[48,1152]{1,0:T(8,128)S(1)} %collective-permute-done.refs_1_, f32[48,1152]{1,0:T(8,128)S(1)} %collective-permute-done.1.refs_2_, ...), custom_call_target="tpu_custom_call" | custom-call | flops 1000 | bytes 1000 | tf_op jit(solution)/shard_map/pallas_call | solution.py:79
  48.4 2.1 %collective-permute-done.13.refs_2_ = f32[48,1152]{1,0:T(8,128)S(1)} collective-permute-done((f32[48,1152]{1,0:T(8,128)S(1)}, f32[48,1152]{1,0:T(8,128)S(1)}, u32[]{:S(2)}, u32[]{:S(2)}) %collective-permute-start.13) | collective-permute-done | bytes 221216 | tf_op jit(solution)/shard_map/ppermute | solution.py:26
  50.5 2.7 %shard_map.77 = (f32[192,576]{1,0:T(8,128)S(1)}, f32[192,576]{1,0:T(8,128)S(1)}) custom-call(f32[48,1152]{1,0:T(8,128)S(1)} %collective-permute-done.11.refs_0_, f32[48,1152]{1,0:T(8,128)S(1)} %collective-permute-done.12.refs_1_, f32[48,1152]{1,0:T(8,128)S(1)} %collective-permute-done.13.refs_2_, f32[48,1152]{1,0:T(8,128)S(1)} %collective-permute-done.14.refs_3_, ...), custom_call_target="tpu_custom_call" | custom-call | flops 1528823808 | bytes 4423680 | tf_op jit(solution)/shard_map/pallas_call | solution.py:79
  53.8 1.4 collective-permute-done.17.refs_3_
  56.6 1.5 %collective-permute-start.19 = (f32[24,1152]{1,0:T(8,128)S(1)}, f32[24,1152]{1,0:T(8,128)S(1)}, u32[]{:S(2)}, u32[]{:S(2)}) collective-permute-start(f32[24,1152]{1,0:T(8,128)S(1)} %get-tuple-element.33), channel_id=1, source_target_pairs={{0,5},{1,0},{4,1},{5,4},{2,7},{3,2},{6,3},{7,6},{8,13},{9,8},{12,9... | collective-permute-start | bytes 331784 | tf_op jit(solution)/shard_map/ppermute | solution.py:18
  58.1 3.1 %collective-permute-done.18.up_ref = f32[24,1152]{1,0:T(8,128)S(1)} collective-permute-done((f32[24,1152]{1,0:T(8,128)S(1)}, f32[24,1152]{1,0:T(8,128)S(1)}, u32[]{:S(2)}, u32[]{:S(2)}) %collective-permute-start.18) | collective-permute-done | bytes 110624 | tf_op jit(solution)/shard_map/ppermute | solution.py:18
  61.2 1.4 collective-permute-done.19.down_ref
  63.0 1.7 %collective-permute-start.21 = (f32[48,1152]{1,0:T(8,128)S(1)}, f32[48,1152]{1,0:T(8,128)S(1)}, u32[]{:S(2)}, u32[]{:S(2)}) collective-permute-start(f32[48,1152]{1,0:T(8,128)S(1)} %get-tuple-element.35), channel_id=1, source_target_pairs={{0,5},{1,0},{4,1},{5,4},{2,7},{3,2},{6,3},{7,6},{8,13},{9,8},{12,9... | collective-permute-start | bytes 663560 | tf_op jit(solution)/shard_map/ppermute | solution.py:18
  64.8 4.3 %collective-permute-done.20.one_ref = f32[48,1152]{1,0:T(8,128)S(1)} collective-permute-done((f32[48,1152]{1,0:T(8,128)S(1)}, f32[48,1152]{1,0:T(8,128)S(1)}, u32[]{:S(2)}, u32[]{:S(2)}) %collective-permute-start.20) | collective-permute-done | bytes 221216 | tf_op jit(solution)/shard_map/ppermute | solution.py:18
  69.1 1.5 collective-permute-done.21.two_ref
  70.7 3.6 %collective-permute-start.22 = (f32[48,576]{1,0:T(8,128)S(1)}, f32[48,576]{1,0:T(8,128)S(1)}, u32[]{:S(2)}, u32[]{:S(2)}) collective-permute-start(f32[48,576]{1,0:T(8,128)S(1)} %get-tuple-element.36), channel_id=1, source_target_pairs={{0,0},{2,34},{1,9},{3,43},{4,20},{6,54},{5,29},{7,63},{8,8},{10,42... | collective-permute-start | bytes 331784 | tf_op jit(solution)/shard_map/ppermute | solution.py:286
  74.4 4.3 %collective-permute-start.23 = (f32[48,576]{1,0:T(8,128)S(1)}, f32[48,576]{1,0:T(8,128)S(1)}, u32[]{:S(2)}, u32[]{:S(2)}) collective-permute-start(f32[48,576]{1,0:T(8,128)S(1)} %get-tuple-element.37), channel_id=1, source_target_pairs={{0,208},{2,242},{1,217},{3,251},{4,228},{6,198},{5,237},{7,207},{8... | collective-permute-start | bytes 331784 | tf_op jit(solution)/shard_map/ppermute | solution.py:286
  78.7 3.6 %collective-permute-done.22.first_ref = f32[48,576]{1,0:T(8,128)S(1)} collective-permute-done((f32[48,576]{1,0:T(8,128)S(1)}, f32[48,576]{1,0:T(8,128)S(1)}, u32[]{:S(2)}, u32[]{:S(2)}) %collective-permute-start.22) | collective-permute-done | bytes 110624 | tf_op jit(solution)/shard_map/ppermute | solution.py:286
  82.3 2.4 %collective-permute-done.23.second_ref = f32[48,576]{1,0:T(8,128)S(1)} collective-permute-done((f32[48,576]{1,0:T(8,128)S(1)}, f32[48,576]{1,0:T(8,128)S(1)}, u32[]{:S(2)}, u32[]{:S(2)}) %collective-permute-start.23) | collective-permute-done | bytes 110624 | tf_op jit(solution)/shard_map/ppermute | solution.py:286
  84.8 3.2 %collective-permute-start.26 = (f32[48,1152]{1,0:T(8,128)S(1)}, f32[48,1152]{1,0:T(8,128)S(1)}, u32[]{:S(2)}, u32[]{:S(2)}) collective-permute-start(f32[48,1152]{1,0:T(8,128)S(1)} %shard_map.81.refs_0_), channel_id=1, source_target_pairs={{0,1},{1,4},{4,5},{5,0},{2,3},{3,6},{6,7},{7,2},{8,9},{9,12},{12,1... | collective-permute-start | bytes 663560 | tf_op jit(solution)/shard_map/ppermute | solution.py:18
  88.1 4.1 %collective-permute-done.24.refs_1_ = f32[48,1152]{1,0:T(8,128)S(1)} collective-permute-done((f32[48,1152]{1,0:T(8,128)S(1)}, f32[48,1152]{1,0:T(8,128)S(1)}, u32[]{:S(2)}, u32[]{:S(2)}) %collective-permute-start.24) | collective-permute-done | bytes 221216 | tf_op jit(solution)/shard_map/ppermute | solution.py:18
  92.5 3.3 %collective-permute-start.27 = (f32[24,1152]{1,0:T(8,128)S(1)}, f32[24,1152]{1,0:T(8,128)S(1)}, u32[]{:S(2)}, u32[]{:S(2)}) collective-permute-start(f32[24,1152]{1,0:T(8,128)S(1)} %slice.9), channel_id=1, source_target_pairs={{0,1},{1,4},{4,5},{5,0},{2,3},{3,6},{6,7},{7,2},{8,9},{9,12},{12,1... | collective-permute-start | bytes 331784 | tf_op jit(solution)/shard_map/ppermute | solution.py:18
  96.3 2.1 %collective-permute-done.25.refs_2_ = f32[24,1152]{1,0:T(8,128)S(1)} collective-permute-done((f32[24,1152]{1,0:T(8,128)S(1)}, f32[24,1152]{1,0:T(8,128)S(1)}, u32[]{:S(2)}, u32[]{:S(2)}) %collective-permute-start.25) | collective-permute-done | bytes 110624 | tf_op jit(solution)/shard_map/ppermute | solution.py:18
  99.0 0.8 collective-permute-done.30.refs_7_
  99.9 4.8 %shard_map.82 = f32[8,48,128]{2,1,0:T(8,128)S(1)} custom-call(f32[48,1152]{1,0:T(8,128)S(1)} %shard_map.81.refs_0_, f32[48,1152]{1,0:T(8,128)S(1)} %collective-permute-done.24.refs_1_, f32[24,1152]{1,0:T(8,128)S(1)} %collective-permute-done.25.refs_2_, f32[24,1152]{1,0:T(8,128)S(1)} %collective-permute-done.27.refs_3_, ...), custom_call_target="tpu_custom_call" | custom-call | tf_op jit(solution)/shard_map/pallas_call | solution.py:196
  104.8 16.0 %all_to_all.10 = f32[8,48,128]{2,1,0:T(8,128)S(1)} all-to-all(f32[8,48,128]{2,1,0:T(8,128)S(1)} %shard_map.82), channel_id=1, replica_groups=mesh['y'=4,'z'=8,'xh'=2,'co'=2,'xl'=2] {'z'}, dimensions={0} | all-to-all | bytes 393216 | tf_op jit(solution)/shard_map/all_to_all | solution.py:303
  120.8 0.7 collective-permute-start.33
  121.5 2.9 %collective-permute-start.34 = (f32[48,128]{1,0:T(8,128)S(1)}, f32[48,128]{1,0:T(8,128)S(1)}, u32[]{:S(2)}, u32[]{:S(2)}) collective-permute-start(f32[48,128]{1,0:T(8,128)S(1)} %reduce_sum.9), channel_id=1, source_target_pairs={{0,64},{64,0},{128,192},{192,128},{1,65},{65,1},{129,193},{193,129... | collective-permute-start | bytes 73736 | tf_op jit(solution)/shard_map/ppermute | solution.py:26
  125.0 1.2 collective-permute-done.33
  126.4 3.0 %collective-permute-done.35 = f32[48,128]{1,0:T(8,128)S(1)} collective-permute-done((f32[48,128]{1,0:T(8,128)S(1)}, f32[48,128]{1,0:T(8,128)S(1)}, u32[]{:S(2)}, u32[]{:S(2)}) %collective-permute-start.35) | collective-permute-done | bytes 24608 | tf_op jit(solution)/shard_map/ppermute | solution.py:26
  129.4 12.2 %all_to_all.11.tiles_ref = f32[8,48,128]{2,1,0:T(8,128)S(1)} all-to-all(f32[8,48,128]{2,1,0:T(8,128)S(1)} %broadcast_in_dim.2), channel_id=1, replica_groups=mesh['y'=4,'z'=8,'xh'=2,'co'=2,'xl'=2] {'z'}, dimensions={0} | all-to-all | bytes 393216 | tf_op jit(solution)/shard_map/all_to_all | solution.py:305
  142.0 1.2 collective-permute-done.36
  143.3 4.4 %collective-permute-start.38 = (f32[104,125]{1,0:T(8,128)S(1)}, f32[104,125]{1,0:T(8,128)S(1)}, u32[]{:S(2)}, u32[]{:S(2)}) collective-permute-start(f32[104,125]{1,0:T(8,128)S(1)} %add.15.a_ref), channel_id=1, source_target_pairs={{0,4},{1,5},{4,0},{5,1},{2,6},{3,7},{6,2},{7,3},{8,12},{9,13},{12,... | collective-permute-start | bytes 156008 | tf_op jit(solution)/shard_map/ppermute | solution.py:26
  148.3 2.3 %collective-permute-done.38.c_ref = f32[104,125]{1,0:T(8,128)S(1)} collective-permute-done((f32[104,125]{1,0:T(8,128)S(1)}, f32[104,125]{1,0:T(8,128)S(1)}, u32[]{:S(2)}, u32[]{:S(2)}) %collective-permute-start.38) | collective-permute-done | bytes 52032 | tf_op jit(solution)/shard_map/ppermute | solution.py:26
  150.7 2.4 %collective-permute-done.39.d_ref = f32[104,125]{1,0:T(8,128)S(1)} collective-permute-done((f32[104,125]{1,0:T(8,128)S(1)}, f32[104,125]{1,0:T(8,128)S(1)}, u32[]{:S(2)}, u32[]{:S(2)}) %collective-permute-start.39) | collective-permute-done | bytes 52032 | tf_op jit(solution)/shard_map/ppermute | solution.py:26
  153.1 0.8 shard_map.85
  (60 shorter events, 7.0 us)
Async XLA Ops:
  0.6 40.5 %collective-permute-start.7 = (f32[288,1152]{1,0:T(8,128)}, f32[288,1152]{1,0:T(8,128)S(1)}, u32[]{:S(2)}, u32[]{:S(2)}) collective-permute-start(f32[288,1152]{1,0:T(8,128)} %refs_8_.1), channel_id=1, source_target_pairs={{0,64},{64,0},{128,192},{192,128},{1,65},{65,1},{129,193},{193,129... | collective-permute-start | bytes 3981320 | tf_op jit(solution)/shard_map/ppermute | solution.py:26
  2.3 10.6 %collective-permute-start = (f32[48,1152]{1,0:T(8,128)}, f32[48,1152]{1,0:T(8,128)S(1)}, u32[]{:S(2)}, u32[]{:S(2)}) collective-permute-start(f32[48,1152]{1,0:T(8,128)} %refs_0_.1), channel_id=1, source_target_pairs={{0,56},{8,0},{16,8},{24,16},{32,24},{40,32},{48,40},{56,48},{1,57}... | collective-permute-start | bytes 663560 | tf_op jit(solution)/shard_map/ppermute | solution.py:18
  8.1 10.5 %collective-permute-start.4 = (f32[48,1152]{1,0:T(8,128)}, f32[48,1152]{1,0:T(8,128)S(1)}, u32[]{:S(2)}, u32[]{:S(2)}) collective-permute-start(f32[48,1152]{1,0:T(8,128)} %refs_0_.1), channel_id=1, source_target_pairs={{0,8},{8,16},{16,24},{24,32},{32,40},{40,48},{48,56},{56,0},{1,9},... | collective-permute-start | bytes 663560 | tf_op jit(solution)/shard_map/ppermute | solution.py:18
  12.9 7.1 %collective-permute-start.1 = (f32[48,1152]{1,0:T(8,128)S(1)}, f32[48,1152]{1,0:T(8,128)S(1)}, u32[]{:S(2)}, u32[]{:S(2)}) collective-permute-start(f32[48,1152]{1,0:T(8,128)S(1)} %collective-permute-done.refs_1_), channel_id=1, source_target_pairs={{0,56},{8,0},{16,8},{24,16},{32,24},{40,32},{48,40},{56,48},{1,57}... | collective-permute-start | bytes 663560 | tf_op jit(solution)/shard_map/ppermute | solution.py:18
  16.5 7.4 %collective-permute-start.9 = (f32[48,1152]{1,0:T(8,128)}, f32[48,1152]{1,0:T(8,128)S(1)}, u32[]{:S(2)}, u32[]{:S(2)}) collective-permute-start(f32[48,1152]{1,0:T(8,128)} %refs_0_.1), channel_id=1, source_target_pairs={{0,192},{64,128},{128,64},{192,0},{1,193},{65,129},{129,65},{193,1... | collective-permute-start | bytes 663560 | tf_op jit(solution)/shard_map/ppermute | solution.py:26
  18.6 7.7 %collective-permute-start.5 = (f32[48,1152]{1,0:T(8,128)S(1)}, f32[48,1152]{1,0:T(8,128)S(1)}, u32[]{:S(2)}, u32[]{:S(2)}) collective-permute-start(f32[48,1152]{1,0:T(8,128)S(1)} %collective-permute-done.4.refs_7_), channel_id=1, source_target_pairs={{0,8},{8,16},{16,24},{24,32},{32,40},{40,48},{48,56},{56,0},{1,9},... | collective-permute-start | bytes 663560 | tf_op jit(solution)/shard_map/ppermute | solution.py:18
  20.0 9.4 %collective-permute-start.2 = (f32[48,1152]{1,0:T(8,128)S(1)}, f32[48,1152]{1,0:T(8,128)S(1)}, u32[]{:S(2)}, u32[]{:S(2)}) collective-permute-start(f32[48,1152]{1,0:T(8,128)S(1)} %collective-permute-done.1.refs_2_), channel_id=1, source_target_pairs={{0,56},{8,0},{16,8},{24,16},{32,24},{40,32},{48,40},{56,48},{1,57}... | collective-permute-start | bytes 663560 | tf_op jit(solution)/shard_map/ppermute | solution.py:18
  23.8 10.3 %collective-permute-start.10 = (f32[48,1152]{1,0:T(8,128)S(1)}, f32[48,1152]{1,0:T(8,128)S(1)}, u32[]{:S(2)}, u32[]{:S(2)}) collective-permute-start(f32[48,1152]{1,0:T(8,128)S(1)} %collective-permute-done.9.refs_6_), channel_id=1, source_target_pairs={{0,56},{8,0},{16,8},{24,16},{32,24},{40,32},{48,40},{56,48},{1,57}... | collective-permute-start | bytes 663560 | tf_op jit(solution)/shard_map/ppermute | solution.py:18
  23.9 13.9 %collective-permute-start.15 = (f32[48,1152]{1,0:T(8,128)S(1)}, f32[48,1152]{1,0:T(8,128)S(1)}, u32[]{:S(2)}, u32[]{:S(2)}) collective-permute-start(f32[48,1152]{1,0:T(8,128)S(1)} %collective-permute-done.9.refs_6_), channel_id=1, source_target_pairs={{0,8},{8,16},{16,24},{24,32},{32,40},{40,48},{48,56},{56,0},{1,9},... | collective-permute-start | bytes 663560 | tf_op jit(solution)/shard_map/ppermute | solution.py:18
  26.4 11.4 %collective-permute-start.6 = (f32[48,1152]{1,0:T(8,128)S(1)}, f32[48,1152]{1,0:T(8,128)S(1)}, u32[]{:S(2)}, u32[]{:S(2)}) collective-permute-start(f32[48,1152]{1,0:T(8,128)S(1)} %collective-permute-done.5.refs_6_), channel_id=1, source_target_pairs={{0,8},{8,16},{16,24},{24,32},{32,40},{40,48},{48,56},{56,0},{1,9},... | collective-permute-start | bytes 663560 | tf_op jit(solution)/shard_map/ppermute | solution.py:18
  29.4 10.7 %collective-permute-start.3 = (f32[48,1152]{1,0:T(8,128)S(1)}, f32[48,1152]{1,0:T(8,128)S(1)}, u32[]{:S(2)}, u32[]{:S(2)}) collective-permute-start(f32[48,1152]{1,0:T(8,128)S(1)} %collective-permute-done.2.refs_3_), channel_id=1, source_target_pairs={{0,56},{8,0},{16,8},{24,16},{32,24},{40,32},{48,40},{56,48},{1,57}... | collective-permute-start | bytes 663560 | tf_op jit(solution)/shard_map/ppermute | solution.py:18
  34.1 14.2 %collective-permute-start.11 = (f32[48,1152]{1,0:T(8,128)S(1)}, f32[48,1152]{1,0:T(8,128)S(1)}, u32[]{:S(2)}, u32[]{:S(2)}) collective-permute-start(f32[48,1152]{1,0:T(8,128)S(1)} %collective-permute-done.10.refs_7_), channel_id=1, source_target_pairs={{0,56},{8,0},{16,8},{24,16},{32,24},{40,32},{48,40},{56,48},{1,57}... | collective-permute-start | bytes 663560 | tf_op jit(solution)/shard_map/ppermute | solution.py:18
  37.8 10.5 %collective-permute-start.16 = (f32[48,1152]{1,0:T(8,128)S(1)}, f32[48,1152]{1,0:T(8,128)S(1)}, u32[]{:S(2)}, u32[]{:S(2)}) collective-permute-start(f32[48,1152]{1,0:T(8,128)S(1)} %collective-permute-done.15.refs_5_), channel_id=1, source_target_pairs={{0,8},{8,16},{16,24},{24,32},{32,40},{40,48},{48,56},{56,0},{1,9},... | collective-permute-start | bytes 663560 | tf_op jit(solution)/shard_map/ppermute | solution.py:18
  37.8 10.5 %collective-permute-start.12 = (f32[48,1152]{1,0:T(8,128)S(1)}, f32[48,1152]{1,0:T(8,128)S(1)}, u32[]{:S(2)}, u32[]{:S(2)}) collective-permute-start(f32[48,1152]{1,0:T(8,128)S(1)} %collective-permute-done.2.refs_3_), channel_id=1, source_target_pairs={{0,192},{64,128},{128,64},{192,0},{1,193},{65,129},{129,65},{193,1... | collective-permute-start | bytes 663560 | tf_op jit(solution)/shard_map/ppermute | solution.py:26
  40.1 8.3 %collective-permute-start.14 = (f32[48,1152]{1,0:T(8,128)S(1)}, f32[48,1152]{1,0:T(8,128)S(1)}, u32[]{:S(2)}, u32[]{:S(2)}) collective-permute-start(f32[48,1152]{1,0:T(8,128)S(1)} %collective-permute-done.6.refs_5_), channel_id=1, source_target_pairs={{0,192},{64,128},{128,64},{192,0},{1,193},{65,129},{129,65},{193,1... | collective-permute-start | bytes 663560 | tf_op jit(solution)/shard_map/ppermute | solution.py:26
  41.1 9.3 %collective-permute-start.13 = (f32[48,1152]{1,0:T(8,128)S(1)}, f32[48,1152]{1,0:T(8,128)S(1)}, u32[]{:S(2)}, u32[]{:S(2)}) collective-permute-start(f32[48,1152]{1,0:T(8,128)S(1)} %collective-permute-done.3.refs_4_), channel_id=1, source_target_pairs={{0,192},{64,128},{128,64},{192,0},{1,193},{65,129},{129,65},{193,1... | collective-permute-start | bytes 663560 | tf_op jit(solution)/shard_map/ppermute | solution.py:26
  43.3 1.3 copy-start.1
  44.6 0.9 copy-start.3
  50.5 49.5 %copy-start = (f32[48,96,500]{2,1,0:T(8,128)S(1)}, f32[48,96,500]{2,1,0:T(8,128)}, u32[]{:S(2)}) copy-start(f32[48,96,500]{2,1,0:T(8,128)} %refs_10_.1) | copy-start | bytes 27648004
  53.2 2.0 %collective-permute-start.17 = (f32[192,576]{1,0:T(8,128)S(1)}, f32[192,576]{1,0:T(8,128)S(1)}, u32[]{:S(2)}, u32[]{:S(2)}) collective-permute-start(f32[192,576]{1,0:T(8,128)S(1)} %get-tuple-element.28), channel_id=1, source_target_pairs={{0,2},{2,0},{1,3},{3,1},{4,6},{6,4},{5,7},{7,5},{8,10},{10,8},{9,1... | collective-permute-start | bytes 1327112 | tf_op jit(solution)/shard_map/ppermute | solution.py:22
  53.3 2.6 %collective-permute-start.8 = (f32[192,576]{1,0:T(8,128)S(1)}, f32[192,576]{1,0:T(8,128)S(1)}, u32[]{:S(2)}, u32[]{:S(2)}) collective-permute-start(f32[192,576]{1,0:T(8,128)S(1)} %get-tuple-element.24), channel_id=1, source_target_pairs={{0,2},{2,0},{1,3},{3,1},{4,6},{6,4},{5,7},{7,5},{8,10},{10,8},{9,1... | collective-permute-start | bytes 1327112 | tf_op jit(solution)/shard_map/ppermute | solution.py:22
  56.0 5.2 %collective-permute-start.18 = (f32[24,1152]{1,0:T(8,128)S(1)}, f32[24,1152]{1,0:T(8,128)S(1)}, u32[]{:S(2)}, u32[]{:S(2)}) collective-permute-start(f32[24,1152]{1,0:T(8,128)S(1)} %get-tuple-element.31), channel_id=1, source_target_pairs={{0,1},{1,4},{4,5},{5,0},{2,3},{3,6},{6,7},{7,2},{8,9},{9,12},{12,1... | collective-permute-start | bytes 331784 | tf_op jit(solution)/shard_map/ppermute | solution.py:18
  56.6 6.0 %collective-permute-start.19 = (f32[24,1152]{1,0:T(8,128)S(1)}, f32[24,1152]{1,0:T(8,128)S(1)}, u32[]{:S(2)}, u32[]{:S(2)}) collective-permute-start(f32[24,1152]{1,0:T(8,128)S(1)} %get-tuple-element.33), channel_id=1, source_target_pairs={{0,5},{1,0},{4,1},{5,4},{2,7},{3,2},{6,3},{7,6},{8,13},{9,8},{12,9... | collective-permute-start | bytes 331784 | tf_op jit(solution)/shard_map/ppermute | solution.py:18
  62.7 6.4 %collective-permute-start.20 = (f32[48,1152]{1,0:T(8,128)S(1)}, f32[48,1152]{1,0:T(8,128)S(1)}, u32[]{:S(2)}, u32[]{:S(2)}) collective-permute-start(f32[48,1152]{1,0:T(8,128)S(1)} %get-tuple-element.34), channel_id=1, source_target_pairs={{0,1},{1,4},{4,5},{5,0},{2,3},{3,6},{6,7},{7,2},{8,9},{9,12},{12,1... | collective-permute-start | bytes 663560 | tf_op jit(solution)/shard_map/ppermute | solution.py:18
  63.0 7.6 %collective-permute-start.21 = (f32[48,1152]{1,0:T(8,128)S(1)}, f32[48,1152]{1,0:T(8,128)S(1)}, u32[]{:S(2)}, u32[]{:S(2)}) collective-permute-start(f32[48,1152]{1,0:T(8,128)S(1)} %get-tuple-element.35), channel_id=1, source_target_pairs={{0,5},{1,0},{4,1},{5,4},{2,7},{3,2},{6,3},{7,6},{8,13},{9,8},{12,9... | collective-permute-start | bytes 663560 | tf_op jit(solution)/shard_map/ppermute | solution.py:18
  70.7 11.5 %collective-permute-start.22 = (f32[48,576]{1,0:T(8,128)S(1)}, f32[48,576]{1,0:T(8,128)S(1)}, u32[]{:S(2)}, u32[]{:S(2)}) collective-permute-start(f32[48,576]{1,0:T(8,128)S(1)} %get-tuple-element.36), channel_id=1, source_target_pairs={{0,0},{2,34},{1,9},{3,43},{4,20},{6,54},{5,29},{7,63},{8,8},{10,42... | collective-permute-start | bytes 331784 | tf_op jit(solution)/shard_map/ppermute | solution.py:286
  74.4 10.3 %collective-permute-start.23 = (f32[48,576]{1,0:T(8,128)S(1)}, f32[48,576]{1,0:T(8,128)S(1)}, u32[]{:S(2)}, u32[]{:S(2)}) collective-permute-start(f32[48,576]{1,0:T(8,128)S(1)} %get-tuple-element.37), channel_id=1, source_target_pairs={{0,208},{2,242},{1,217},{3,251},{4,228},{6,198},{5,237},{7,207},{8... | collective-permute-start | bytes 331784 | tf_op jit(solution)/shard_map/ppermute | solution.py:286
  84.8 7.4 %collective-permute-start.24 = (f32[48,1152]{1,0:T(8,128)S(1)}, f32[48,1152]{1,0:T(8,128)S(1)}, u32[]{:S(2)}, u32[]{:S(2)}) collective-permute-start(f32[48,1152]{1,0:T(8,128)S(1)} %shard_map.81.refs_0_), channel_id=1, source_target_pairs={{0,5},{1,0},{4,1},{5,4},{2,7},{3,2},{6,3},{7,6},{8,13},{9,8},{12,9... | collective-permute-start | bytes 663560 | tf_op jit(solution)/shard_map/ppermute | solution.py:18
  84.8 7.7 %collective-permute-start.26 = (f32[48,1152]{1,0:T(8,128)S(1)}, f32[48,1152]{1,0:T(8,128)S(1)}, u32[]{:S(2)}, u32[]{:S(2)}) collective-permute-start(f32[48,1152]{1,0:T(8,128)S(1)} %shard_map.81.refs_0_), channel_id=1, source_target_pairs={{0,1},{1,4},{4,5},{5,0},{2,3},{3,6},{6,7},{7,2},{8,9},{9,12},{12,1... | collective-permute-start | bytes 663560 | tf_op jit(solution)/shard_map/ppermute | solution.py:18
  88.1 10.9 %collective-permute-start.28 = (f32[48,1152]{1,0:T(8,128)S(1)}, f32[48,1152]{1,0:T(8,128)S(1)}, u32[]{:S(2)}, u32[]{:S(2)}) collective-permute-start(f32[48,1152]{1,0:T(8,128)S(1)} %shard_map.81.refs_0_), channel_id=1, source_target_pairs={{0,2},{2,0},{1,3},{3,1},{4,6},{6,4},{5,7},{7,5},{8,10},{10,8},{9,1... | collective-permute-start | bytes 663560 | tf_op jit(solution)/shard_map/ppermute | solution.py:22
  92.2 6.3 %collective-permute-start.25 = (f32[24,1152]{1,0:T(8,128)S(1)}, f32[24,1152]{1,0:T(8,128)S(1)}, u32[]{:S(2)}, u32[]{:S(2)}) collective-permute-start(f32[24,1152]{1,0:T(8,128)S(1)} %slice.8), channel_id=1, source_target_pairs={{0,5},{1,0},{4,1},{5,4},{2,7},{3,2},{6,3},{7,6},{8,13},{9,8},{12,9... | collective-permute-start | bytes 331784 | tf_op jit(solution)/shard_map/ppermute | solution.py:18
  92.5 5.9 %collective-permute-start.27 = (f32[24,1152]{1,0:T(8,128)S(1)}, f32[24,1152]{1,0:T(8,128)S(1)}, u32[]{:S(2)}, u32[]{:S(2)}) collective-permute-start(f32[24,1152]{1,0:T(8,128)S(1)} %slice.9), channel_id=1, source_target_pairs={{0,1},{1,4},{4,5},{5,0},{2,3},{3,6},{6,7},{7,2},{8,9},{9,12},{12,1... | collective-permute-start | bytes 331784 | tf_op jit(solution)/shard_map/ppermute | solution.py:18
  95.8 4.1 %collective-permute-start.29 = (f32[48,1152]{1,0:T(8,128)S(1)}, f32[48,1152]{1,0:T(8,128)S(1)}, u32[]{:S(2)}, u32[]{:S(2)}) collective-permute-start(f32[48,1152]{1,0:T(8,128)S(1)} %collective-permute-done.24.refs_1_), channel_id=1, source_target_pairs={{0,2},{2,0},{1,3},{3,1},{4,6},{6,4},{5,7},{7,5},{8,10},{10,8},{9,1... | collective-permute-start | bytes 663560 | tf_op jit(solution)/shard_map/ppermute | solution.py:22
  95.8 4.1 %collective-permute-start.32 = (f32[48,1152]{1,0:T(8,128)S(1)}, f32[48,1152]{1,0:T(8,128)S(1)}, u32[]{:S(2)}, u32[]{:S(2)}) collective-permute-start(f32[48,1152]{1,0:T(8,128)S(1)} %collective-permute-done.26.refs_4_), channel_id=1, source_target_pairs={{0,2},{2,0},{1,3},{3,1},{4,6},{6,4},{5,7},{7,5},{8,10},{10,8},{9,1... | collective-permute-start | bytes 663560 | tf_op jit(solution)/shard_map/ppermute | solution.py:22
  98.5 1.3 collective-permute-start.30
  98.5 1.5 collective-permute-start.31
  104.7 36.9 %copy-start.2 = (f32[125,500]{0,1:T(8,128)S(1)}, f32[125,500]{0,1:T(8,128)}, u32[]{:S(2)}) copy-start(f32[125,500]{0,1:T(8,128)} %param.8) | copy-start | bytes 750004
  104.8 43.2 %copy-start.4 = (f32[125,96]{0,1:T(8,128)S(1)}, f32[125,96]{0,1:T(8,128)}, u32[]{:S(2)}) copy-start(f32[125,96]{0,1:T(8,128)} %param.9) | copy-start | bytes 144004
  120.8 5.4 %collective-permute-start.33 = (f32[48,128]{1,0:T(8,128)S(1)}, f32[48,128]{1,0:T(8,128)S(1)}, u32[]{:S(2)}, u32[]{:S(2)}) collective-permute-start(f32[48,128]{1,0:T(8,128)S(1)} %reduce_sum.9), channel_id=1, source_target_pairs={{0,128},{64,192},{128,0},{192,64},{1,129},{65,193},{129,1},{193,65... | collective-permute-start | bytes 73736 | tf_op jit(solution)/shard_map/ppermute | solution.py:26
  121.5 4.9 %collective-permute-start.34 = (f32[48,128]{1,0:T(8,128)S(1)}, f32[48,128]{1,0:T(8,128)S(1)}, u32[]{:S(2)}, u32[]{:S(2)}) collective-permute-start(f32[48,128]{1,0:T(8,128)S(1)} %reduce_sum.9), channel_id=1, source_target_pairs={{0,64},{64,0},{128,192},{192,128},{1,65},{65,1},{129,193},{193,129... | collective-permute-start | bytes 73736 | tf_op jit(solution)/shard_map/ppermute | solution.py:26
  124.4 5.0 %collective-permute-start.35 = (f32[48,128]{1,0:T(8,128)S(1)}, f32[48,128]{1,0:T(8,128)S(1)}, u32[]{:S(2)}, u32[]{:S(2)}) collective-permute-start(f32[48,128]{1,0:T(8,128)S(1)} %reduce_sum.9), channel_id=1, source_target_pairs={{0,192},{64,128},{128,64},{192,0},{1,193},{65,129},{129,65},{193,1... | collective-permute-start | bytes 73736 | tf_op jit(solution)/shard_map/ppermute | solution.py:26
  141.9 1.3 collective-permute-start.36
  143.2 5.1 %collective-permute-start.37 = (f32[104,125]{1,0:T(8,128)S(1)}, f32[104,125]{1,0:T(8,128)S(1)}, u32[]{:S(2)}, u32[]{:S(2)}) collective-permute-start(f32[104,125]{1,0:T(8,128)S(1)} %add.15.a_ref), channel_id=1, source_target_pairs={{0,1},{1,0},{4,5},{5,4},{2,3},{3,2},{6,7},{7,6},{8,9},{9,8},{12,13... | collective-permute-start | bytes 156008 | tf_op jit(solution)/shard_map/ppermute | solution.py:26
  143.3 7.4 %collective-permute-start.38 = (f32[104,125]{1,0:T(8,128)S(1)}, f32[104,125]{1,0:T(8,128)S(1)}, u32[]{:S(2)}, u32[]{:S(2)}) collective-permute-start(f32[104,125]{1,0:T(8,128)S(1)} %add.15.a_ref), channel_id=1, source_target_pairs={{0,4},{1,5},{4,0},{5,1},{2,6},{3,7},{6,2},{7,3},{8,12},{9,13},{12,... | collective-permute-start | bytes 156008 | tf_op jit(solution)/shard_map/ppermute | solution.py:26
  147.7 5.3 %collective-permute-start.39 = (f32[104,125]{1,0:T(8,128)S(1)}, f32[104,125]{1,0:T(8,128)S(1)}, u32[]{:S(2)}, u32[]{:S(2)}) collective-permute-start(f32[104,125]{1,0:T(8,128)S(1)} %add.15.a_ref), channel_id=1, source_target_pairs={{0,5},{1,4},{4,1},{5,0},{2,7},{3,6},{6,3},{7,2},{8,13},{9,12},{12,... | collective-permute-start | bytes 156008 | tf_op jit(solution)/shard_map/ppermute | solution.py:26

commit v5 on v4

--- a/solution.py
+++ b/solution.py
@@ -22,6 +22,11 @@
     return lax.ppermute(value, "co", [(0, 1), (1, 0)])
 
 
+def around(value, sign):
+    pairs = [(z * 2 + c, (z - sign * (1 - 2 * c)) % NZ * 2 + c) for z in range(NZ) for c in range(2)]
+    return lax.ppermute(value, ("z", "co"), pairs)
+
+
 def swap(value, axis, size, mask):
     return lax.ppermute(value, axis, [(i, i ^ mask) for i in range(size)])
 
@@ -43,7 +48,7 @@
     return total + lax.dot_general(rest, first, dims, preferred_element_type=jnp.float32)
 
 
-def pair_kernel(n_p, fresh, *refs):
+def pair_kernel(n_p, turn, fresh, *refs):
     p_head, p_rest = refs[-2:]
     p_refs = refs[:n_p]
     if fresh:
@@ -59,7 +64,8 @@
     half, n_cols = kept_ref.shape
     for k, ref in enumerate(p_refs):
         rows = ref.shape[0]
-        start = ((k // NX) ^ core) * half + ((k % NX - x) & (NX - 1)) * rows
+        offset = (k * (1 - 2 * core) - turn) & (NZ - 1)
+        start = ((offset >> 2) ^ core) * half + ((offset - x) & (NX - 1)) * rows
         place = pl.ds(pl.multiple_of(start, 16), rows)
         p_head[place, :], p_rest[place, :] = split(ref[...])
     for low in range(0, n_cols, 256):
@@ -70,14 +76,14 @@
         sent_ref[:, low:high] = total[half:]
 
 
-def pair_product(p_pieces, rows, fresh):
+def pair_product(p_pieces, rows, turn, fresh):
     depth = p_pieces[0].shape[1]
     n_rows = sum(p.shape[0] for p in p_pieces)
     n_cols = sum(r.shape[0] for r in rows) if fresh else rows[0].shape[0]
     shape = jax.ShapeDtypeStruct((n_rows // 2, n_cols), jnp.float32)
     parts = jax.ShapeDtypeStruct((n_cols, depth), jnp.bfloat16)
     return pl.pallas_call(
-        functools.partial(pair_kernel, len(p_pieces), fresh),
+        functools.partial(pair_kernel, len(p_pieces), turn, fresh),
         out_shape=(shape, shape) + ((parts, parts) if fresh else ()),
         scratch_shapes=[pltpu.VMEM((n_rows, depth), jnp.bfloat16)] * 2,
         compiler_params=pltpu.CompilerParams(vmem_limit_bytes=16 * 2**20),
@@ -260,15 +266,15 @@
     for k in range(1, NZ // 2):
         for found in (near, far):
             if found is near or k < 3:
-                found[k] = shift(found[k - 1], "z", NZ, -1)
-                found[NZ - k] = shift(found[(NZ - k + 1) % NZ], "z", NZ, 1)
-    near[4] = shift(near[3], "z", NZ, -1)
+                found[k] = around(found[k - 1], 1)
+                found[NZ - k] = around(found[(NZ - k + 1) % NZ], -1)
+    near[4] = around(near[3], 1)
     for k in (3, 5, 4):
         far[k] = swap(near[k], "y", NY, 3)
 
-    kept, sent, *rows = pair_product([near[k] for k in range(NZ)], rows, True)
+    kept, sent, *rows = pair_product([near[k] for k in range(NZ)], rows, 0, True)
     chunks = [kept, swap_core(sent)]
-    kept, sent = pair_product([far[(k + TURN) % NZ] for k in range(NZ)], rows, False)
+    kept, sent = pair_product([far[k] for k in range(NZ)], rows, TURN, False)
     chunks += [kept, swap_core(sent)]
     first, second = sum_over_x(chunks)
 

time: 154 us -> 156 us (1.013)
  waiting for transfers between devices: 48.9 us -> 54.2 us
  blocking collectives: 28.2 us -> 26 us
  starting transfers between devices: 61.6 us -> 60 us
    ppermute x19 -> x8, starting transfers between devices: 33.7 us -> 11.1 us  [shift(): lax.ppermute(value, axis, [(i, (i + step) % size) for i in range(size)])]
    ppermute x0 -> x11, starting transfers between devices: none -> 19.9 us  [around(): return lax.ppermute(value, ('z', 'co'), pairs)]
    ppermute x0 -> x11, waiting for transfers between devices: none -> 13.7 us  [around(): return lax.ppermute(value, ('z', 'co'), pairs)]
    ppermute x19 -> x8, waiting for transfers between devices: 27.2 us -> 16.3 us  [shift(): lax.ppermute(value, axis, [(i, (i + step) % size) for i in range(size)])]
    ppermute x2, waiting for transfers between devices: 5.98 us -> 9.88 us  [send_home(): return lax.ppermute(value, ('y', 'z', 'xh', 'co', 'xl'), pairs)]
    all_to_all x1, blocking collectives: 16 us -> 13.8 us  [on_device(): lax.all_to_all(tiles, 'z', split_axis=0, concat_axis=0, tiled=True)]
  transfers between devices with their start and end apart: 40 -> 40, of which waited for: 25 -> 24; matrix products, arithmetic and copies ran while one was open for 0% -> 0% of each run, Pallas kernels for 2% -> 2%
where the time goes in v5:
time: 156 us; the launch traced here: 155 us
  starting transfers between devices  60 us (38%)
  waiting for transfers between devices  54.2 us (35%)
  blocking collectives  26 us (17%)
  Pallas kernels  12.1 us (8%)
  local copies, waits for them, and re-layouts  2.31 us (1%)
    ppermute x11, starting transfers between devices, around(): return lax.ppermute(value, ('z', 'co'), pairs)  19.9 us
    ppermute x11, starting transfers between devices, swap(): return lax.ppermute(value, axis, [(i, i ^ mask) for i in range(size)])  18.5 us
    ppermute x8, waiting for transfers between devices, shift(): lax.ppermute(value, axis, [(i, (i + step) % size) for i in range(size)])  16.3 us
    all_to_all x1, blocking collectives, on_device(): lax.all_to_all(tiles, 'z', split_axis=0, concat_axis=0, tiled=True)  13.8 us
    ppermute x11, waiting for transfers between devices, around(): return lax.ppermute(value, ('z', 'co'), pairs)  13.7 us
    all_to_all x1, blocking collectives, on_device(): lax.all_to_all(jnp.broadcast_to(piece[None], tiles.shape), 'z', split_axi...  12.2 us
    ppermute x8, starting transfers between devices, shift(): lax.ppermute(value, axis, [(i, (i + step) % size) for i in range(size)])  11.1 us
    ppermute x11, waiting for transfers between devices, swap(): return lax.ppermute(value, axis, [(i, i ^ mask) for i in range(size)])  10.1 us
  transfers between devices with their start and end apart: 40, of which 24 were waited for; matrix products, arithmetic and copies ran while one was open for 0% of the time, Pallas kernels for 2%

profile of v5, /device:TPU:6, one launch (start us, length us, event | category | flops | bytes accessed | tf_op | source)
XLA Modules:
  0.0 155.5 jit_solution(70473959986876316)
XLA Ops:
  0.6 1.7 %collective-permute-start.7 = (f32[288,1152]{1,0:T(8,128)}, f32[288,1152]{1,0:T(8,128)S(1)}, u32[]{:S(2)}, u32[]{:S(2)}) collective-permute-start(f32[288,1152]{1,0:T(8,128)} %refs_8_.1), channel_id=1, source_target_pairs={{0,64},{64,0},{128,192},{192,128},{1,65},{65,1},{129,193},{193,129... | collective-permute-start | bytes 3981320 | tf_op jit(solution)/shard_map/ppermute | solution.py:31
  2.3 5.9 %collective-permute-start = (f32[48,1152]{1,0:T(8,128)}, f32[48,1152]{1,0:T(8,128)S(1)}, u32[]{:S(2)}, u32[]{:S(2)}) collective-permute-start(f32[48,1152]{1,0:T(8,128)} %refs_0_.1), channel_id=1, source_target_pairs={{0,56},{2,10},{8,0},{10,18},{16,8},{18,26},{24,16},{26,34},{32,24}... | collective-permute-start | bytes 663560 | tf_op jit(solution)/shard_map/ppermute | solution.py:27
  8.2 4.7 %collective-permute-done.refs_1_ = f32[48,1152]{1,0:T(8,128)S(1)} collective-permute-done((f32[48,1152]{1,0:T(8,128)}, f32[48,1152]{1,0:T(8,128)S(1)}, u32[]{:S(2)}, u32[]{:S(2)}) %collective-permute-start) | collective-permute-done | bytes 221216 | tf_op jit(solution)/shard_map/ppermute | solution.py:27
  12.9 3.6 %collective-permute-start.1 = (f32[48,1152]{1,0:T(8,128)S(1)}, f32[48,1152]{1,0:T(8,128)S(1)}, u32[]{:S(2)}, u32[]{:S(2)}) collective-permute-start(f32[48,1152]{1,0:T(8,128)S(1)} %collective-permute-done.refs_1_), channel_id=1, source_target_pairs={{0,56},{2,10},{8,0},{10,18},{16,8},{18,26},{24,16},{26,34},{32,24}... | collective-permute-start | bytes 663560 | tf_op jit(solution)/shard_map/ppermute | solution.py:27
  16.5 2.2 %collective-permute-start.9 = (f32[48,1152]{1,0:T(8,128)}, f32[48,1152]{1,0:T(8,128)S(1)}, u32[]{:S(2)}, u32[]{:S(2)}) collective-permute-start(f32[48,1152]{1,0:T(8,128)} %refs_0_.1), channel_id=1, source_target_pairs={{0,192},{64,128},{128,64},{192,0},{1,193},{65,129},{129,65},{193,1... | collective-permute-start | bytes 663560 | tf_op jit(solution)/shard_map/ppermute | solution.py:31
  18.6 2.0 %collective-permute-done.1.refs_2_ = f32[48,1152]{1,0:T(8,128)S(1)} collective-permute-done((f32[48,1152]{1,0:T(8,128)S(1)}, f32[48,1152]{1,0:T(8,128)S(1)}, u32[]{:S(2)}, u32[]{:S(2)}) %collective-permute-start.1) | collective-permute-done | bytes 221216 | tf_op jit(solution)/shard_map/ppermute | solution.py:27
  20.7 3.7 %collective-permute-start.2 = (f32[48,1152]{1,0:T(8,128)S(1)}, f32[48,1152]{1,0:T(8,128)S(1)}, u32[]{:S(2)}, u32[]{:S(2)}) collective-permute-start(f32[48,1152]{1,0:T(8,128)S(1)} %collective-permute-done.1.refs_2_), channel_id=1, source_target_pairs={{0,56},{2,10},{8,0},{10,18},{16,8},{18,26},{24,16},{26,34},{32,24}... | collective-permute-start | bytes 663560 | tf_op jit(solution)/shard_map/ppermute | solution.py:27
  24.4 2.0 %collective-permute-start.15 = (f32[48,1152]{1,0:T(8,128)S(1)}, f32[48,1152]{1,0:T(8,128)S(1)}, u32[]{:S(2)}, u32[]{:S(2)}) collective-permute-start(f32[48,1152]{1,0:T(8,128)S(1)} %collective-permute-done.9.refs_0_), channel_id=1, source_target_pairs={{0,8},{2,58},{8,16},{10,2},{16,24},{18,10},{24,32},{26,18},{32,40}... | collective-permute-start | bytes 663560 | tf_op jit(solution)/shard_map/ppermute | solution.py:27
  26.4 1.8 %collective-permute-done.5.refs_6_ = f32[48,1152]{1,0:T(8,128)S(1)} collective-permute-done((f32[48,1152]{1,0:T(8,128)S(1)}, f32[48,1152]{1,0:T(8,128)S(1)}, u32[]{:S(2)}, u32[]{:S(2)}) %collective-permute-start.5) | collective-permute-done | bytes 221216 | tf_op jit(solution)/shard_map/ppermute | solution.py:27
  28.2 0.8 collective-permute-done.2.refs_3_
  29.0 2.6 %collective-permute-start.3 = (f32[48,1152]{1,0:T(8,128)S(1)}, f32[48,1152]{1,0:T(8,128)S(1)}, u32[]{:S(2)}, u32[]{:S(2)}) collective-permute-start(f32[48,1152]{1,0:T(8,128)S(1)} %collective-permute-done.2.refs_3_), channel_id=1, source_target_pairs={{0,56},{2,10},{8,0},{10,18},{16,8},{18,26},{24,16},{26,34},{32,24}... | collective-permute-start | bytes 663560 | tf_op jit(solution)/shard_map/ppermute | solution.py:27
  31.8 2.2 %collective-permute-start.11 = (f32[48,1152]{1,0:T(8,128)S(1)}, f32[48,1152]{1,0:T(8,128)S(1)}, u32[]{:S(2)}, u32[]{:S(2)}) collective-permute-start(f32[48,1152]{1,0:T(8,128)S(1)} %collective-permute-done.10.refs_1_), channel_id=1, source_target_pairs={{0,56},{2,10},{8,0},{10,18},{16,8},{18,26},{24,16},{26,34},{32,24}... | collective-permute-start | bytes 663560 | tf_op jit(solution)/shard_map/ppermute | solution.py:27
  34.0 4.1 %collective-permute-done.6.refs_5_ = f32[48,1152]{1,0:T(8,128)S(1)} collective-permute-done((f32[48,1152]{1,0:T(8,128)S(1)}, f32[48,1152]{1,0:T(8,128)S(1)}, u32[]{:S(2)}, u32[]{:S(2)}) %collective-permute-start.6) | collective-permute-done | bytes 221216 | tf_op jit(solution)/shard_map/ppermute | solution.py:27
  38.1 2.4 %collective-permute-start.12 = (f32[48,1152]{1,0:T(8,128)S(1)}, f32[48,1152]{1,0:T(8,128)S(1)}, u32[]{:S(2)}, u32[]{:S(2)}) collective-permute-start(f32[48,1152]{1,0:T(8,128)S(1)} %collective-permute-done.2.refs_3_), channel_id=1, source_target_pairs={{0,192},{64,128},{128,64},{192,0},{1,193},{65,129},{129,65},{193,1... | collective-permute-start | bytes 663560 | tf_op jit(solution)/shard_map/ppermute | solution.py:31
  40.5 0.8 collective-permute-start.14
  41.3 2.4 %collective-permute-start.13 = (f32[48,1152]{1,0:T(8,128)S(1)}, f32[48,1152]{1,0:T(8,128)S(1)}, u32[]{:S(2)}, u32[]{:S(2)}) collective-permute-start(f32[48,1152]{1,0:T(8,128)S(1)} %collective-permute-done.3.refs_4_), channel_id=1, source_target_pairs={{0,192},{64,128},{128,64},{192,0},{1,193},{65,129},{129,65},{193,1... | collective-permute-start | bytes 663560 | tf_op jit(solution)/shard_map/ppermute | solution.py:31
  43.8 1.3 copy-done.1
  45.1 0.9 copy-done.3
  46.0 2.7 %shard_map.76 = (f32[192,576]{1,0:T(8,128)S(1)}, f32[192,576]{1,0:T(8,128)S(1)}, bf16[576,1152]{1,0:T(8,128)(2,1)S(1)}, bf16[576,1152]{1,0:T(8,128)(2,1)S(1)}) custom-call(f32[48,1152]{1,0:T(8,128)S(1)} %copy-done.3, f32[48,1152]{1,0:T(8,128)S(1)} %collective-permute-done.refs_1_, f32[48,1152]{1,0:T(8,128)S(1)} %collective-permute-done.1.refs_2_, ...), custom_call_target="tpu_custom_call" | custom-call | flops 1000 | bytes 1000 | tf_op jit(solution)/shard_map/pallas_call | solution.py:85
  48.8 1.2 collective-permute-done.13.refs_4_
  50.0 2.7 %shard_map.77 = (f32[192,576]{1,0:T(8,128)S(1)}, f32[192,576]{1,0:T(8,128)S(1)}) custom-call(f32[48,1152]{1,0:T(8,128)S(1)} %collective-permute-done.9.refs_0_, f32[48,1152]{1,0:T(8,128)S(1)} %collective-permute-done.10.refs_1_, f32[48,1152]{1,0:T(8,128)S(1)} %collective-permute-done.11.refs_2_, f32[48,1152]{1,0:T(8,128)S(1)} %collective-permute-done.12.refs_3_, ...), custom_call_target="tpu_custom_call" | custom-call | flops 1528823808 | bytes 4423680 | tf_op jit(solution)/shard_map/pallas_call | solution.py:85
  53.3 1.4 collective-permute-done.17.refs_3_
  56.1 1.5 collective-permute-start.19
  57.7 3.1 %collective-permute-done.18.up_ref = f32[24,1152]{1,0:T(8,128)S(1)} collective-permute-done((f32[24,1152]{1,0:T(8,128)S(1)}, f32[24,1152]{1,0:T(8,128)S(1)}, u32[]{:S(2)}, u32[]{:S(2)}) %collective-permute-start.18) | collective-permute-done | bytes 110624 | tf_op jit(solution)/shard_map/ppermute | solution.py:18
  60.8 1.4 collective-permute-done.19.down_ref
  62.6 1.7 %collective-permute-start.21 = (f32[48,1152]{1,0:T(8,128)S(1)}, f32[48,1152]{1,0:T(8,128)S(1)}, u32[]{:S(2)}, u32[]{:S(2)}) collective-permute-start(f32[48,1152]{1,0:T(8,128)S(1)} %get-tuple-element.35), channel_id=1, source_target_pairs={{0,5},{1,0},{4,1},{5,4},{2,7},{3,2},{6,3},{7,6},{8,13},{9,8},{12,9... | collective-permute-start | bytes 663560 | tf_op jit(solution)/shard_map/ppermute | solution.py:18
  64.3 4.3 %collective-permute-done.20.one_ref = f32[48,1152]{1,0:T(8,128)S(1)} collective-permute-done((f32[48,1152]{1,0:T(8,128)S(1)}, f32[48,1152]{1,0:T(8,128)S(1)}, u32[]{:S(2)}, u32[]{:S(2)}) %collective-permute-start.20) | collective-permute-done | bytes 221216 | tf_op jit(solution)/shard_map/ppermute | solution.py:18
  68.6 1.5 collective-permute-done.21.two_ref
  70.3 7.9 %collective-permute-start.22 = (f32[48,576]{1,0:T(8,128)S(1)}, f32[48,576]{1,0:T(8,128)S(1)}, u32[]{:S(2)}, u32[]{:S(2)}) collective-permute-start(f32[48,576]{1,0:T(8,128)S(1)} %get-tuple-element.36), channel_id=1, source_target_pairs={{0,0},{2,34},{1,9},{3,43},{4,20},{6,54},{5,29},{7,63},{8,8},{10,42... | collective-permute-start | bytes 331784 | tf_op jit(solution)/shard_map/ppermute | solution.py:292
  78.1 1.0 collective-permute-start.23
  79.1 3.3 %collective-permute-done.22.first_ref = f32[48,576]{1,0:T(8,128)S(1)} collective-permute-done((f32[48,576]{1,0:T(8,128)S(1)}, f32[48,576]{1,0:T(8,128)S(1)}, u32[]{:S(2)}, u32[]{:S(2)}) %collective-permute-start.22) | collective-permute-done | bytes 110624 | tf_op jit(solution)/shard_map/ppermute | solution.py:292
  82.4 6.6 %collective-permute-done.23.second_ref = f32[48,576]{1,0:T(8,128)S(1)} collective-permute-done((f32[48,576]{1,0:T(8,128)S(1)}, f32[48,576]{1,0:T(8,128)S(1)}, u32[]{:S(2)}, u32[]{:S(2)}) %collective-permute-start.23) | collective-permute-done | bytes 110624 | tf_op jit(solution)/shard_map/ppermute | solution.py:292
  89.2 3.2 %collective-permute-start.26 = (f32[48,1152]{1,0:T(8,128)S(1)}, f32[48,1152]{1,0:T(8,128)S(1)}, u32[]{:S(2)}, u32[]{:S(2)}) collective-permute-start(f32[48,1152]{1,0:T(8,128)S(1)} %shard_map.81.refs_0_), channel_id=1, source_target_pairs={{0,1},{1,4},{4,5},{5,0},{2,3},{3,6},{6,7},{7,2},{8,9},{9,12},{12,1... | collective-permute-start | bytes 663560 | tf_op jit(solution)/shard_map/ppermute | solution.py:18
  92.4 3.9 %collective-permute-done.24.refs_1_ = f32[48,1152]{1,0:T(8,128)S(1)} collective-permute-done((f32[48,1152]{1,0:T(8,128)S(1)}, f32[48,1152]{1,0:T(8,128)S(1)}, u32[]{:S(2)}, u32[]{:S(2)}) %collective-permute-start.24) | collective-permute-done | bytes 221216 | tf_op jit(solution)/shard_map/ppermute | solution.py:18
  96.6 3.3 %collective-permute-start.27 = (f32[24,1152]{1,0:T(8,128)S(1)}, f32[24,1152]{1,0:T(8,128)S(1)}, u32[]{:S(2)}, u32[]{:S(2)}) collective-permute-start(f32[24,1152]{1,0:T(8,128)S(1)} %slice.9), channel_id=1, source_target_pairs={{0,1},{1,4},{4,5},{5,0},{2,3},{3,6},{6,7},{7,2},{8,9},{9,12},{12,1... | collective-permute-start | bytes 331784 | tf_op jit(solution)/shard_map/ppermute | solution.py:18
  100.4 2.1 %collective-permute-done.25.refs_2_ = f32[24,1152]{1,0:T(8,128)S(1)} collective-permute-done((f32[24,1152]{1,0:T(8,128)S(1)}, f32[24,1152]{1,0:T(8,128)S(1)}, u32[]{:S(2)}, u32[]{:S(2)}) %collective-permute-start.25) | collective-permute-done | bytes 110624 | tf_op jit(solution)/shard_map/ppermute | solution.py:18
  104.1 4.8 %shard_map.82 = f32[8,48,128]{2,1,0:T(8,128)S(1)} custom-call(f32[48,1152]{1,0:T(8,128)S(1)} %shard_map.81.refs_0_, f32[48,1152]{1,0:T(8,128)S(1)} %collective-permute-done.24.refs_1_, f32[24,1152]{1,0:T(8,128)S(1)} %collective-permute-done.25.refs_2_, f32[24,1152]{1,0:T(8,128)S(1)} %collective-permute-done.27.refs_3_, ...), custom_call_target="tpu_custom_call" | custom-call | tf_op jit(solution)/shard_map/pallas_call | solution.py:202
  108.9 13.8 %all_to_all.10 = f32[8,48,128]{2,1,0:T(8,128)S(1)} all-to-all(f32[8,48,128]{2,1,0:T(8,128)S(1)} %shard_map.82), channel_id=1, replica_groups=mesh['y'=4,'z'=8,'xh'=2,'co'=2,'xl'=2] {'z'}, dimensions={0} | all-to-all | bytes 393216 | tf_op jit(solution)/shard_map/all_to_all | solution.py:309
  122.8 3.1 %collective-permute-start.34 = (f32[48,128]{1,0:T(8,128)S(1)}, f32[48,128]{1,0:T(8,128)S(1)}, u32[]{:S(2)}, u32[]{:S(2)}) collective-permute-start(f32[48,128]{1,0:T(8,128)S(1)} %reduce_sum.9), channel_id=1, source_target_pairs={{0,64},{64,0},{128,192},{192,128},{1,65},{65,1},{129,193},{193,129... | collective-permute-start | bytes 73736 | tf_op jit(solution)/shard_map/ppermute | solution.py:31
  125.9 0.9 collective-permute-start.35
  126.9 1.2 collective-permute-done.33
  128.1 2.8 %collective-permute-done.35 = f32[48,128]{1,0:T(8,128)S(1)} collective-permute-done((f32[48,128]{1,0:T(8,128)S(1)}, f32[48,128]{1,0:T(8,128)S(1)}, u32[]{:S(2)}, u32[]{:S(2)}) %collective-permute-start.35) | collective-permute-done | bytes 24608 | tf_op jit(solution)/shard_map/ppermute | solution.py:31
  131.0 12.2 %all_to_all.11.tiles_ref = f32[8,48,128]{2,1,0:T(8,128)S(1)} all-to-all(f32[8,48,128]{2,1,0:T(8,128)S(1)} %broadcast_in_dim.2), channel_id=1, replica_groups=mesh['y'=4,'z'=8,'xh'=2,'co'=2,'xl'=2] {'z'}, dimensions={0} | all-to-all | bytes 393216 | tf_op jit(solution)/shard_map/all_to_all | solution.py:311
  143.5 1.2 collective-permute-done.36
  144.9 4.4 %collective-permute-start.38 = (f32[104,125]{1,0:T(8,128)S(1)}, f32[104,125]{1,0:T(8,128)S(1)}, u32[]{:S(2)}, u32[]{:S(2)}) collective-permute-start(f32[104,125]{1,0:T(8,128)S(1)} %add.15.a_ref), channel_id=1, source_target_pairs={{0,4},{1,5},{4,0},{5,1},{2,6},{3,7},{6,2},{7,3},{8,12},{9,13},{12,... | collective-permute-start | bytes 156008 | tf_op jit(solution)/shard_map/ppermute | solution.py:31
  149.9 2.4 %collective-permute-done.38.c_ref = f32[104,125]{1,0:T(8,128)S(1)} collective-permute-done((f32[104,125]{1,0:T(8,128)S(1)}, f32[104,125]{1,0:T(8,128)S(1)}, u32[]{:S(2)}, u32[]{:S(2)}) %collective-permute-start.38) | collective-permute-done | bytes 52032 | tf_op jit(solution)/shard_map/ppermute | solution.py:31
  152.2 2.4 %collective-permute-done.39.d_ref = f32[104,125]{1,0:T(8,128)S(1)} collective-permute-done((f32[104,125]{1,0:T(8,128)S(1)}, f32[104,125]{1,0:T(8,128)S(1)}, u32[]{:S(2)}, u32[]{:S(2)}) %collective-permute-start.39) | collective-permute-done | bytes 52032 | tf_op jit(solution)/shard_map/ppermute | solution.py:31
  154.6 0.8 shard_map.85
  (60 shorter events, 6.5 us)
Async XLA Ops:
  0.6 40.7 %collective-permute-start.7 = (f32[288,1152]{1,0:T(8,128)}, f32[288,1152]{1,0:T(8,128)S(1)}, u32[]{:S(2)}, u32[]{:S(2)}) collective-permute-start(f32[288,1152]{1,0:T(8,128)} %refs_8_.1), channel_id=1, source_target_pairs={{0,64},{64,0},{128,192},{192,128},{1,65},{65,1},{129,193},{193,129... | collective-permute-start | bytes 3981320 | tf_op jit(solution)/shard_map/ppermute | solution.py:31
  2.3 10.6 %collective-permute-start = (f32[48,1152]{1,0:T(8,128)}, f32[48,1152]{1,0:T(8,128)S(1)}, u32[]{:S(2)}, u32[]{:S(2)}) collective-permute-start(f32[48,1152]{1,0:T(8,128)} %refs_0_.1), channel_id=1, source_target_pairs={{0,56},{2,10},{8,0},{10,18},{16,8},{18,26},{24,16},{26,34},{32,24}... | collective-permute-start | bytes 663560 | tf_op jit(solution)/shard_map/ppermute | solution.py:27
  8.1 10.5 %collective-permute-start.4 = (f32[48,1152]{1,0:T(8,128)}, f32[48,1152]{1,0:T(8,128)S(1)}, u32[]{:S(2)}, u32[]{:S(2)}) collective-permute-start(f32[48,1152]{1,0:T(8,128)} %refs_0_.1), channel_id=1, source_target_pairs={{0,8},{2,58},{8,16},{10,2},{16,24},{18,10},{24,32},{26,18},{32,40}... | collective-permute-start | bytes 663560 | tf_op jit(solution)/shard_map/ppermute | solution.py:27
  12.9 7.8 %collective-permute-start.1 = (f32[48,1152]{1,0:T(8,128)S(1)}, f32[48,1152]{1,0:T(8,128)S(1)}, u32[]{:S(2)}, u32[]{:S(2)}) collective-permute-start(f32[48,1152]{1,0:T(8,128)S(1)} %collective-permute-done.refs_1_), channel_id=1, source_target_pairs={{0,56},{2,10},{8,0},{10,18},{16,8},{18,26},{24,16},{26,34},{32,24}... | collective-permute-start | bytes 663560 | tf_op jit(solution)/shard_map/ppermute | solution.py:27
  16.5 7.9 %collective-permute-start.9 = (f32[48,1152]{1,0:T(8,128)}, f32[48,1152]{1,0:T(8,128)S(1)}, u32[]{:S(2)}, u32[]{:S(2)}) collective-permute-start(f32[48,1152]{1,0:T(8,128)} %refs_0_.1), channel_id=1, source_target_pairs={{0,192},{64,128},{128,64},{192,0},{1,193},{65,129},{129,65},{193,1... | collective-permute-start | bytes 663560 | tf_op jit(solution)/shard_map/ppermute | solution.py:31
  18.6 9.6 %collective-permute-start.5 = (f32[48,1152]{1,0:T(8,128)S(1)}, f32[48,1152]{1,0:T(8,128)S(1)}, u32[]{:S(2)}, u32[]{:S(2)}) collective-permute-start(f32[48,1152]{1,0:T(8,128)S(1)} %collective-permute-done.4.refs_7_), channel_id=1, source_target_pairs={{0,8},{2,58},{8,16},{10,2},{16,24},{18,10},{24,32},{26,18},{32,40}... | collective-permute-start | bytes 663560 | tf_op jit(solution)/shard_map/ppermute | solution.py:27
  20.7 8.4 %collective-permute-start.2 = (f32[48,1152]{1,0:T(8,128)S(1)}, f32[48,1152]{1,0:T(8,128)S(1)}, u32[]{:S(2)}, u32[]{:S(2)}) collective-permute-start(f32[48,1152]{1,0:T(8,128)S(1)} %collective-permute-done.1.refs_2_), channel_id=1, source_target_pairs={{0,56},{2,10},{8,0},{10,18},{16,8},{18,26},{24,16},{26,34},{32,24}... | collective-permute-start | bytes 663560 | tf_op jit(solution)/shard_map/ppermute | solution.py:27
  24.4 7.4 %collective-permute-start.10 = (f32[48,1152]{1,0:T(8,128)S(1)}, f32[48,1152]{1,0:T(8,128)S(1)}, u32[]{:S(2)}, u32[]{:S(2)}) collective-permute-start(f32[48,1152]{1,0:T(8,128)S(1)} %collective-permute-done.9.refs_0_), channel_id=1, source_target_pairs={{0,56},{2,10},{8,0},{10,18},{16,8},{18,26},{24,16},{26,34},{32,24}... | collective-permute-start | bytes 663560 | tf_op jit(solution)/shard_map/ppermute | solution.py:27
  24.4 9.6 %collective-permute-start.15 = (f32[48,1152]{1,0:T(8,128)S(1)}, f32[48,1152]{1,0:T(8,128)S(1)}, u32[]{:S(2)}, u32[]{:S(2)}) collective-permute-start(f32[48,1152]{1,0:T(8,128)S(1)} %collective-permute-done.9.refs_0_), channel_id=1, source_target_pairs={{0,8},{2,58},{8,16},{10,2},{16,24},{18,10},{24,32},{26,18},{32,40}... | collective-permute-start | bytes 663560 | tf_op jit(solution)/shard_map/ppermute | solution.py:27
  28.2 9.9 %collective-permute-start.6 = (f32[48,1152]{1,0:T(8,128)S(1)}, f32[48,1152]{1,0:T(8,128)S(1)}, u32[]{:S(2)}, u32[]{:S(2)}) collective-permute-start(f32[48,1152]{1,0:T(8,128)S(1)} %collective-permute-done.5.refs_6_), channel_id=1, source_target_pairs={{0,8},{2,58},{8,16},{10,2},{16,24},{18,10},{24,32},{26,18},{32,40}... | collective-permute-start | bytes 663560 | tf_op jit(solution)/shard_map/ppermute | solution.py:27
  29.0 11.5 %collective-permute-start.3 = (f32[48,1152]{1,0:T(8,128)S(1)}, f32[48,1152]{1,0:T(8,128)S(1)}, u32[]{:S(2)}, u32[]{:S(2)}) collective-permute-start(f32[48,1152]{1,0:T(8,128)S(1)} %collective-permute-done.2.refs_3_), channel_id=1, source_target_pairs={{0,56},{2,10},{8,0},{10,18},{16,8},{18,26},{24,16},{26,34},{32,24}... | collective-permute-start | bytes 663560 | tf_op jit(solution)/shard_map/ppermute | solution.py:27
  31.8 17.0 %collective-permute-start.11 = (f32[48,1152]{1,0:T(8,128)S(1)}, f32[48,1152]{1,0:T(8,128)S(1)}, u32[]{:S(2)}, u32[]{:S(2)}) collective-permute-start(f32[48,1152]{1,0:T(8,128)S(1)} %collective-permute-done.10.refs_1_), channel_id=1, source_target_pairs={{0,56},{2,10},{8,0},{10,18},{16,8},{18,26},{24,16},{26,34},{32,24}... | collective-permute-start | bytes 663560 | tf_op jit(solution)/shard_map/ppermute | solution.py:27
  34.0 14.8 %collective-permute-start.16 = (f32[48,1152]{1,0:T(8,128)S(1)}, f32[48,1152]{1,0:T(8,128)S(1)}, u32[]{:S(2)}, u32[]{:S(2)}) collective-permute-start(f32[48,1152]{1,0:T(8,128)S(1)} %collective-permute-done.15.refs_7_), channel_id=1, source_target_pairs={{0,8},{2,58},{8,16},{10,2},{16,24},{18,10},{24,32},{26,18},{32,40}... | collective-permute-start | bytes 663560 | tf_op jit(solution)/shard_map/ppermute | solution.py:27
  38.1 10.7 %collective-permute-start.12 = (f32[48,1152]{1,0:T(8,128)S(1)}, f32[48,1152]{1,0:T(8,128)S(1)}, u32[]{:S(2)}, u32[]{:S(2)}) collective-permute-start(f32[48,1152]{1,0:T(8,128)S(1)} %collective-permute-done.2.refs_3_), channel_id=1, source_target_pairs={{0,192},{64,128},{128,64},{192,0},{1,193},{65,129},{129,65},{193,1... | collective-permute-start | bytes 663560 | tf_op jit(solution)/shard_map/ppermute | solution.py:31
  40.5 8.3 %collective-permute-start.14 = (f32[48,1152]{1,0:T(8,128)S(1)}, f32[48,1152]{1,0:T(8,128)S(1)}, u32[]{:S(2)}, u32[]{:S(2)}) collective-permute-start(f32[48,1152]{1,0:T(8,128)S(1)} %collective-permute-done.6.refs_5_), channel_id=1, source_target_pairs={{0,192},{64,128},{128,64},{192,0},{1,193},{65,129},{129,65},{193,1... | collective-permute-start | bytes 663560 | tf_op jit(solution)/shard_map/ppermute | solution.py:31
  41.3 8.7 %collective-permute-start.13 = (f32[48,1152]{1,0:T(8,128)S(1)}, f32[48,1152]{1,0:T(8,128)S(1)}, u32[]{:S(2)}, u32[]{:S(2)}) collective-permute-start(f32[48,1152]{1,0:T(8,128)S(1)} %collective-permute-done.3.refs_4_), channel_id=1, source_target_pairs={{0,192},{64,128},{128,64},{192,0},{1,193},{65,129},{129,65},{193,1... | collective-permute-start | bytes 663560 | tf_op jit(solution)/shard_map/ppermute | solution.py:31
  43.8 1.3 copy-start.1
  45.1 0.9 copy-start.3
  50.0 54.0 %copy-start = (f32[48,96,500]{2,1,0:T(8,128)S(1)}, f32[48,96,500]{2,1,0:T(8,128)}, u32[]{:S(2)}) copy-start(f32[48,96,500]{2,1,0:T(8,128)} %refs_10_.1) | copy-start | bytes 27648004
  52.7 2.0 %collective-permute-start.17 = (f32[192,576]{1,0:T(8,128)S(1)}, f32[192,576]{1,0:T(8,128)S(1)}, u32[]{:S(2)}, u32[]{:S(2)}) collective-permute-start(f32[192,576]{1,0:T(8,128)S(1)} %get-tuple-element.28), channel_id=1, source_target_pairs={{0,2},{2,0},{1,3},{3,1},{4,6},{6,4},{5,7},{7,5},{8,10},{10,8},{9,1... | collective-permute-start | bytes 1327112 | tf_op jit(solution)/shard_map/ppermute | solution.py:22
  52.8 2.6 %collective-permute-start.8 = (f32[192,576]{1,0:T(8,128)S(1)}, f32[192,576]{1,0:T(8,128)S(1)}, u32[]{:S(2)}, u32[]{:S(2)}) collective-permute-start(f32[192,576]{1,0:T(8,128)S(1)} %get-tuple-element.24), channel_id=1, source_target_pairs={{0,2},{2,0},{1,3},{3,1},{4,6},{6,4},{5,7},{7,5},{8,10},{10,8},{9,1... | collective-permute-start | bytes 1327112 | tf_op jit(solution)/shard_map/ppermute | solution.py:22
  55.6 5.2 %collective-permute-start.18 = (f32[24,1152]{1,0:T(8,128)S(1)}, f32[24,1152]{1,0:T(8,128)S(1)}, u32[]{:S(2)}, u32[]{:S(2)}) collective-permute-start(f32[24,1152]{1,0:T(8,128)S(1)} %get-tuple-element.31), channel_id=1, source_target_pairs={{0,1},{1,4},{4,5},{5,0},{2,3},{3,6},{6,7},{7,2},{8,9},{9,12},{12,1... | collective-permute-start | bytes 331784 | tf_op jit(solution)/shard_map/ppermute | solution.py:18
  56.1 6.0 %collective-permute-start.19 = (f32[24,1152]{1,0:T(8,128)S(1)}, f32[24,1152]{1,0:T(8,128)S(1)}, u32[]{:S(2)}, u32[]{:S(2)}) collective-permute-start(f32[24,1152]{1,0:T(8,128)S(1)} %get-tuple-element.33), channel_id=1, source_target_pairs={{0,5},{1,0},{4,1},{5,4},{2,7},{3,2},{6,3},{7,6},{8,13},{9,8},{12,9... | collective-permute-start | bytes 331784 | tf_op jit(solution)/shard_map/ppermute | solution.py:18
  62.2 6.4 %collective-permute-start.20 = (f32[48,1152]{1,0:T(8,128)S(1)}, f32[48,1152]{1,0:T(8,128)S(1)}, u32[]{:S(2)}, u32[]{:S(2)}) collective-permute-start(f32[48,1152]{1,0:T(8,128)S(1)} %get-tuple-element.34), channel_id=1, source_target_pairs={{0,1},{1,4},{4,5},{5,0},{2,3},{3,6},{6,7},{7,2},{8,9},{9,12},{12,1... | collective-permute-start | bytes 663560 | tf_op jit(solution)/shard_map/ppermute | solution.py:18
  62.6 7.6 %collective-permute-start.21 = (f32[48,1152]{1,0:T(8,128)S(1)}, f32[48,1152]{1,0:T(8,128)S(1)}, u32[]{:S(2)}, u32[]{:S(2)}) collective-permute-start(f32[48,1152]{1,0:T(8,128)S(1)} %get-tuple-element.35), channel_id=1, source_target_pairs={{0,5},{1,0},{4,1},{5,4},{2,7},{3,2},{6,3},{7,6},{8,13},{9,8},{12,9... | collective-permute-start | bytes 663560 | tf_op jit(solution)/shard_map/ppermute | solution.py:18
  70.3 12.1 %collective-permute-start.22 = (f32[48,576]{1,0:T(8,128)S(1)}, f32[48,576]{1,0:T(8,128)S(1)}, u32[]{:S(2)}, u32[]{:S(2)}) collective-permute-start(f32[48,576]{1,0:T(8,128)S(1)} %get-tuple-element.36), channel_id=1, source_target_pairs={{0,0},{2,34},{1,9},{3,43},{4,20},{6,54},{5,29},{7,63},{8,8},{10,42... | collective-permute-start | bytes 331784 | tf_op jit(solution)/shard_map/ppermute | solution.py:292
  78.1 10.8 %collective-permute-start.23 = (f32[48,576]{1,0:T(8,128)S(1)}, f32[48,576]{1,0:T(8,128)S(1)}, u32[]{:S(2)}, u32[]{:S(2)}) collective-permute-start(f32[48,576]{1,0:T(8,128)S(1)} %get-tuple-element.37), channel_id=1, source_target_pairs={{0,208},{2,242},{1,217},{3,251},{4,228},{6,198},{5,237},{7,207},{8... | collective-permute-start | bytes 331784 | tf_op jit(solution)/shard_map/ppermute | solution.py:292
  89.1 7.2 %collective-permute-start.24 = (f32[48,1152]{1,0:T(8,128)S(1)}, f32[48,1152]{1,0:T(8,128)S(1)}, u32[]{:S(2)}, u32[]{:S(2)}) collective-permute-start(f32[48,1152]{1,0:T(8,128)S(1)} %shard_map.81.refs_0_), channel_id=1, source_target_pairs={{0,5},{1,0},{4,1},{5,4},{2,7},{3,2},{6,3},{7,6},{8,13},{9,8},{12,9... | collective-permute-start | bytes 663560 | tf_op jit(solution)/shard_map/ppermute | solution.py:18
  89.2 7.5 %collective-permute-start.26 = (f32[48,1152]{1,0:T(8,128)S(1)}, f32[48,1152]{1,0:T(8,128)S(1)}, u32[]{:S(2)}, u32[]{:S(2)}) collective-permute-start(f32[48,1152]{1,0:T(8,128)S(1)} %shard_map.81.refs_0_), channel_id=1, source_target_pairs={{0,1},{1,4},{4,5},{5,0},{2,3},{3,6},{6,7},{7,2},{8,9},{9,12},{12,1... | collective-permute-start | bytes 663560 | tf_op jit(solution)/shard_map/ppermute | solution.py:18
  92.4 10.7 %collective-permute-start.28 = (f32[48,1152]{1,0:T(8,128)S(1)}, f32[48,1152]{1,0:T(8,128)S(1)}, u32[]{:S(2)}, u32[]{:S(2)}) collective-permute-start(f32[48,1152]{1,0:T(8,128)S(1)} %shard_map.81.refs_0_), channel_id=1, source_target_pairs={{0,2},{2,0},{1,3},{3,1},{4,6},{6,4},{5,7},{7,5},{8,10},{10,8},{9,1... | collective-permute-start | bytes 663560 | tf_op jit(solution)/shard_map/ppermute | solution.py:22
  96.3 6.3 %collective-permute-start.25 = (f32[24,1152]{1,0:T(8,128)S(1)}, f32[24,1152]{1,0:T(8,128)S(1)}, u32[]{:S(2)}, u32[]{:S(2)}) collective-permute-start(f32[24,1152]{1,0:T(8,128)S(1)} %slice.8), channel_id=1, source_target_pairs={{0,5},{1,0},{4,1},{5,4},{2,7},{3,2},{6,3},{7,6},{8,13},{9,8},{12,9... | collective-permute-start | bytes 331784 | tf_op jit(solution)/shard_map/ppermute | solution.py:18
  96.6 5.9 %collective-permute-start.27 = (f32[24,1152]{1,0:T(8,128)S(1)}, f32[24,1152]{1,0:T(8,128)S(1)}, u32[]{:S(2)}, u32[]{:S(2)}) collective-permute-start(f32[24,1152]{1,0:T(8,128)S(1)} %slice.9), channel_id=1, source_target_pairs={{0,1},{1,4},{4,5},{5,0},{2,3},{3,6},{6,7},{7,2},{8,9},{9,12},{12,1... | collective-permute-start | bytes 331784 | tf_op jit(solution)/shard_map/ppermute | solution.py:18
  99.9 4.1 %collective-permute-start.29 = (f32[48,1152]{1,0:T(8,128)S(1)}, f32[48,1152]{1,0:T(8,128)S(1)}, u32[]{:S(2)}, u32[]{:S(2)}) collective-permute-start(f32[48,1152]{1,0:T(8,128)S(1)} %collective-permute-done.24.refs_1_), channel_id=1, source_target_pairs={{0,2},{2,0},{1,3},{3,1},{4,6},{6,4},{5,7},{7,5},{8,10},{10,8},{9,1... | collective-permute-start | bytes 663560 | tf_op jit(solution)/shard_map/ppermute | solution.py:22
  99.9 4.1 %collective-permute-start.32 = (f32[48,1152]{1,0:T(8,128)S(1)}, f32[48,1152]{1,0:T(8,128)S(1)}, u32[]{:S(2)}, u32[]{:S(2)}) collective-permute-start(f32[48,1152]{1,0:T(8,128)S(1)} %collective-permute-done.26.refs_4_), channel_id=1, source_target_pairs={{0,2},{2,0},{1,3},{3,1},{4,6},{6,4},{5,7},{7,5},{8,10},{10,8},{9,1... | collective-permute-start | bytes 663560 | tf_op jit(solution)/shard_map/ppermute | solution.py:22
  102.6 1.3 collective-permute-start.30
  102.6 1.5 collective-permute-start.31
  108.9 34.3 %copy-start.2 = (f32[125,500]{0,1:T(8,128)S(1)}, f32[125,500]{0,1:T(8,128)}, u32[]{:S(2)}) copy-start(f32[125,500]{0,1:T(8,128)} %param.8) | copy-start | bytes 750004
  108.9 40.7 %copy-start.4 = (f32[125,96]{0,1:T(8,128)S(1)}, f32[125,96]{0,1:T(8,128)}, u32[]{:S(2)}) copy-start(f32[125,96]{0,1:T(8,128)} %param.9) | copy-start | bytes 144004
  122.7 5.4 %collective-permute-start.33 = (f32[48,128]{1,0:T(8,128)S(1)}, f32[48,128]{1,0:T(8,128)S(1)}, u32[]{:S(2)}, u32[]{:S(2)}) collective-permute-start(f32[48,128]{1,0:T(8,128)S(1)} %reduce_sum.9), channel_id=1, source_target_pairs={{0,128},{64,192},{128,0},{192,64},{1,129},{65,193},{129,1},{193,65... | collective-permute-start | bytes 73736 | tf_op jit(solution)/shard_map/ppermute | solution.py:31
  122.8 5.3 %collective-permute-start.34 = (f32[48,128]{1,0:T(8,128)S(1)}, f32[48,128]{1,0:T(8,128)S(1)}, u32[]{:S(2)}, u32[]{:S(2)}) collective-permute-start(f32[48,128]{1,0:T(8,128)S(1)} %reduce_sum.9), channel_id=1, source_target_pairs={{0,64},{64,0},{128,192},{192,128},{1,65},{65,1},{129,193},{193,129... | collective-permute-start | bytes 73736 | tf_op jit(solution)/shard_map/ppermute | solution.py:31
  125.9 5.0 %collective-permute-start.35 = (f32[48,128]{1,0:T(8,128)S(1)}, f32[48,128]{1,0:T(8,128)S(1)}, u32[]{:S(2)}, u32[]{:S(2)}) collective-permute-start(f32[48,128]{1,0:T(8,128)S(1)} %reduce_sum.9), channel_id=1, source_target_pairs={{0,192},{64,128},{128,64},{192,0},{1,193},{65,129},{129,65},{193,1... | collective-permute-start | bytes 73736 | tf_op jit(solution)/shard_map/ppermute | solution.py:31
  143.4 1.3 collective-permute-start.36
  144.8 5.1 %collective-permute-start.37 = (f32[104,125]{1,0:T(8,128)S(1)}, f32[104,125]{1,0:T(8,128)S(1)}, u32[]{:S(2)}, u32[]{:S(2)}) collective-permute-start(f32[104,125]{1,0:T(8,128)S(1)} %add.15.a_ref), channel_id=1, source_target_pairs={{0,1},{1,0},{4,5},{5,4},{2,3},{3,2},{6,7},{7,6},{8,9},{9,8},{12,13... | collective-permute-start | bytes 156008 | tf_op jit(solution)/shard_map/ppermute | solution.py:31
  144.9 7.4 %collective-permute-start.38 = (f32[104,125]{1,0:T(8,128)S(1)}, f32[104,125]{1,0:T(8,128)S(1)}, u32[]{:S(2)}, u32[]{:S(2)}) collective-permute-start(f32[104,125]{1,0:T(8,128)S(1)} %add.15.a_ref), channel_id=1, source_target_pairs={{0,4},{1,5},{4,0},{5,1},{2,6},{3,7},{6,2},{7,3},{8,12},{9,13},{12,... | collective-permute-start | bytes 156008 | tf_op jit(solution)/shard_map/ppermute | solution.py:31
  149.3 5.3 %collective-permute-start.39 = (f32[104,125]{1,0:T(8,128)S(1)}, f32[104,125]{1,0:T(8,128)S(1)}, u32[]{:S(2)}, u32[]{:S(2)}) collective-permute-start(f32[104,125]{1,0:T(8,128)S(1)} %add.15.a_ref), channel_id=1, source_target_pairs={{0,5},{1,4},{4,1},{5,0},{2,7},{3,6},{6,3},{7,2},{8,13},{9,12},{12,... | collective-permute-start | bytes 156008 | tf_op jit(solution)/shard_map/ppermute | solution.py:31

commit v6 on v4

--- a/solution.py
+++ b/solution.py
@@ -257,13 +257,12 @@
     rows = [rdm, swap(rdm, "y", NY, 1)]
     near = {0: pair_coeffs}
     far = {0: swap(pair_coeffs, "y", NY, 3)}
+    far[1], far[7] = shift(far[0], "z", NZ, -1), shift(far[0], "z", NZ, 1)
     for k in range(1, NZ // 2):
-        for found in (near, far):
-            if found is near or k < 3:
-                found[k] = shift(found[k - 1], "z", NZ, -1)
-                found[NZ - k] = shift(found[(NZ - k + 1) % NZ], "z", NZ, 1)
+        near[k] = shift(near[k - 1], "z", NZ, -1)
+        near[NZ - k] = shift(near[(NZ - k + 1) % NZ], "z", NZ, 1)
     near[4] = shift(near[3], "z", NZ, -1)
-    for k in (3, 5, 4):
+    for k in (2, 6, 3, 5, 4):
         far[k] = swap(near[k], "y", NY, 3)
 
     kept, sent, *rows = pair_product([near[k] for k in range(NZ)], rows, True)

time: 154 us -> 158 us (1.026)
  waiting for transfers between devices: 48.9 us -> 51.8 us
    ppermute x11 -> x13, waiting for transfers between devices: 11.5 us -> 16.7 us  [swap(): return lax.ppermute(value, axis, [(i, i ^ mask) for i in range(size)])]
    ppermute x11 -> x13, starting transfers between devices: 18.3 us -> 21.5 us  [swap(): return lax.ppermute(value, axis, [(i, i ^ mask) for i in range(size)])]
    ppermute x19 -> x17, starting transfers between devices: 33.7 us -> 31.2 us  [shift(): lax.ppermute(value, axis, [(i, (i + step) % size) for i in range(size)])]
    ppermute x19 -> x17, waiting for transfers between devices: 27.2 us -> 24.7 us  [shift(): lax.ppermute(value, axis, [(i, (i + step) % size) for i in range(size)])]
where the time goes in v6:
time: 158 us
  starting transfers between devices  62 us (39%)
  waiting for transfers between devices  51.8 us (33%)
  blocking collectives  28.9 us (18%)
  Pallas kernels  12.1 us (8%)
  local copies, waits for them, and re-layouts  2.31 us (1%)
    ppermute x17, starting transfers between devices, shift(): lax.ppermute(value, axis, [(i, (i + step) % size) for i in range(size)])  31.2 us
    ppermute x17, waiting for transfers between devices, shift(): lax.ppermute(value, axis, [(i, (i + step) % size) for i in range(size)])  24.7 us
    ppermute x13, starting transfers between devices, swap(): return lax.ppermute(value, axis, [(i, i ^ mask) for i in range(size)])  21.5 us
    all_to_all x1, blocking collectives, on_device(): lax.all_to_all(tiles, 'z', split_axis=0, concat_axis=0, tiled=True)  16.7 us
    ppermute x13, waiting for transfers between devices, swap(): return lax.ppermute(value, axis, [(i, i ^ mask) for i in range(size)])  16.7 us
    all_to_all x1, blocking collectives, on_device(): lax.all_to_all(jnp.broadcast_to(piece[None], tiles.shape), 'z', split_axi...  12.2 us
    ppermute x2, starting transfers between devices, send_home(): return lax.ppermute(value, ('y', 'z', 'xh', 'co', 'xl'), pairs)  7.68 us
    ppermute x2, waiting for transfers between devices, send_home(): return lax.ppermute(value, ('y', 'z', 'xh', 'co', 'xl'), pairs)  6.16 us
  transfers between devices with their start and end apart: 40, of which 25 were waited for; matrix products, arithmetic and copies ran while one was open for 0% of the time, Pallas kernels for 2%

profile of v6, /device:TPU:6, one launch (start us, length us, event | category | flops | bytes accessed | tf_op | source)
XLA Modules:
  0.0 158.0 jit_solution(10792728410009526917)
XLA Ops:
  0.6 1.7 %collective-permute-start.7 = (f32[288,1152]{1,0:T(8,128)}, f32[288,1152]{1,0:T(8,128)S(1)}, u32[]{:S(2)}, u32[]{:S(2)}) collective-permute-start(f32[288,1152]{1,0:T(8,128)} %refs_8_.1), channel_id=1, source_target_pairs={{0,64},{64,0},{128,192},{192,128},{1,65},{65,1},{129,193},{193,129... | collective-permute-start | bytes 3981320 | tf_op jit(solution)/shard_map/ppermute | solution.py:26
  2.3 5.9 %collective-permute-start = (f32[48,1152]{1,0:T(8,128)}, f32[48,1152]{1,0:T(8,128)S(1)}, u32[]{:S(2)}, u32[]{:S(2)}) collective-permute-start(f32[48,1152]{1,0:T(8,128)} %refs_0_.1), channel_id=1, source_target_pairs={{0,56},{8,0},{16,8},{24,16},{32,24},{40,32},{48,40},{56,48},{1,57}... | collective-permute-start | bytes 663560 | tf_op jit(solution)/shard_map/ppermute | solution.py:18
  8.2 4.7 %collective-permute-done.refs_1_ = f32[48,1152]{1,0:T(8,128)S(1)} collective-permute-done((f32[48,1152]{1,0:T(8,128)}, f32[48,1152]{1,0:T(8,128)S(1)}, u32[]{:S(2)}, u32[]{:S(2)}) %collective-permute-start) | collective-permute-done | bytes 221216 | tf_op jit(solution)/shard_map/ppermute | solution.py:18
  12.9 3.6 %collective-permute-start.1 = (f32[48,1152]{1,0:T(8,128)S(1)}, f32[48,1152]{1,0:T(8,128)S(1)}, u32[]{:S(2)}, u32[]{:S(2)}) collective-permute-start(f32[48,1152]{1,0:T(8,128)S(1)} %collective-permute-done.refs_1_), channel_id=1, source_target_pairs={{0,56},{8,0},{16,8},{24,16},{32,24},{40,32},{48,40},{56,48},{1,57}... | collective-permute-start | bytes 663560 | tf_op jit(solution)/shard_map/ppermute | solution.py:18
  16.5 2.2 %collective-permute-start.14 = (f32[48,1152]{1,0:T(8,128)}, f32[48,1152]{1,0:T(8,128)S(1)}, u32[]{:S(2)}, u32[]{:S(2)}) collective-permute-start(f32[48,1152]{1,0:T(8,128)} %refs_0_.1), channel_id=1, source_target_pairs={{0,192},{64,128},{128,64},{192,0},{1,193},{65,129},{129,65},{193,1... | collective-permute-start | bytes 663560 | tf_op jit(solution)/shard_map/ppermute | solution.py:26
  18.6 1.3 collective-permute-done.1.refs_2_
  20.0 3.7 %collective-permute-start.2 = (f32[48,1152]{1,0:T(8,128)S(1)}, f32[48,1152]{1,0:T(8,128)S(1)}, u32[]{:S(2)}, u32[]{:S(2)}) collective-permute-start(f32[48,1152]{1,0:T(8,128)S(1)} %collective-permute-done.1.refs_2_), channel_id=1, source_target_pairs={{0,56},{8,0},{16,8},{24,16},{32,24},{40,32},{48,40},{56,48},{1,57}... | collective-permute-start | bytes 663560 | tf_op jit(solution)/shard_map/ppermute | solution.py:18
  23.8 3.2 %collective-permute-start.16 = (f32[48,1152]{1,0:T(8,128)S(1)}, f32[48,1152]{1,0:T(8,128)S(1)}, u32[]{:S(2)}, u32[]{:S(2)}) collective-permute-start(f32[48,1152]{1,0:T(8,128)S(1)} %collective-permute-done.14.refs_6_), channel_id=1, source_target_pairs={{0,56},{8,0},{16,8},{24,16},{32,24},{40,32},{48,40},{56,48},{1,57}... | collective-permute-start | bytes 663560 | tf_op jit(solution)/shard_map/ppermute | solution.py:18
  27.1 2.4 %collective-permute-done.2.refs_3_ = f32[48,1152]{1,0:T(8,128)S(1)} collective-permute-done((f32[48,1152]{1,0:T(8,128)S(1)}, f32[48,1152]{1,0:T(8,128)S(1)}, u32[]{:S(2)}, u32[]{:S(2)}) %collective-permute-start.2) | collective-permute-done | bytes 221216 | tf_op jit(solution)/shard_map/ppermute | solution.py:18
  29.4 3.7 %collective-permute-start.3 = (f32[48,1152]{1,0:T(8,128)S(1)}, f32[48,1152]{1,0:T(8,128)S(1)}, u32[]{:S(2)}, u32[]{:S(2)}) collective-permute-start(f32[48,1152]{1,0:T(8,128)S(1)} %collective-permute-done.2.refs_3_), channel_id=1, source_target_pairs={{0,56},{8,0},{16,8},{24,16},{32,24},{40,32},{48,40},{56,48},{1,57}... | collective-permute-start | bytes 663560 | tf_op jit(solution)/shard_map/ppermute | solution.py:18
  33.1 2.2 %collective-permute-start.13 = (f32[48,1152]{1,0:T(8,128)S(1)}, f32[48,1152]{1,0:T(8,128)S(1)}, u32[]{:S(2)}, u32[]{:S(2)}) collective-permute-start(f32[48,1152]{1,0:T(8,128)S(1)} %collective-permute-done.5.refs_6_), channel_id=1, source_target_pairs={{0,192},{64,128},{128,64},{192,0},{1,193},{65,129},{129,65},{193,1... | collective-permute-start | bytes 663560 | tf_op jit(solution)/shard_map/ppermute | solution.py:26
  35.3 1.1 collective-permute-start.9
  36.4 2.2 %collective-permute-start.10 = (f32[48,1152]{1,0:T(8,128)S(1)}, f32[48,1152]{1,0:T(8,128)S(1)}, u32[]{:S(2)}, u32[]{:S(2)}) collective-permute-start(f32[48,1152]{1,0:T(8,128)S(1)} %collective-permute-done.2.refs_3_), channel_id=1, source_target_pairs={{0,192},{64,128},{128,64},{192,0},{1,193},{65,129},{129,65},{193,1... | collective-permute-start | bytes 663560 | tf_op jit(solution)/shard_map/ppermute | solution.py:26
  38.5 1.1 collective-permute-start.12
  39.6 2.2 %collective-permute-start.11 = (f32[48,1152]{1,0:T(8,128)S(1)}, f32[48,1152]{1,0:T(8,128)S(1)}, u32[]{:S(2)}, u32[]{:S(2)}) collective-permute-start(f32[48,1152]{1,0:T(8,128)S(1)} %collective-permute-done.3.refs_4_), channel_id=1, source_target_pairs={{0,192},{64,128},{128,64},{192,0},{1,193},{65,129},{129,65},{193,1... | collective-permute-start | bytes 663560 | tf_op jit(solution)/shard_map/ppermute | solution.py:26
  41.8 1.3 copy-done.1
  43.1 0.9 copy-done.3
  44.0 2.7 %shard_map.76 = (f32[192,576]{1,0:T(8,128)S(1)}, f32[192,576]{1,0:T(8,128)S(1)}, bf16[576,1152]{1,0:T(8,128)(2,1)S(1)}, bf16[576,1152]{1,0:T(8,128)(2,1)S(1)}) custom-call(f32[48,1152]{1,0:T(8,128)S(1)} %copy-done.3, f32[48,1152]{1,0:T(8,128)S(1)} %collective-permute-done.refs_1_, f32[48,1152]{1,0:T(8,128)S(1)} %collective-permute-done.1.refs_2_, ...), custom_call_target="tpu_custom_call" | custom-call | flops 1000 | bytes 1000 | tf_op jit(solution)/shard_map/pallas_call | solution.py:79
  47.4 3.3 %collective-permute-done.10.refs_1_ = f32[48,1152]{1,0:T(8,128)S(1)} collective-permute-done((f32[48,1152]{1,0:T(8,128)S(1)}, f32[48,1152]{1,0:T(8,128)S(1)}, u32[]{:S(2)}, u32[]{:S(2)}) %collective-permute-start.10) | collective-permute-done | bytes 221216 | tf_op jit(solution)/shard_map/ppermute | solution.py:26
  50.7 2.4 %collective-permute-done.12.refs_3_ = f32[48,1152]{1,0:T(8,128)S(1)} collective-permute-done((f32[48,1152]{1,0:T(8,128)S(1)}, f32[48,1152]{1,0:T(8,128)S(1)}, u32[]{:S(2)}, u32[]{:S(2)}) %collective-permute-start.12) | collective-permute-done | bytes 221216 | tf_op jit(solution)/shard_map/ppermute | solution.py:26
  53.1 2.4 %collective-permute-done.11.refs_2_ = f32[48,1152]{1,0:T(8,128)S(1)} collective-permute-done((f32[48,1152]{1,0:T(8,128)S(1)}, f32[48,1152]{1,0:T(8,128)S(1)}, u32[]{:S(2)}, u32[]{:S(2)}) %collective-permute-start.11) | collective-permute-done | bytes 221216 | tf_op jit(solution)/shard_map/ppermute | solution.py:26
  55.5 2.7 %shard_map.77 = (f32[192,576]{1,0:T(8,128)S(1)}, f32[192,576]{1,0:T(8,128)S(1)}) custom-call(f32[48,1152]{1,0:T(8,128)S(1)} %collective-permute-done.9.refs_0_, f32[48,1152]{1,0:T(8,128)S(1)} %collective-permute-done.10.refs_1_, f32[48,1152]{1,0:T(8,128)S(1)} %collective-permute-done.11.refs_2_, f32[48,1152]{1,0:T(8,128)S(1)} %collective-permute-done.12.refs_3_, ...), custom_call_target="tpu_custom_call" | custom-call | flops 1528823808 | bytes 4423680 | tf_op jit(solution)/shard_map/pallas_call | solution.py:79
  58.8 1.4 collective-permute-done.17.refs_3_
  61.6 1.5 collective-permute-start.19
  63.1 3.1 %collective-permute-done.18.up_ref = f32[24,1152]{1,0:T(8,128)S(1)} collective-permute-done((f32[24,1152]{1,0:T(8,128)S(1)}, f32[24,1152]{1,0:T(8,128)S(1)}, u32[]{:S(2)}, u32[]{:S(2)}) %collective-permute-start.18) | collective-permute-done | bytes 110624 | tf_op jit(solution)/shard_map/ppermute | solution.py:18
  66.2 1.4 collective-permute-done.19.down_ref
  68.0 1.7 %collective-permute-start.21 = (f32[48,1152]{1,0:T(8,128)S(1)}, f32[48,1152]{1,0:T(8,128)S(1)}, u32[]{:S(2)}, u32[]{:S(2)}) collective-permute-start(f32[48,1152]{1,0:T(8,128)S(1)} %get-tuple-element.35), channel_id=1, source_target_pairs={{0,5},{1,0},{4,1},{5,4},{2,7},{3,2},{6,3},{7,6},{8,13},{9,8},{12,9... | collective-permute-start | bytes 663560 | tf_op jit(solution)/shard_map/ppermute | solution.py:18
  69.8 4.3 %collective-permute-done.20.one_ref = f32[48,1152]{1,0:T(8,128)S(1)} collective-permute-done((f32[48,1152]{1,0:T(8,128)S(1)}, f32[48,1152]{1,0:T(8,128)S(1)}, u32[]{:S(2)}, u32[]{:S(2)}) %collective-permute-start.20) | collective-permute-done | bytes 221216 | tf_op jit(solution)/shard_map/ppermute | solution.py:18
  74.0 1.5 collective-permute-done.21.two_ref
  75.7 3.3 %collective-permute-start.22 = (f32[48,576]{1,0:T(8,128)S(1)}, f32[48,576]{1,0:T(8,128)S(1)}, u32[]{:S(2)}, u32[]{:S(2)}) collective-permute-start(f32[48,576]{1,0:T(8,128)S(1)} %get-tuple-element.36), channel_id=1, source_target_pairs={{0,0},{2,34},{1,9},{3,43},{4,20},{6,54},{5,29},{7,63},{8,8},{10,42... | collective-permute-start | bytes 331784 | tf_op jit(solution)/shard_map/ppermute | solution.py:285
  79.0 4.4 %collective-permute-start.23 = (f32[48,576]{1,0:T(8,128)S(1)}, f32[48,576]{1,0:T(8,128)S(1)}, u32[]{:S(2)}, u32[]{:S(2)}) collective-permute-start(f32[48,576]{1,0:T(8,128)S(1)} %get-tuple-element.37), channel_id=1, source_target_pairs={{0,208},{2,242},{1,217},{3,251},{4,228},{6,198},{5,237},{7,207},{8... | collective-permute-start | bytes 331784 | tf_op jit(solution)/shard_map/ppermute | solution.py:285
  83.4 4.2 %collective-permute-done.22.first_ref = f32[48,576]{1,0:T(8,128)S(1)} collective-permute-done((f32[48,576]{1,0:T(8,128)S(1)}, f32[48,576]{1,0:T(8,128)S(1)}, u32[]{:S(2)}, u32[]{:S(2)}) %collective-permute-start.22) | collective-permute-done | bytes 110624 | tf_op jit(solution)/shard_map/ppermute | solution.py:285
  87.6 2.0 %collective-permute-done.23.second_ref = f32[48,576]{1,0:T(8,128)S(1)} collective-permute-done((f32[48,576]{1,0:T(8,128)S(1)}, f32[48,576]{1,0:T(8,128)S(1)}, u32[]{:S(2)}, u32[]{:S(2)}) %collective-permute-start.23) | collective-permute-done | bytes 110624 | tf_op jit(solution)/shard_map/ppermute | solution.py:285
  89.8 3.2 %collective-permute-start.26 = (f32[48,1152]{1,0:T(8,128)S(1)}, f32[48,1152]{1,0:T(8,128)S(1)}, u32[]{:S(2)}, u32[]{:S(2)}) collective-permute-start(f32[48,1152]{1,0:T(8,128)S(1)} %shard_map.81.refs_0_), channel_id=1, source_target_pairs={{0,1},{1,4},{4,5},{5,0},{2,3},{3,6},{6,7},{7,2},{8,9},{9,12},{12,1... | collective-permute-start | bytes 663560 | tf_op jit(solution)/shard_map/ppermute | solution.py:18
  93.0 3.9 %collective-permute-done.24.refs_1_ = f32[48,1152]{1,0:T(8,128)S(1)} collective-permute-done((f32[48,1152]{1,0:T(8,128)S(1)}, f32[48,1152]{1,0:T(8,128)S(1)}, u32[]{:S(2)}, u32[]{:S(2)}) %collective-permute-start.24) | collective-permute-done | bytes 221216 | tf_op jit(solution)/shard_map/ppermute | solution.py:18
  97.2 3.3 %collective-permute-start.27 = (f32[24,1152]{1,0:T(8,128)S(1)}, f32[24,1152]{1,0:T(8,128)S(1)}, u32[]{:S(2)}, u32[]{:S(2)}) collective-permute-start(f32[24,1152]{1,0:T(8,128)S(1)} %slice.9), channel_id=1, source_target_pairs={{0,1},{1,4},{4,5},{5,0},{2,3},{3,6},{6,7},{7,2},{8,9},{9,12},{12,1... | collective-permute-start | bytes 331784 | tf_op jit(solution)/shard_map/ppermute | solution.py:18
  101.0 2.1 %collective-permute-done.25.refs_2_ = f32[24,1152]{1,0:T(8,128)S(1)} collective-permute-done((f32[24,1152]{1,0:T(8,128)S(1)}, f32[24,1152]{1,0:T(8,128)S(1)}, u32[]{:S(2)}, u32[]{:S(2)}) %collective-permute-start.25) | collective-permute-done | bytes 110624 | tf_op jit(solution)/shard_map/ppermute | solution.py:18
  104.6 4.8 %shard_map.82 = f32[8,48,128]{2,1,0:T(8,128)S(1)} custom-call(f32[48,1152]{1,0:T(8,128)S(1)} %shard_map.81.refs_0_, f32[48,1152]{1,0:T(8,128)S(1)} %collective-permute-done.24.refs_1_, f32[24,1152]{1,0:T(8,128)S(1)} %collective-permute-done.25.refs_2_, f32[24,1152]{1,0:T(8,128)S(1)} %collective-permute-done.27.refs_3_, ...), custom_call_target="tpu_custom_call" | custom-call | tf_op jit(solution)/shard_map/pallas_call | solution.py:196
  109.5 16.7 %all_to_all.10 = f32[8,48,128]{2,1,0:T(8,128)S(1)} all-to-all(f32[8,48,128]{2,1,0:T(8,128)S(1)} %shard_map.82), channel_id=1, replica_groups=mesh['y'=4,'z'=8,'xh'=2,'co'=2,'xl'=2] {'z'}, dimensions={0} | all-to-all | bytes 393216 | tf_op jit(solution)/shard_map/all_to_all | solution.py:302
  126.3 2.2 %collective-permute-start.34 = (f32[48,128]{1,0:T(8,128)S(1)}, f32[48,128]{1,0:T(8,128)S(1)}, u32[]{:S(2)}, u32[]{:S(2)}) collective-permute-start(f32[48,128]{1,0:T(8,128)S(1)} %reduce_sum.9), channel_id=1, source_target_pairs={{0,64},{64,0},{128,192},{192,128},{1,65},{65,1},{129,193},{193,129... | collective-permute-start | bytes 73736 | tf_op jit(solution)/shard_map/ppermute | solution.py:26
  128.5 1.9 %collective-permute-start.35 = (f32[48,128]{1,0:T(8,128)S(1)}, f32[48,128]{1,0:T(8,128)S(1)}, u32[]{:S(2)}, u32[]{:S(2)}) collective-permute-start(f32[48,128]{1,0:T(8,128)S(1)} %reduce_sum.9), channel_id=1, source_target_pairs={{0,192},{64,128},{128,64},{192,0},{1,193},{65,129},{129,65},{193,1... | collective-permute-start | bytes 73736 | tf_op jit(solution)/shard_map/ppermute | solution.py:26
  130.4 1.2 collective-permute-done.33
  131.6 1.9 %collective-permute-done.35 = f32[48,128]{1,0:T(8,128)S(1)} collective-permute-done((f32[48,128]{1,0:T(8,128)S(1)}, f32[48,128]{1,0:T(8,128)S(1)}, u32[]{:S(2)}, u32[]{:S(2)}) %collective-permute-start.35) | collective-permute-done | bytes 24608 | tf_op jit(solution)/shard_map/ppermute | solution.py:26
  133.5 12.2 %all_to_all.11.tiles_ref = f32[8,48,128]{2,1,0:T(8,128)S(1)} all-to-all(f32[8,48,128]{2,1,0:T(8,128)S(1)} %broadcast_in_dim.2), channel_id=1, replica_groups=mesh['y'=4,'z'=8,'xh'=2,'co'=2,'xl'=2] {'z'}, dimensions={0} | all-to-all | bytes 393216 | tf_op jit(solution)/shard_map/all_to_all | solution.py:304
  146.1 1.2 collective-permute-done.36
  147.4 4.4 %collective-permute-start.38 = (f32[104,125]{1,0:T(8,128)S(1)}, f32[104,125]{1,0:T(8,128)S(1)}, u32[]{:S(2)}, u32[]{:S(2)}) collective-permute-start(f32[104,125]{1,0:T(8,128)S(1)} %add.15.a_ref), channel_id=1, source_target_pairs={{0,4},{1,5},{4,0},{5,1},{2,6},{3,7},{6,2},{7,3},{8,12},{9,13},{12,... | collective-permute-start | bytes 156008 | tf_op jit(solution)/shard_map/ppermute | solution.py:26
  152.4 2.3 %collective-permute-done.38.c_ref = f32[104,125]{1,0:T(8,128)S(1)} collective-permute-done((f32[104,125]{1,0:T(8,128)S(1)}, f32[104,125]{1,0:T(8,128)S(1)}, u32[]{:S(2)}, u32[]{:S(2)}) %collective-permute-start.38) | collective-permute-done | bytes 52032 | tf_op jit(solution)/shard_map/ppermute | solution.py:26
  154.8 2.4 %collective-permute-done.39.d_ref = f32[104,125]{1,0:T(8,128)S(1)} collective-permute-done((f32[104,125]{1,0:T(8,128)S(1)}, f32[104,125]{1,0:T(8,128)S(1)}, u32[]{:S(2)}, u32[]{:S(2)}) %collective-permute-start.39) | collective-permute-done | bytes 52032 | tf_op jit(solution)/shard_map/ppermute | solution.py:26
  (60 shorter events, 7.9 us)
Async XLA Ops:
  0.6 39.0 %collective-permute-start.7 = (f32[288,1152]{1,0:T(8,128)}, f32[288,1152]{1,0:T(8,128)S(1)}, u32[]{:S(2)}, u32[]{:S(2)}) collective-permute-start(f32[288,1152]{1,0:T(8,128)} %refs_8_.1), channel_id=1, source_target_pairs={{0,64},{64,0},{128,192},{192,128},{1,65},{65,1},{129,193},{193,129... | collective-permute-start | bytes 3981320 | tf_op jit(solution)/shard_map/ppermute | solution.py:26
  2.3 10.6 %collective-permute-start = (f32[48,1152]{1,0:T(8,128)}, f32[48,1152]{1,0:T(8,128)S(1)}, u32[]{:S(2)}, u32[]{:S(2)}) collective-permute-start(f32[48,1152]{1,0:T(8,128)} %refs_0_.1), channel_id=1, source_target_pairs={{0,56},{8,0},{16,8},{24,16},{32,24},{40,32},{48,40},{56,48},{1,57}... | collective-permute-start | bytes 663560 | tf_op jit(solution)/shard_map/ppermute | solution.py:18
  8.1 10.5 %collective-permute-start.4 = (f32[48,1152]{1,0:T(8,128)}, f32[48,1152]{1,0:T(8,128)S(1)}, u32[]{:S(2)}, u32[]{:S(2)}) collective-permute-start(f32[48,1152]{1,0:T(8,128)} %refs_0_.1), channel_id=1, source_target_pairs={{0,8},{8,16},{16,24},{24,32},{32,40},{40,48},{48,56},{56,0},{1,9},... | collective-permute-start | bytes 663560 | tf_op jit(solution)/shard_map/ppermute | solution.py:18
  12.9 7.1 %collective-permute-start.1 = (f32[48,1152]{1,0:T(8,128)S(1)}, f32[48,1152]{1,0:T(8,128)S(1)}, u32[]{:S(2)}, u32[]{:S(2)}) collective-permute-start(f32[48,1152]{1,0:T(8,128)S(1)} %collective-permute-done.refs_1_), channel_id=1, source_target_pairs={{0,56},{8,0},{16,8},{24,16},{32,24},{40,32},{48,40},{56,48},{1,57}... | collective-permute-start | bytes 663560 | tf_op jit(solution)/shard_map/ppermute | solution.py:18
  16.5 7.4 %collective-permute-start.14 = (f32[48,1152]{1,0:T(8,128)}, f32[48,1152]{1,0:T(8,128)S(1)}, u32[]{:S(2)}, u32[]{:S(2)}) collective-permute-start(f32[48,1152]{1,0:T(8,128)} %refs_0_.1), channel_id=1, source_target_pairs={{0,192},{64,128},{128,64},{192,0},{1,193},{65,129},{129,65},{193,1... | collective-permute-start | bytes 663560 | tf_op jit(solution)/shard_map/ppermute | solution.py:26
  18.6 8.4 %collective-permute-start.5 = (f32[48,1152]{1,0:T(8,128)S(1)}, f32[48,1152]{1,0:T(8,128)S(1)}, u32[]{:S(2)}, u32[]{:S(2)}) collective-permute-start(f32[48,1152]{1,0:T(8,128)S(1)} %collective-permute-done.4.refs_7_), channel_id=1, source_target_pairs={{0,8},{8,16},{16,24},{24,32},{32,40},{40,48},{48,56},{56,0},{1,9},... | collective-permute-start | bytes 663560 | tf_op jit(solution)/shard_map/ppermute | solution.py:18
  20.0 9.5 %collective-permute-start.2 = (f32[48,1152]{1,0:T(8,128)S(1)}, f32[48,1152]{1,0:T(8,128)S(1)}, u32[]{:S(2)}, u32[]{:S(2)}) collective-permute-start(f32[48,1152]{1,0:T(8,128)S(1)} %collective-permute-done.1.refs_2_), channel_id=1, source_target_pairs={{0,56},{8,0},{16,8},{24,16},{32,24},{40,32},{48,40},{56,48},{1,57}... | collective-permute-start | bytes 663560 | tf_op jit(solution)/shard_map/ppermute | solution.py:18
  23.8 9.3 %collective-permute-start.15 = (f32[48,1152]{1,0:T(8,128)S(1)}, f32[48,1152]{1,0:T(8,128)S(1)}, u32[]{:S(2)}, u32[]{:S(2)}) collective-permute-start(f32[48,1152]{1,0:T(8,128)S(1)} %collective-permute-done.14.refs_6_), channel_id=1, source_target_pairs={{0,8},{8,16},{16,24},{24,32},{32,40},{40,48},{48,56},{56,0},{1,9},... | collective-permute-start | bytes 663560 | tf_op jit(solution)/shard_map/ppermute | solution.py:18
  23.8 11.5 %collective-permute-start.16 = (f32[48,1152]{1,0:T(8,128)S(1)}, f32[48,1152]{1,0:T(8,128)S(1)}, u32[]{:S(2)}, u32[]{:S(2)}) collective-permute-start(f32[48,1152]{1,0:T(8,128)S(1)} %collective-permute-done.14.refs_6_), channel_id=1, source_target_pairs={{0,56},{8,0},{16,8},{24,16},{32,24},{40,32},{48,40},{56,48},{1,57}... | collective-permute-start | bytes 663560 | tf_op jit(solution)/shard_map/ppermute | solution.py:18
  27.1 9.3 %collective-permute-start.6 = (f32[48,1152]{1,0:T(8,128)S(1)}, f32[48,1152]{1,0:T(8,128)S(1)}, u32[]{:S(2)}, u32[]{:S(2)}) collective-permute-start(f32[48,1152]{1,0:T(8,128)S(1)} %collective-permute-done.5.refs_6_), channel_id=1, source_target_pairs={{0,8},{8,16},{16,24},{24,32},{32,40},{40,48},{48,56},{56,0},{1,9},... | collective-permute-start | bytes 663560 | tf_op jit(solution)/shard_map/ppermute | solution.py:18
  29.4 9.1 %collective-permute-start.3 = (f32[48,1152]{1,0:T(8,128)S(1)}, f32[48,1152]{1,0:T(8,128)S(1)}, u32[]{:S(2)}, u32[]{:S(2)}) collective-permute-start(f32[48,1152]{1,0:T(8,128)S(1)} %collective-permute-done.2.refs_3_), channel_id=1, source_target_pairs={{0,56},{8,0},{16,8},{24,16},{32,24},{40,32},{48,40},{56,48},{1,57}... | collective-permute-start | bytes 663560 | tf_op jit(solution)/shard_map/ppermute | solution.py:18
  33.1 13.7 %collective-permute-start.13 = (f32[48,1152]{1,0:T(8,128)S(1)}, f32[48,1152]{1,0:T(8,128)S(1)}, u32[]{:S(2)}, u32[]{:S(2)}) collective-permute-start(f32[48,1152]{1,0:T(8,128)S(1)} %collective-permute-done.5.refs_6_), channel_id=1, source_target_pairs={{0,192},{64,128},{128,64},{192,0},{1,193},{65,129},{129,65},{193,1... | collective-permute-start | bytes 663560 | tf_op jit(solution)/shard_map/ppermute | solution.py:26
  35.3 12.1 %collective-permute-start.9 = (f32[48,1152]{1,0:T(8,128)S(1)}, f32[48,1152]{1,0:T(8,128)S(1)}, u32[]{:S(2)}, u32[]{:S(2)}) collective-permute-start(f32[48,1152]{1,0:T(8,128)S(1)} %collective-permute-done.1.refs_2_), channel_id=1, source_target_pairs={{0,192},{64,128},{128,64},{192,0},{1,193},{65,129},{129,65},{193,1... | collective-permute-start | bytes 663560 | tf_op jit(solution)/shard_map/ppermute | solution.py:26
  36.4 14.4 %collective-permute-start.10 = (f32[48,1152]{1,0:T(8,128)S(1)}, f32[48,1152]{1,0:T(8,128)S(1)}, u32[]{:S(2)}, u32[]{:S(2)}) collective-permute-start(f32[48,1152]{1,0:T(8,128)S(1)} %collective-permute-done.2.refs_3_), channel_id=1, source_target_pairs={{0,192},{64,128},{128,64},{192,0},{1,193},{65,129},{129,65},{193,1... | collective-permute-start | bytes 663560 | tf_op jit(solution)/shard_map/ppermute | solution.py:26
  38.5 14.6 %collective-permute-start.12 = (f32[48,1152]{1,0:T(8,128)S(1)}, f32[48,1152]{1,0:T(8,128)S(1)}, u32[]{:S(2)}, u32[]{:S(2)}) collective-permute-start(f32[48,1152]{1,0:T(8,128)S(1)} %collective-permute-done.6.refs_5_), channel_id=1, source_target_pairs={{0,192},{64,128},{128,64},{192,0},{1,193},{65,129},{129,65},{193,1... | collective-permute-start | bytes 663560 | tf_op jit(solution)/shard_map/ppermute | solution.py:26
  39.6 15.9 %collective-permute-start.11 = (f32[48,1152]{1,0:T(8,128)S(1)}, f32[48,1152]{1,0:T(8,128)S(1)}, u32[]{:S(2)}, u32[]{:S(2)}) collective-permute-start(f32[48,1152]{1,0:T(8,128)S(1)} %collective-permute-done.3.refs_4_), channel_id=1, source_target_pairs={{0,192},{64,128},{128,64},{192,0},{1,193},{65,129},{129,65},{193,1... | collective-permute-start | bytes 663560 | tf_op jit(solution)/shard_map/ppermute | solution.py:26
  41.8 1.3 copy-start.1
  43.1 0.9 copy-start.3
  55.5 49.2 %copy-start = (f32[48,96,500]{2,1,0:T(8,128)S(1)}, f32[48,96,500]{2,1,0:T(8,128)}, u32[]{:S(2)}) copy-start(f32[48,96,500]{2,1,0:T(8,128)} %refs_10_.1) | copy-start | bytes 27648004
  58.2 2.0 %collective-permute-start.17 = (f32[192,576]{1,0:T(8,128)S(1)}, f32[192,576]{1,0:T(8,128)S(1)}, u32[]{:S(2)}, u32[]{:S(2)}) collective-permute-start(f32[192,576]{1,0:T(8,128)S(1)} %get-tuple-element.28), channel_id=1, source_target_pairs={{0,2},{2,0},{1,3},{3,1},{4,6},{6,4},{5,7},{7,5},{8,10},{10,8},{9,1... | collective-permute-start | bytes 1327112 | tf_op jit(solution)/shard_map/ppermute | solution.py:22
  58.3 2.6 %collective-permute-start.8 = (f32[192,576]{1,0:T(8,128)S(1)}, f32[192,576]{1,0:T(8,128)S(1)}, u32[]{:S(2)}, u32[]{:S(2)}) collective-permute-start(f32[192,576]{1,0:T(8,128)S(1)} %get-tuple-element.24), channel_id=1, source_target_pairs={{0,2},{2,0},{1,3},{3,1},{4,6},{6,4},{5,7},{7,5},{8,10},{10,8},{9,1... | collective-permute-start | bytes 1327112 | tf_op jit(solution)/shard_map/ppermute | solution.py:22
  61.0 5.2 %collective-permute-start.18 = (f32[24,1152]{1,0:T(8,128)S(1)}, f32[24,1152]{1,0:T(8,128)S(1)}, u32[]{:S(2)}, u32[]{:S(2)}) collective-permute-start(f32[24,1152]{1,0:T(8,128)S(1)} %get-tuple-element.31), channel_id=1, source_target_pairs={{0,1},{1,4},{4,5},{5,0},{2,3},{3,6},{6,7},{7,2},{8,9},{9,12},{12,1... | collective-permute-start | bytes 331784 | tf_op jit(solution)/shard_map/ppermute | solution.py:18
  61.6 6.0 %collective-permute-start.19 = (f32[24,1152]{1,0:T(8,128)S(1)}, f32[24,1152]{1,0:T(8,128)S(1)}, u32[]{:S(2)}, u32[]{:S(2)}) collective-permute-start(f32[24,1152]{1,0:T(8,128)S(1)} %get-tuple-element.33), channel_id=1, source_target_pairs={{0,5},{1,0},{4,1},{5,4},{2,7},{3,2},{6,3},{7,6},{8,13},{9,8},{12,9... | collective-permute-start | bytes 331784 | tf_op jit(solution)/shard_map/ppermute | solution.py:18
  67.6 6.4 %collective-permute-start.20 = (f32[48,1152]{1,0:T(8,128)S(1)}, f32[48,1152]{1,0:T(8,128)S(1)}, u32[]{:S(2)}, u32[]{:S(2)}) collective-permute-start(f32[48,1152]{1,0:T(8,128)S(1)} %get-tuple-element.34), channel_id=1, source_target_pairs={{0,1},{1,4},{4,5},{5,0},{2,3},{3,6},{6,7},{7,2},{8,9},{9,12},{12,1... | collective-permute-start | bytes 663560 | tf_op jit(solution)/shard_map/ppermute | solution.py:18
  68.0 7.6 %collective-permute-start.21 = (f32[48,1152]{1,0:T(8,128)S(1)}, f32[48,1152]{1,0:T(8,128)S(1)}, u32[]{:S(2)}, u32[]{:S(2)}) collective-permute-start(f32[48,1152]{1,0:T(8,128)S(1)} %get-tuple-element.35), channel_id=1, source_target_pairs={{0,5},{1,0},{4,1},{5,4},{2,7},{3,2},{6,3},{7,6},{8,13},{9,8},{12,9... | collective-permute-start | bytes 663560 | tf_op jit(solution)/shard_map/ppermute | solution.py:18
  75.7 11.9 %collective-permute-start.22 = (f32[48,576]{1,0:T(8,128)S(1)}, f32[48,576]{1,0:T(8,128)S(1)}, u32[]{:S(2)}, u32[]{:S(2)}) collective-permute-start(f32[48,576]{1,0:T(8,128)S(1)} %get-tuple-element.36), channel_id=1, source_target_pairs={{0,0},{2,34},{1,9},{3,43},{4,20},{6,54},{5,29},{7,63},{8,8},{10,42... | collective-permute-start | bytes 331784 | tf_op jit(solution)/shard_map/ppermute | solution.py:285
  79.0 10.5 %collective-permute-start.23 = (f32[48,576]{1,0:T(8,128)S(1)}, f32[48,576]{1,0:T(8,128)S(1)}, u32[]{:S(2)}, u32[]{:S(2)}) collective-permute-start(f32[48,576]{1,0:T(8,128)S(1)} %get-tuple-element.37), channel_id=1, source_target_pairs={{0,208},{2,242},{1,217},{3,251},{4,228},{6,198},{5,237},{7,207},{8... | collective-permute-start | bytes 331784 | tf_op jit(solution)/shard_map/ppermute | solution.py:285
  89.7 7.2 %collective-permute-start.24 = (f32[48,1152]{1,0:T(8,128)S(1)}, f32[48,1152]{1,0:T(8,128)S(1)}, u32[]{:S(2)}, u32[]{:S(2)}) collective-permute-start(f32[48,1152]{1,0:T(8,128)S(1)} %shard_map.81.refs_0_), channel_id=1, source_target_pairs={{0,5},{1,0},{4,1},{5,4},{2,7},{3,2},{6,3},{7,6},{8,13},{9,8},{12,9... | collective-permute-start | bytes 663560 | tf_op jit(solution)/shard_map/ppermute | solution.py:18
  89.8 7.5 %collective-permute-start.26 = (f32[48,1152]{1,0:T(8,128)S(1)}, f32[48,1152]{1,0:T(8,128)S(1)}, u32[]{:S(2)}, u32[]{:S(2)}) collective-permute-start(f32[48,1152]{1,0:T(8,128)S(1)} %shard_map.81.refs_0_), channel_id=1, source_target_pairs={{0,1},{1,4},{4,5},{5,0},{2,3},{3,6},{6,7},{7,2},{8,9},{9,12},{12,1... | collective-permute-start | bytes 663560 | tf_op jit(solution)/shard_map/ppermute | solution.py:18
  93.0 10.7 %collective-permute-start.28 = (f32[48,1152]{1,0:T(8,128)S(1)}, f32[48,1152]{1,0:T(8,128)S(1)}, u32[]{:S(2)}, u32[]{:S(2)}) collective-permute-start(f32[48,1152]{1,0:T(8,128)S(1)} %shard_map.81.refs_0_), channel_id=1, source_target_pairs={{0,2},{2,0},{1,3},{3,1},{4,6},{6,4},{5,7},{7,5},{8,10},{10,8},{9,1... | collective-permute-start | bytes 663560 | tf_op jit(solution)/shard_map/ppermute | solution.py:22
  96.9 6.3 %collective-permute-start.25 = (f32[24,1152]{1,0:T(8,128)S(1)}, f32[24,1152]{1,0:T(8,128)S(1)}, u32[]{:S(2)}, u32[]{:S(2)}) collective-permute-start(f32[24,1152]{1,0:T(8,128)S(1)} %slice.8), channel_id=1, source_target_pairs={{0,5},{1,0},{4,1},{5,4},{2,7},{3,2},{6,3},{7,6},{8,13},{9,8},{12,9... | collective-permute-start | bytes 331784 | tf_op jit(solution)/shard_map/ppermute | solution.py:18
  97.2 5.9 %collective-permute-start.27 = (f32[24,1152]{1,0:T(8,128)S(1)}, f32[24,1152]{1,0:T(8,128)S(1)}, u32[]{:S(2)}, u32[]{:S(2)}) collective-permute-start(f32[24,1152]{1,0:T(8,128)S(1)} %slice.9), channel_id=1, source_target_pairs={{0,1},{1,4},{4,5},{5,0},{2,3},{3,6},{6,7},{7,2},{8,9},{9,12},{12,1... | collective-permute-start | bytes 331784 | tf_op jit(solution)/shard_map/ppermute | solution.py:18
  100.5 4.1 %collective-permute-start.29 = (f32[48,1152]{1,0:T(8,128)S(1)}, f32[48,1152]{1,0:T(8,128)S(1)}, u32[]{:S(2)}, u32[]{:S(2)}) collective-permute-start(f32[48,1152]{1,0:T(8,128)S(1)} %collective-permute-done.24.refs_1_), channel_id=1, source_target_pairs={{0,2},{2,0},{1,3},{3,1},{4,6},{6,4},{5,7},{7,5},{8,10},{10,8},{9,1... | collective-permute-start | bytes 663560 | tf_op jit(solution)/shard_map/ppermute | solution.py:22
  100.5 4.1 %collective-permute-start.32 = (f32[48,1152]{1,0:T(8,128)S(1)}, f32[48,1152]{1,0:T(8,128)S(1)}, u32[]{:S(2)}, u32[]{:S(2)}) collective-permute-start(f32[48,1152]{1,0:T(8,128)S(1)} %collective-permute-done.26.refs_4_), channel_id=1, source_target_pairs={{0,2},{2,0},{1,3},{3,1},{4,6},{6,4},{5,7},{7,5},{8,10},{10,8},{9,1... | collective-permute-start | bytes 663560 | tf_op jit(solution)/shard_map/ppermute | solution.py:22
  103.2 1.3 collective-permute-start.30
  103.2 1.5 collective-permute-start.31
  109.5 36.3 %copy-start.2 = (f32[125,500]{0,1:T(8,128)S(1)}, f32[125,500]{0,1:T(8,128)}, u32[]{:S(2)}) copy-start(f32[125,500]{0,1:T(8,128)} %param.8) | copy-start | bytes 750004
  109.5 42.6 %copy-start.4 = (f32[125,96]{0,1:T(8,128)S(1)}, f32[125,96]{0,1:T(8,128)}, u32[]{:S(2)}) copy-start(f32[125,96]{0,1:T(8,128)} %param.9) | copy-start | bytes 144004
  126.2 5.4 %collective-permute-start.33 = (f32[48,128]{1,0:T(8,128)S(1)}, f32[48,128]{1,0:T(8,128)S(1)}, u32[]{:S(2)}, u32[]{:S(2)}) collective-permute-start(f32[48,128]{1,0:T(8,128)S(1)} %reduce_sum.9), channel_id=1, source_target_pairs={{0,128},{64,192},{128,0},{192,64},{1,129},{65,193},{129,1},{193,65... | collective-permute-start | bytes 73736 | tf_op jit(solution)/shard_map/ppermute | solution.py:26
  126.3 5.3 %collective-permute-start.34 = (f32[48,128]{1,0:T(8,128)S(1)}, f32[48,128]{1,0:T(8,128)S(1)}, u32[]{:S(2)}, u32[]{:S(2)}) collective-permute-start(f32[48,128]{1,0:T(8,128)S(1)} %reduce_sum.9), channel_id=1, source_target_pairs={{0,64},{64,0},{128,192},{192,128},{1,65},{65,1},{129,193},{193,129... | collective-permute-start | bytes 73736 | tf_op jit(solution)/shard_map/ppermute | solution.py:26
  128.5 5.0 %collective-permute-start.35 = (f32[48,128]{1,0:T(8,128)S(1)}, f32[48,128]{1,0:T(8,128)S(1)}, u32[]{:S(2)}, u32[]{:S(2)}) collective-permute-start(f32[48,128]{1,0:T(8,128)S(1)} %reduce_sum.9), channel_id=1, source_target_pairs={{0,192},{64,128},{128,64},{192,0},{1,193},{65,129},{129,65},{193,1... | collective-permute-start | bytes 73736 | tf_op jit(solution)/shard_map/ppermute | solution.py:26
  146.0 1.3 collective-permute-start.36
  147.3 5.1 %collective-permute-start.37 = (f32[104,125]{1,0:T(8,128)S(1)}, f32[104,125]{1,0:T(8,128)S(1)}, u32[]{:S(2)}, u32[]{:S(2)}) collective-permute-start(f32[104,125]{1,0:T(8,128)S(1)} %add.15.a_ref), channel_id=1, source_target_pairs={{0,1},{1,0},{4,5},{5,4},{2,3},{3,2},{6,7},{7,6},{8,9},{9,8},{12,13... | collective-permute-start | bytes 156008 | tf_op jit(solution)/shard_map/ppermute | solution.py:26
  147.4 7.4 %collective-permute-start.38 = (f32[104,125]{1,0:T(8,128)S(1)}, f32[104,125]{1,0:T(8,128)S(1)}, u32[]{:S(2)}, u32[]{:S(2)}) collective-permute-start(f32[104,125]{1,0:T(8,128)S(1)} %add.15.a_ref), channel_id=1, source_target_pairs={{0,4},{1,5},{4,0},{5,1},{2,6},{3,7},{6,2},{7,3},{8,12},{9,13},{12,... | collective-permute-start | bytes 156008 | tf_op jit(solution)/shard_map/ppermute | solution.py:26
  151.8 5.3 %collective-permute-start.39 = (f32[104,125]{1,0:T(8,128)S(1)}, f32[104,125]{1,0:T(8,128)S(1)}, u32[]{:S(2)}, u32[]{:S(2)}) collective-permute-start(f32[104,125]{1,0:T(8,128)S(1)} %add.15.a_ref), channel_id=1, source_target_pairs={{0,5},{1,4},{4,1},{5,0},{2,7},{3,6},{6,3},{7,2},{8,13},{9,12},{12,... | collective-permute-start | bytes 156008 | tf_op jit(solution)/shard_map/ppermute | solution.py:26

commit v7 on v4

--- a/solution.py
+++ b/solution.py
@@ -44,28 +44,30 @@
 
 
 def pair_kernel(n_p, fresh, *refs):
-    p_head, p_rest = refs[-2:]
+    p_both = refs[-1]
     p_refs = refs[:n_p]
     if fresh:
-        r_refs, (kept_ref, sent_ref, r_head, r_rest) = refs[n_p:-6], refs[-6:-2]
+        r_refs, (kept_ref, sent_ref, r_head, r_rest) = refs[n_p:-5], refs[-5:-1]
         start = 0
         for ref in r_refs:
             rows = ref.shape[0]
             r_head[start : start + rows, :], r_rest[start : start + rows, :] = split(ref[...])
             start += rows
     else:
-        r_head, r_rest, kept_ref, sent_ref = refs[n_p:-2]
+        r_head, r_rest, kept_ref, sent_ref = refs[n_p:-1]
     _, _, x, core = position()
     half, n_cols = kept_ref.shape
     for k, ref in enumerate(p_refs):
         rows = ref.shape[0]
         start = ((k // NX) ^ core) * half + ((k % NX - x) & (NX - 1)) * rows
-        place = pl.ds(pl.multiple_of(start, 16), rows)
-        p_head[place, :], p_rest[place, :] = split(ref[...])
+        start = pl.multiple_of(start, 16)
+        p_both[pl.ds(start, rows), :], p_both[pl.ds(start + 2 * half, rows), :] = split(ref[...])
     for low in range(0, n_cols, 256):
         high = min(low + 256, n_cols)
-        pieces = (r_head[low:high, :], r_rest[low:high, :])
-        total = product((p_head[...], p_rest[...]), pieces, (((1,), (1,)), ((), ())))
+        dims = (((1,), (1,)), ((), ()))
+        both = lax.dot_general(p_both[...], r_head[low:high, :], dims, preferred_element_type=jnp.float32)
+        cross = lax.dot_general(p_both[: 2 * half], r_rest[low:high, :], dims, preferred_element_type=jnp.float32)
+        total = both[: 2 * half] + (both[2 * half :] + cross)
         kept_ref[:, low:high] = total[:half]
         sent_ref[:, low:high] = total[half:]
 
@@ -79,7 +81,7 @@
     return pl.pallas_call(
         functools.partial(pair_kernel, len(p_pieces), fresh),
         out_shape=(shape, shape) + ((parts, parts) if fresh else ()),
-        scratch_shapes=[pltpu.VMEM((n_rows, depth), jnp.bfloat16)] * 2,
+        scratch_shapes=[pltpu.VMEM((2 * n_rows, depth), jnp.bfloat16)],
         compiler_params=pltpu.CompilerParams(vmem_limit_bytes=16 * 2**20),
         cost_estimate=pl.CostEstimate(
             flops=1000 if fresh else 6 * n_rows * n_cols * depth,

time: 154 us -> 154 us (level)
  no operation moved by 1% of the time
where the time goes in v7:
time: 154 us
  starting transfers between devices  61.6 us (40%)
  waiting for transfers between devices  48.8 us (32%)
  blocking collectives  28.2 us (18%)
  Pallas kernels  12.2 us (8%)
  local copies, waits for them, and re-layouts  2.31 us (2%)
    ppermute x19, starting transfers between devices, shift(): lax.ppermute(value, axis, [(i, (i + step) % size) for i in range(size)])  33.7 us
    ppermute x19, waiting for transfers between devices, shift(): lax.ppermute(value, axis, [(i, (i + step) % size) for i in range(size)])  27.1 us
    ppermute x11, starting transfers between devices, swap(): return lax.ppermute(value, axis, [(i, i ^ mask) for i in range(size)])  18.3 us
    all_to_all x1, blocking collectives, on_device(): lax.all_to_all(tiles, 'z', split_axis=0, concat_axis=0, tiled=True)  16 us
    all_to_all x1, blocking collectives, on_device(): lax.all_to_all(jnp.broadcast_to(piece[None], tiles.shape), 'z', split_axi...  12.2 us
    ppermute x11, waiting for transfers between devices, swap(): return lax.ppermute(value, axis, [(i, i ^ mask) for i in range(size)])  11.4 us
    ppermute x2, starting transfers between devices, send_home(): return lax.ppermute(value, ('y', 'z', 'xh', 'co', 'xl'), pairs)  7.93 us
    ppermute x2, waiting for transfers between devices, send_home(): return lax.ppermute(value, ('y', 'z', 'xh', 'co', 'xl'), pairs)  5.99 us
  transfers between devices with their start and end apart: 40, of which 25 were waited for; matrix products, arithmetic and copies ran while one was open for 0% of the time, Pallas kernels for 2%

profile of v7, /device:TPU:6, one launch (start us, length us, event | category | flops | bytes accessed | tf_op | source)
XLA Modules:
  0.0 154.0 jit_solution(13672934171269969656)
XLA Ops:
  0.6 1.7 %collective-permute-start.7 = (f32[288,1152]{1,0:T(8,128)}, f32[288,1152]{1,0:T(8,128)S(1)}, u32[]{:S(2)}, u32[]{:S(2)}) collective-permute-start(f32[288,1152]{1,0:T(8,128)} %refs_8_.1), channel_id=1, source_target_pairs={{0,64},{64,0},{128,192},{192,128},{1,65},{65,1},{129,193},{193,129... | collective-permute-start | bytes 3981320 | tf_op jit(solution)/shard_map/ppermute | solution.py:26
  2.3 5.9 %collective-permute-start = (f32[48,1152]{1,0:T(8,128)}, f32[48,1152]{1,0:T(8,128)S(1)}, u32[]{:S(2)}, u32[]{:S(2)}) collective-permute-start(f32[48,1152]{1,0:T(8,128)} %refs_0_.1), channel_id=1, source_target_pairs={{0,56},{8,0},{16,8},{24,16},{32,24},{40,32},{48,40},{56,48},{1,57}... | collective-permute-start | bytes 663560 | tf_op jit(solution)/shard_map/ppermute | solution.py:18
  8.2 4.7 %collective-permute-done.refs_1_ = f32[48,1152]{1,0:T(8,128)S(1)} collective-permute-done((f32[48,1152]{1,0:T(8,128)}, f32[48,1152]{1,0:T(8,128)S(1)}, u32[]{:S(2)}, u32[]{:S(2)}) %collective-permute-start) | collective-permute-done | bytes 221216 | tf_op jit(solution)/shard_map/ppermute | solution.py:18
  12.9 3.6 %collective-permute-start.1 = (f32[48,1152]{1,0:T(8,128)S(1)}, f32[48,1152]{1,0:T(8,128)S(1)}, u32[]{:S(2)}, u32[]{:S(2)}) collective-permute-start(f32[48,1152]{1,0:T(8,128)S(1)} %collective-permute-done.refs_1_), channel_id=1, source_target_pairs={{0,56},{8,0},{16,8},{24,16},{32,24},{40,32},{48,40},{56,48},{1,57}... | collective-permute-start | bytes 663560 | tf_op jit(solution)/shard_map/ppermute | solution.py:18
  16.5 2.2 %collective-permute-start.9 = (f32[48,1152]{1,0:T(8,128)}, f32[48,1152]{1,0:T(8,128)S(1)}, u32[]{:S(2)}, u32[]{:S(2)}) collective-permute-start(f32[48,1152]{1,0:T(8,128)} %refs_0_.1), channel_id=1, source_target_pairs={{0,192},{64,128},{128,64},{192,0},{1,193},{65,129},{129,65},{193,1... | collective-permute-start | bytes 663560 | tf_op jit(solution)/shard_map/ppermute | solution.py:26
  18.6 1.3 collective-permute-done.1.refs_2_
  20.0 3.7 %collective-permute-start.2 = (f32[48,1152]{1,0:T(8,128)S(1)}, f32[48,1152]{1,0:T(8,128)S(1)}, u32[]{:S(2)}, u32[]{:S(2)}) collective-permute-start(f32[48,1152]{1,0:T(8,128)S(1)} %collective-permute-done.1.refs_2_), channel_id=1, source_target_pairs={{0,56},{8,0},{16,8},{24,16},{32,24},{40,32},{48,40},{56,48},{1,57}... | collective-permute-start | bytes 663560 | tf_op jit(solution)/shard_map/ppermute | solution.py:18
  23.9 2.0 %collective-permute-start.15 = (f32[48,1152]{1,0:T(8,128)S(1)}, f32[48,1152]{1,0:T(8,128)S(1)}, u32[]{:S(2)}, u32[]{:S(2)}) collective-permute-start(f32[48,1152]{1,0:T(8,128)S(1)} %collective-permute-done.9.refs_6_), channel_id=1, source_target_pairs={{0,8},{8,16},{16,24},{24,32},{32,40},{40,48},{48,56},{56,0},{1,9},... | collective-permute-start | bytes 663560 | tf_op jit(solution)/shard_map/ppermute | solution.py:18
  26.4 3.0 %collective-permute-done.2.refs_3_ = f32[48,1152]{1,0:T(8,128)S(1)} collective-permute-done((f32[48,1152]{1,0:T(8,128)S(1)}, f32[48,1152]{1,0:T(8,128)S(1)}, u32[]{:S(2)}, u32[]{:S(2)}) %collective-permute-start.2) | collective-permute-done | bytes 221216 | tf_op jit(solution)/shard_map/ppermute | solution.py:18
  29.4 3.7 %collective-permute-start.3 = (f32[48,1152]{1,0:T(8,128)S(1)}, f32[48,1152]{1,0:T(8,128)S(1)}, u32[]{:S(2)}, u32[]{:S(2)}) collective-permute-start(f32[48,1152]{1,0:T(8,128)S(1)} %collective-permute-done.2.refs_3_), channel_id=1, source_target_pairs={{0,56},{8,0},{16,8},{24,16},{32,24},{40,32},{48,40},{56,48},{1,57}... | collective-permute-start | bytes 663560 | tf_op jit(solution)/shard_map/ppermute | solution.py:18
  33.1 1.0 collective-permute-done.10.refs_7_
  34.1 3.7 %collective-permute-start.11 = (f32[48,1152]{1,0:T(8,128)S(1)}, f32[48,1152]{1,0:T(8,128)S(1)}, u32[]{:S(2)}, u32[]{:S(2)}) collective-permute-start(f32[48,1152]{1,0:T(8,128)S(1)} %collective-permute-done.10.refs_7_), channel_id=1, source_target_pairs={{0,56},{8,0},{16,8},{24,16},{32,24},{40,32},{48,40},{56,48},{1,57}... | collective-permute-start | bytes 663560 | tf_op jit(solution)/shard_map/ppermute | solution.py:18
  37.8 2.3 %collective-permute-start.12 = (f32[48,1152]{1,0:T(8,128)S(1)}, f32[48,1152]{1,0:T(8,128)S(1)}, u32[]{:S(2)}, u32[]{:S(2)}) collective-permute-start(f32[48,1152]{1,0:T(8,128)S(1)} %collective-permute-done.2.refs_3_), channel_id=1, source_target_pairs={{0,192},{64,128},{128,64},{192,0},{1,193},{65,129},{129,65},{193,1... | collective-permute-start | bytes 663560 | tf_op jit(solution)/shard_map/ppermute | solution.py:26
  40.1 1.1 collective-permute-start.14
  41.1 2.2 %collective-permute-start.13 = (f32[48,1152]{1,0:T(8,128)S(1)}, f32[48,1152]{1,0:T(8,128)S(1)}, u32[]{:S(2)}, u32[]{:S(2)}) collective-permute-start(f32[48,1152]{1,0:T(8,128)S(1)} %collective-permute-done.3.refs_4_), channel_id=1, source_target_pairs={{0,192},{64,128},{128,64},{192,0},{1,193},{65,129},{129,65},{193,1... | collective-permute-start | bytes 663560 | tf_op jit(solution)/shard_map/ppermute | solution.py:26
  43.3 1.3 copy-done.1
  44.7 0.9 copy-done.3
  45.6 2.8 %shard_map.76 = (f32[192,576]{1,0:T(8,128)S(1)}, f32[192,576]{1,0:T(8,128)S(1)}, bf16[576,1152]{1,0:T(8,128)(2,1)S(1)}, bf16[576,1152]{1,0:T(8,128)(2,1)S(1)}) custom-call(f32[48,1152]{1,0:T(8,128)S(1)} %copy-done.3, f32[48,1152]{1,0:T(8,128)S(1)} %collective-permute-done.refs_1_, f32[48,1152]{1,0:T(8,128)S(1)} %collective-permute-done.1.refs_2_, ...), custom_call_target="tpu_custom_call" | custom-call | flops 1000 | bytes 1000 | tf_op jit(solution)/shard_map/pallas_call | solution.py:81
  48.4 2.0 %collective-permute-done.13.refs_2_ = f32[48,1152]{1,0:T(8,128)S(1)} collective-permute-done((f32[48,1152]{1,0:T(8,128)S(1)}, f32[48,1152]{1,0:T(8,128)S(1)}, u32[]{:S(2)}, u32[]{:S(2)}) %collective-permute-start.13) | collective-permute-done | bytes 221216 | tf_op jit(solution)/shard_map/ppermute | solution.py:26
  50.5 2.8 %shard_map.77 = (f32[192,576]{1,0:T(8,128)S(1)}, f32[192,576]{1,0:T(8,128)S(1)}) custom-call(f32[48,1152]{1,0:T(8,128)S(1)} %collective-permute-done.11.refs_0_, f32[48,1152]{1,0:T(8,128)S(1)} %collective-permute-done.12.refs_1_, f32[48,1152]{1,0:T(8,128)S(1)} %collective-permute-done.13.refs_2_, f32[48,1152]{1,0:T(8,128)S(1)} %collective-permute-done.14.refs_3_, ...), custom_call_target="tpu_custom_call" | custom-call | flops 1528823808 | bytes 4423680 | tf_op jit(solution)/shard_map/pallas_call | solution.py:81
  53.9 1.4 collective-permute-done.17.refs_3_
  56.7 1.6 %collective-permute-start.19 = (f32[24,1152]{1,0:T(8,128)S(1)}, f32[24,1152]{1,0:T(8,128)S(1)}, u32[]{:S(2)}, u32[]{:S(2)}) collective-permute-start(f32[24,1152]{1,0:T(8,128)S(1)} %get-tuple-element.33), channel_id=1, source_target_pairs={{0,5},{1,0},{4,1},{5,4},{2,7},{3,2},{6,3},{7,6},{8,13},{9,8},{12,9... | collective-permute-start | bytes 331784 | tf_op jit(solution)/shard_map/ppermute | solution.py:18
  58.2 3.1 %collective-permute-done.18.up_ref = f32[24,1152]{1,0:T(8,128)S(1)} collective-permute-done((f32[24,1152]{1,0:T(8,128)S(1)}, f32[24,1152]{1,0:T(8,128)S(1)}, u32[]{:S(2)}, u32[]{:S(2)}) %collective-permute-start.18) | collective-permute-done | bytes 110624 | tf_op jit(solution)/shard_map/ppermute | solution.py:18
  61.3 1.4 collective-permute-done.19.down_ref
  63.1 1.7 %collective-permute-start.21 = (f32[48,1152]{1,0:T(8,128)S(1)}, f32[48,1152]{1,0:T(8,128)S(1)}, u32[]{:S(2)}, u32[]{:S(2)}) collective-permute-start(f32[48,1152]{1,0:T(8,128)S(1)} %get-tuple-element.35), channel_id=1, source_target_pairs={{0,5},{1,0},{4,1},{5,4},{2,7},{3,2},{6,3},{7,6},{8,13},{9,8},{12,9... | collective-permute-start | bytes 663560 | tf_op jit(solution)/shard_map/ppermute | solution.py:18
  64.8 4.3 %collective-permute-done.20.one_ref = f32[48,1152]{1,0:T(8,128)S(1)} collective-permute-done((f32[48,1152]{1,0:T(8,128)S(1)}, f32[48,1152]{1,0:T(8,128)S(1)}, u32[]{:S(2)}, u32[]{:S(2)}) %collective-permute-start.20) | collective-permute-done | bytes 221216 | tf_op jit(solution)/shard_map/ppermute | solution.py:18
  69.1 1.5 collective-permute-done.21.two_ref
  70.8 3.6 %collective-permute-start.22 = (f32[48,576]{1,0:T(8,128)S(1)}, f32[48,576]{1,0:T(8,128)S(1)}, u32[]{:S(2)}, u32[]{:S(2)}) collective-permute-start(f32[48,576]{1,0:T(8,128)S(1)} %get-tuple-element.36), channel_id=1, source_target_pairs={{0,0},{2,34},{1,9},{3,43},{4,20},{6,54},{5,29},{7,63},{8,8},{10,42... | collective-permute-start | bytes 331784 | tf_op jit(solution)/shard_map/ppermute | solution.py:288
  74.5 4.3 %collective-permute-start.23 = (f32[48,576]{1,0:T(8,128)S(1)}, f32[48,576]{1,0:T(8,128)S(1)}, u32[]{:S(2)}, u32[]{:S(2)}) collective-permute-start(f32[48,576]{1,0:T(8,128)S(1)} %get-tuple-element.37), channel_id=1, source_target_pairs={{0,208},{2,242},{1,217},{3,251},{4,228},{6,198},{5,237},{7,207},{8... | collective-permute-start | bytes 331784 | tf_op jit(solution)/shard_map/ppermute | solution.py:288
  78.7 3.6 %collective-permute-done.22.first_ref = f32[48,576]{1,0:T(8,128)S(1)} collective-permute-done((f32[48,576]{1,0:T(8,128)S(1)}, f32[48,576]{1,0:T(8,128)S(1)}, u32[]{:S(2)}, u32[]{:S(2)}) %collective-permute-start.22) | collective-permute-done | bytes 110624 | tf_op jit(solution)/shard_map/ppermute | solution.py:288
  82.3 2.4 %collective-permute-done.23.second_ref = f32[48,576]{1,0:T(8,128)S(1)} collective-permute-done((f32[48,576]{1,0:T(8,128)S(1)}, f32[48,576]{1,0:T(8,128)S(1)}, u32[]{:S(2)}, u32[]{:S(2)}) %collective-permute-start.23) | collective-permute-done | bytes 110624 | tf_op jit(solution)/shard_map/ppermute | solution.py:288
  84.9 3.2 %collective-permute-start.26 = (f32[48,1152]{1,0:T(8,128)S(1)}, f32[48,1152]{1,0:T(8,128)S(1)}, u32[]{:S(2)}, u32[]{:S(2)}) collective-permute-start(f32[48,1152]{1,0:T(8,128)S(1)} %shard_map.81.refs_0_), channel_id=1, source_target_pairs={{0,1},{1,4},{4,5},{5,0},{2,3},{3,6},{6,7},{7,2},{8,9},{9,12},{12,1... | collective-permute-start | bytes 663560 | tf_op jit(solution)/shard_map/ppermute | solution.py:18
  88.2 4.1 %collective-permute-done.24.refs_1_ = f32[48,1152]{1,0:T(8,128)S(1)} collective-permute-done((f32[48,1152]{1,0:T(8,128)S(1)}, f32[48,1152]{1,0:T(8,128)S(1)}, u32[]{:S(2)}, u32[]{:S(2)}) %collective-permute-start.24) | collective-permute-done | bytes 221216 | tf_op jit(solution)/shard_map/ppermute | solution.py:18
  92.6 3.3 %collective-permute-start.27 = (f32[24,1152]{1,0:T(8,128)S(1)}, f32[24,1152]{1,0:T(8,128)S(1)}, u32[]{:S(2)}, u32[]{:S(2)}) collective-permute-start(f32[24,1152]{1,0:T(8,128)S(1)} %slice.9), channel_id=1, source_target_pairs={{0,1},{1,4},{4,5},{5,0},{2,3},{3,6},{6,7},{7,2},{8,9},{9,12},{12,1... | collective-permute-start | bytes 331784 | tf_op jit(solution)/shard_map/ppermute | solution.py:18
  96.4 2.1 %collective-permute-done.25.refs_2_ = f32[24,1152]{1,0:T(8,128)S(1)} collective-permute-done((f32[24,1152]{1,0:T(8,128)S(1)}, f32[24,1152]{1,0:T(8,128)S(1)}, u32[]{:S(2)}, u32[]{:S(2)}) %collective-permute-start.25) | collective-permute-done | bytes 110624 | tf_op jit(solution)/shard_map/ppermute | solution.py:18
  99.0 0.8 collective-permute-done.30.refs_7_
  100.0 4.8 %shard_map.82 = f32[8,48,128]{2,1,0:T(8,128)S(1)} custom-call(f32[48,1152]{1,0:T(8,128)S(1)} %shard_map.81.refs_0_, f32[48,1152]{1,0:T(8,128)S(1)} %collective-permute-done.24.refs_1_, f32[24,1152]{1,0:T(8,128)S(1)} %collective-permute-done.25.refs_2_, f32[24,1152]{1,0:T(8,128)S(1)} %collective-permute-done.27.refs_3_, ...), custom_call_target="tpu_custom_call" | custom-call | tf_op jit(solution)/shard_map/pallas_call | solution.py:198
  104.8 16.0 %all_to_all.10 = f32[8,48,128]{2,1,0:T(8,128)S(1)} all-to-all(f32[8,48,128]{2,1,0:T(8,128)S(1)} %shard_map.82), channel_id=1, replica_groups=mesh['y'=4,'z'=8,'xh'=2,'co'=2,'xl'=2] {'z'}, dimensions={0} | all-to-all | bytes 393216 | tf_op jit(solution)/shard_map/all_to_all | solution.py:305
  120.9 0.7 collective-permute-start.33
  121.6 2.9 %collective-permute-start.34 = (f32[48,128]{1,0:T(8,128)S(1)}, f32[48,128]{1,0:T(8,128)S(1)}, u32[]{:S(2)}, u32[]{:S(2)}) collective-permute-start(f32[48,128]{1,0:T(8,128)S(1)} %reduce_sum.9), channel_id=1, source_target_pairs={{0,64},{64,0},{128,192},{192,128},{1,65},{65,1},{129,193},{193,129... | collective-permute-start | bytes 73736 | tf_op jit(solution)/shard_map/ppermute | solution.py:26
  125.0 1.2 collective-permute-done.33
  126.5 3.0 %collective-permute-done.35 = f32[48,128]{1,0:T(8,128)S(1)} collective-permute-done((f32[48,128]{1,0:T(8,128)S(1)}, f32[48,128]{1,0:T(8,128)S(1)}, u32[]{:S(2)}, u32[]{:S(2)}) %collective-permute-start.35) | collective-permute-done | bytes 24608 | tf_op jit(solution)/shard_map/ppermute | solution.py:26
  129.5 12.2 %all_to_all.11.tiles_ref = f32[8,48,128]{2,1,0:T(8,128)S(1)} all-to-all(f32[8,48,128]{2,1,0:T(8,128)S(1)} %broadcast_in_dim.2), channel_id=1, replica_groups=mesh['y'=4,'z'=8,'xh'=2,'co'=2,'xl'=2] {'z'}, dimensions={0} | all-to-all | bytes 393216 | tf_op jit(solution)/shard_map/all_to_all | solution.py:307
  142.0 1.2 collective-permute-done.36
  143.4 4.4 %collective-permute-start.38 = (f32[104,125]{1,0:T(8,128)S(1)}, f32[104,125]{1,0:T(8,128)S(1)}, u32[]{:S(2)}, u32[]{:S(2)}) collective-permute-start(f32[104,125]{1,0:T(8,128)S(1)} %add.15.a_ref), channel_id=1, source_target_pairs={{0,4},{1,5},{4,0},{5,1},{2,6},{3,7},{6,2},{7,3},{8,12},{9,13},{12,... | collective-permute-start | bytes 156008 | tf_op jit(solution)/shard_map/ppermute | solution.py:26
  148.4 2.3 %collective-permute-done.38.c_ref = f32[104,125]{1,0:T(8,128)S(1)} collective-permute-done((f32[104,125]{1,0:T(8,128)S(1)}, f32[104,125]{1,0:T(8,128)S(1)}, u32[]{:S(2)}, u32[]{:S(2)}) %collective-permute-start.38) | collective-permute-done | bytes 52032 | tf_op jit(solution)/shard_map/ppermute | solution.py:26
  150.8 2.4 %collective-permute-done.39.d_ref = f32[104,125]{1,0:T(8,128)S(1)} collective-permute-done((f32[104,125]{1,0:T(8,128)S(1)}, f32[104,125]{1,0:T(8,128)S(1)}, u32[]{:S(2)}, u32[]{:S(2)}) %collective-permute-start.39) | collective-permute-done | bytes 52032 | tf_op jit(solution)/shard_map/ppermute | solution.py:26
  153.1 0.8 shard_map.85
  (60 shorter events, 7.0 us)
Async XLA Ops:
  0.6 40.5 %collective-permute-start.7 = (f32[288,1152]{1,0:T(8,128)}, f32[288,1152]{1,0:T(8,128)S(1)}, u32[]{:S(2)}, u32[]{:S(2)}) collective-permute-start(f32[288,1152]{1,0:T(8,128)} %refs_8_.1), channel_id=1, source_target_pairs={{0,64},{64,0},{128,192},{192,128},{1,65},{65,1},{129,193},{193,129... | collective-permute-start | bytes 3981320 | tf_op jit(solution)/shard_map/ppermute | solution.py:26
  2.3 10.6 %collective-permute-start = (f32[48,1152]{1,0:T(8,128)}, f32[48,1152]{1,0:T(8,128)S(1)}, u32[]{:S(2)}, u32[]{:S(2)}) collective-permute-start(f32[48,1152]{1,0:T(8,128)} %refs_0_.1), channel_id=1, source_target_pairs={{0,56},{8,0},{16,8},{24,16},{32,24},{40,32},{48,40},{56,48},{1,57}... | collective-permute-start | bytes 663560 | tf_op jit(solution)/shard_map/ppermute | solution.py:18
  8.1 10.5 %collective-permute-start.4 = (f32[48,1152]{1,0:T(8,128)}, f32[48,1152]{1,0:T(8,128)S(1)}, u32[]{:S(2)}, u32[]{:S(2)}) collective-permute-start(f32[48,1152]{1,0:T(8,128)} %refs_0_.1), channel_id=1, source_target_pairs={{0,8},{8,16},{16,24},{24,32},{32,40},{40,48},{48,56},{56,0},{1,9},... | collective-permute-start | bytes 663560 | tf_op jit(solution)/shard_map/ppermute | solution.py:18
  12.9 7.1 %collective-permute-start.1 = (f32[48,1152]{1,0:T(8,128)S(1)}, f32[48,1152]{1,0:T(8,128)S(1)}, u32[]{:S(2)}, u32[]{:S(2)}) collective-permute-start(f32[48,1152]{1,0:T(8,128)S(1)} %collective-permute-done.refs_1_), channel_id=1, source_target_pairs={{0,56},{8,0},{16,8},{24,16},{32,24},{40,32},{48,40},{56,48},{1,57}... | collective-permute-start | bytes 663560 | tf_op jit(solution)/shard_map/ppermute | solution.py:18
  16.5 7.4 %collective-permute-start.9 = (f32[48,1152]{1,0:T(8,128)}, f32[48,1152]{1,0:T(8,128)S(1)}, u32[]{:S(2)}, u32[]{:S(2)}) collective-permute-start(f32[48,1152]{1,0:T(8,128)} %refs_0_.1), channel_id=1, source_target_pairs={{0,192},{64,128},{128,64},{192,0},{1,193},{65,129},{129,65},{193,1... | collective-permute-start | bytes 663560 | tf_op jit(solution)/shard_map/ppermute | solution.py:26
  18.6 7.7 %collective-permute-start.5 = (f32[48,1152]{1,0:T(8,128)S(1)}, f32[48,1152]{1,0:T(8,128)S(1)}, u32[]{:S(2)}, u32[]{:S(2)}) collective-permute-start(f32[48,1152]{1,0:T(8,128)S(1)} %collective-permute-done.4.refs_7_), channel_id=1, source_target_pairs={{0,8},{8,16},{16,24},{24,32},{32,40},{40,48},{48,56},{56,0},{1,9},... | collective-permute-start | bytes 663560 | tf_op jit(solution)/shard_map/ppermute | solution.py:18
  20.0 9.4 %collective-permute-start.2 = (f32[48,1152]{1,0:T(8,128)S(1)}, f32[48,1152]{1,0:T(8,128)S(1)}, u32[]{:S(2)}, u32[]{:S(2)}) collective-permute-start(f32[48,1152]{1,0:T(8,128)S(1)} %collective-permute-done.1.refs_2_), channel_id=1, source_target_pairs={{0,56},{8,0},{16,8},{24,16},{32,24},{40,32},{48,40},{56,48},{1,57}... | collective-permute-start | bytes 663560 | tf_op jit(solution)/shard_map/ppermute | solution.py:18
  23.8 10.3 %collective-permute-start.10 = (f32[48,1152]{1,0:T(8,128)S(1)}, f32[48,1152]{1,0:T(8,128)S(1)}, u32[]{:S(2)}, u32[]{:S(2)}) collective-permute-start(f32[48,1152]{1,0:T(8,128)S(1)} %collective-permute-done.9.refs_6_), channel_id=1, source_target_pairs={{0,56},{8,0},{16,8},{24,16},{32,24},{40,32},{48,40},{56,48},{1,57}... | collective-permute-start | bytes 663560 | tf_op jit(solution)/shard_map/ppermute | solution.py:18
  23.9 13.9 %collective-permute-start.15 = (f32[48,1152]{1,0:T(8,128)S(1)}, f32[48,1152]{1,0:T(8,128)S(1)}, u32[]{:S(2)}, u32[]{:S(2)}) collective-permute-start(f32[48,1152]{1,0:T(8,128)S(1)} %collective-permute-done.9.refs_6_), channel_id=1, source_target_pairs={{0,8},{8,16},{16,24},{24,32},{32,40},{40,48},{48,56},{56,0},{1,9},... | collective-permute-start | bytes 663560 | tf_op jit(solution)/shard_map/ppermute | solution.py:18
  26.4 11.4 %collective-permute-start.6 = (f32[48,1152]{1,0:T(8,128)S(1)}, f32[48,1152]{1,0:T(8,128)S(1)}, u32[]{:S(2)}, u32[]{:S(2)}) collective-permute-start(f32[48,1152]{1,0:T(8,128)S(1)} %collective-permute-done.5.refs_6_), channel_id=1, source_target_pairs={{0,8},{8,16},{16,24},{24,32},{32,40},{40,48},{48,56},{56,0},{1,9},... | collective-permute-start | bytes 663560 | tf_op jit(solution)/shard_map/ppermute | solution.py:18
  29.4 10.7 %collective-permute-start.3 = (f32[48,1152]{1,0:T(8,128)S(1)}, f32[48,1152]{1,0:T(8,128)S(1)}, u32[]{:S(2)}, u32[]{:S(2)}) collective-permute-start(f32[48,1152]{1,0:T(8,128)S(1)} %collective-permute-done.2.refs_3_), channel_id=1, source_target_pairs={{0,56},{8,0},{16,8},{24,16},{32,24},{40,32},{48,40},{56,48},{1,57}... | collective-permute-start | bytes 663560 | tf_op jit(solution)/shard_map/ppermute | solution.py:18
  34.1 14.3 %collective-permute-start.11 = (f32[48,1152]{1,0:T(8,128)S(1)}, f32[48,1152]{1,0:T(8,128)S(1)}, u32[]{:S(2)}, u32[]{:S(2)}) collective-permute-start(f32[48,1152]{1,0:T(8,128)S(1)} %collective-permute-done.10.refs_7_), channel_id=1, source_target_pairs={{0,56},{8,0},{16,8},{24,16},{32,24},{40,32},{48,40},{56,48},{1,57}... | collective-permute-start | bytes 663560 | tf_op jit(solution)/shard_map/ppermute | solution.py:18
  37.8 10.6 %collective-permute-start.16 = (f32[48,1152]{1,0:T(8,128)S(1)}, f32[48,1152]{1,0:T(8,128)S(1)}, u32[]{:S(2)}, u32[]{:S(2)}) collective-permute-start(f32[48,1152]{1,0:T(8,128)S(1)} %collective-permute-done.15.refs_5_), channel_id=1, source_target_pairs={{0,8},{8,16},{16,24},{24,32},{32,40},{40,48},{48,56},{56,0},{1,9},... | collective-permute-start | bytes 663560 | tf_op jit(solution)/shard_map/ppermute | solution.py:18
  37.8 10.6 %collective-permute-start.12 = (f32[48,1152]{1,0:T(8,128)S(1)}, f32[48,1152]{1,0:T(8,128)S(1)}, u32[]{:S(2)}, u32[]{:S(2)}) collective-permute-start(f32[48,1152]{1,0:T(8,128)S(1)} %collective-permute-done.2.refs_3_), channel_id=1, source_target_pairs={{0,192},{64,128},{128,64},{192,0},{1,193},{65,129},{129,65},{193,1... | collective-permute-start | bytes 663560 | tf_op jit(solution)/shard_map/ppermute | solution.py:26
  40.1 8.3 %collective-permute-start.14 = (f32[48,1152]{1,0:T(8,128)S(1)}, f32[48,1152]{1,0:T(8,128)S(1)}, u32[]{:S(2)}, u32[]{:S(2)}) collective-permute-start(f32[48,1152]{1,0:T(8,128)S(1)} %collective-permute-done.6.refs_5_), channel_id=1, source_target_pairs={{0,192},{64,128},{128,64},{192,0},{1,193},{65,129},{129,65},{193,1... | collective-permute-start | bytes 663560 | tf_op jit(solution)/shard_map/ppermute | solution.py:26
  41.1 9.3 %collective-permute-start.13 = (f32[48,1152]{1,0:T(8,128)S(1)}, f32[48,1152]{1,0:T(8,128)S(1)}, u32[]{:S(2)}, u32[]{:S(2)}) collective-permute-start(f32[48,1152]{1,0:T(8,128)S(1)} %collective-permute-done.3.refs_4_), channel_id=1, source_target_pairs={{0,192},{64,128},{128,64},{192,0},{1,193},{65,129},{129,65},{193,1... | collective-permute-start | bytes 663560 | tf_op jit(solution)/shard_map/ppermute | solution.py:26
  43.3 1.3 copy-start.1
  44.6 0.9 copy-start.3
  50.5 49.5 %copy-start = (f32[48,96,500]{2,1,0:T(8,128)S(1)}, f32[48,96,500]{2,1,0:T(8,128)}, u32[]{:S(2)}) copy-start(f32[48,96,500]{2,1,0:T(8,128)} %refs_10_.1) | copy-start | bytes 27648004
  53.3 2.0 %collective-permute-start.17 = (f32[192,576]{1,0:T(8,128)S(1)}, f32[192,576]{1,0:T(8,128)S(1)}, u32[]{:S(2)}, u32[]{:S(2)}) collective-permute-start(f32[192,576]{1,0:T(8,128)S(1)} %get-tuple-element.28), channel_id=1, source_target_pairs={{0,2},{2,0},{1,3},{3,1},{4,6},{6,4},{5,7},{7,5},{8,10},{10,8},{9,1... | collective-permute-start | bytes 1327112 | tf_op jit(solution)/shard_map/ppermute | solution.py:22
  53.4 2.6 %collective-permute-start.8 = (f32[192,576]{1,0:T(8,128)S(1)}, f32[192,576]{1,0:T(8,128)S(1)}, u32[]{:S(2)}, u32[]{:S(2)}) collective-permute-start(f32[192,576]{1,0:T(8,128)S(1)} %get-tuple-element.24), channel_id=1, source_target_pairs={{0,2},{2,0},{1,3},{3,1},{4,6},{6,4},{5,7},{7,5},{8,10},{10,8},{9,1... | collective-permute-start | bytes 1327112 | tf_op jit(solution)/shard_map/ppermute | solution.py:22
  56.1 5.2 %collective-permute-start.18 = (f32[24,1152]{1,0:T(8,128)S(1)}, f32[24,1152]{1,0:T(8,128)S(1)}, u32[]{:S(2)}, u32[]{:S(2)}) collective-permute-start(f32[24,1152]{1,0:T(8,128)S(1)} %get-tuple-element.31), channel_id=1, source_target_pairs={{0,1},{1,4},{4,5},{5,0},{2,3},{3,6},{6,7},{7,2},{8,9},{9,12},{12,1... | collective-permute-start | bytes 331784 | tf_op jit(solution)/shard_map/ppermute | solution.py:18
  56.7 6.0 %collective-permute-start.19 = (f32[24,1152]{1,0:T(8,128)S(1)}, f32[24,1152]{1,0:T(8,128)S(1)}, u32[]{:S(2)}, u32[]{:S(2)}) collective-permute-start(f32[24,1152]{1,0:T(8,128)S(1)} %get-tuple-element.33), channel_id=1, source_target_pairs={{0,5},{1,0},{4,1},{5,4},{2,7},{3,2},{6,3},{7,6},{8,13},{9,8},{12,9... | collective-permute-start | bytes 331784 | tf_op jit(solution)/shard_map/ppermute | solution.py:18
  62.7 6.4 %collective-permute-start.20 = (f32[48,1152]{1,0:T(8,128)S(1)}, f32[48,1152]{1,0:T(8,128)S(1)}, u32[]{:S(2)}, u32[]{:S(2)}) collective-permute-start(f32[48,1152]{1,0:T(8,128)S(1)} %get-tuple-element.34), channel_id=1, source_target_pairs={{0,1},{1,4},{4,5},{5,0},{2,3},{3,6},{6,7},{7,2},{8,9},{9,12},{12,1... | collective-permute-start | bytes 663560 | tf_op jit(solution)/shard_map/ppermute | solution.py:18
  63.1 7.6 %collective-permute-start.21 = (f32[48,1152]{1,0:T(8,128)S(1)}, f32[48,1152]{1,0:T(8,128)S(1)}, u32[]{:S(2)}, u32[]{:S(2)}) collective-permute-start(f32[48,1152]{1,0:T(8,128)S(1)} %get-tuple-element.35), channel_id=1, source_target_pairs={{0,5},{1,0},{4,1},{5,4},{2,7},{3,2},{6,3},{7,6},{8,13},{9,8},{12,9... | collective-permute-start | bytes 663560 | tf_op jit(solution)/shard_map/ppermute | solution.py:18
  70.8 11.5 %collective-permute-start.22 = (f32[48,576]{1,0:T(8,128)S(1)}, f32[48,576]{1,0:T(8,128)S(1)}, u32[]{:S(2)}, u32[]{:S(2)}) collective-permute-start(f32[48,576]{1,0:T(8,128)S(1)} %get-tuple-element.36), channel_id=1, source_target_pairs={{0,0},{2,34},{1,9},{3,43},{4,20},{6,54},{5,29},{7,63},{8,8},{10,42... | collective-permute-start | bytes 331784 | tf_op jit(solution)/shard_map/ppermute | solution.py:288
  74.5 10.3 %collective-permute-start.23 = (f32[48,576]{1,0:T(8,128)S(1)}, f32[48,576]{1,0:T(8,128)S(1)}, u32[]{:S(2)}, u32[]{:S(2)}) collective-permute-start(f32[48,576]{1,0:T(8,128)S(1)} %get-tuple-element.37), channel_id=1, source_target_pairs={{0,208},{2,242},{1,217},{3,251},{4,228},{6,198},{5,237},{7,207},{8... | collective-permute-start | bytes 331784 | tf_op jit(solution)/shard_map/ppermute | solution.py:288
  84.8 7.4 %collective-permute-start.24 = (f32[48,1152]{1,0:T(8,128)S(1)}, f32[48,1152]{1,0:T(8,128)S(1)}, u32[]{:S(2)}, u32[]{:S(2)}) collective-permute-start(f32[48,1152]{1,0:T(8,128)S(1)} %shard_map.81.refs_0_), channel_id=1, source_target_pairs={{0,5},{1,0},{4,1},{5,4},{2,7},{3,2},{6,3},{7,6},{8,13},{9,8},{12,9... | collective-permute-start | bytes 663560 | tf_op jit(solution)/shard_map/ppermute | solution.py:18
  84.9 7.7 %collective-permute-start.26 = (f32[48,1152]{1,0:T(8,128)S(1)}, f32[48,1152]{1,0:T(8,128)S(1)}, u32[]{:S(2)}, u32[]{:S(2)}) collective-permute-start(f32[48,1152]{1,0:T(8,128)S(1)} %shard_map.81.refs_0_), channel_id=1, source_target_pairs={{0,1},{1,4},{4,5},{5,0},{2,3},{3,6},{6,7},{7,2},{8,9},{9,12},{12,1... | collective-permute-start | bytes 663560 | tf_op jit(solution)/shard_map/ppermute | solution.py:18
  88.1 10.9 %collective-permute-start.28 = (f32[48,1152]{1,0:T(8,128)S(1)}, f32[48,1152]{1,0:T(8,128)S(1)}, u32[]{:S(2)}, u32[]{:S(2)}) collective-permute-start(f32[48,1152]{1,0:T(8,128)S(1)} %shard_map.81.refs_0_), channel_id=1, source_target_pairs={{0,2},{2,0},{1,3},{3,1},{4,6},{6,4},{5,7},{7,5},{8,10},{10,8},{9,1... | collective-permute-start | bytes 663560 | tf_op jit(solution)/shard_map/ppermute | solution.py:22
  92.3 6.3 %collective-permute-start.25 = (f32[24,1152]{1,0:T(8,128)S(1)}, f32[24,1152]{1,0:T(8,128)S(1)}, u32[]{:S(2)}, u32[]{:S(2)}) collective-permute-start(f32[24,1152]{1,0:T(8,128)S(1)} %slice.8), channel_id=1, source_target_pairs={{0,5},{1,0},{4,1},{5,4},{2,7},{3,2},{6,3},{7,6},{8,13},{9,8},{12,9... | collective-permute-start | bytes 331784 | tf_op jit(solution)/shard_map/ppermute | solution.py:18
  92.6 5.9 %collective-permute-start.27 = (f32[24,1152]{1,0:T(8,128)S(1)}, f32[24,1152]{1,0:T(8,128)S(1)}, u32[]{:S(2)}, u32[]{:S(2)}) collective-permute-start(f32[24,1152]{1,0:T(8,128)S(1)} %slice.9), channel_id=1, source_target_pairs={{0,1},{1,4},{4,5},{5,0},{2,3},{3,6},{6,7},{7,2},{8,9},{9,12},{12,1... | collective-permute-start | bytes 331784 | tf_op jit(solution)/shard_map/ppermute | solution.py:18
  95.9 4.1 %collective-permute-start.29 = (f32[48,1152]{1,0:T(8,128)S(1)}, f32[48,1152]{1,0:T(8,128)S(1)}, u32[]{:S(2)}, u32[]{:S(2)}) collective-permute-start(f32[48,1152]{1,0:T(8,128)S(1)} %collective-permute-done.24.refs_1_), channel_id=1, source_target_pairs={{0,2},{2,0},{1,3},{3,1},{4,6},{6,4},{5,7},{7,5},{8,10},{10,8},{9,1... | collective-permute-start | bytes 663560 | tf_op jit(solution)/shard_map/ppermute | solution.py:22
  95.9 4.1 %collective-permute-start.32 = (f32[48,1152]{1,0:T(8,128)S(1)}, f32[48,1152]{1,0:T(8,128)S(1)}, u32[]{:S(2)}, u32[]{:S(2)}) collective-permute-start(f32[48,1152]{1,0:T(8,128)S(1)} %collective-permute-done.26.refs_4_), channel_id=1, source_target_pairs={{0,2},{2,0},{1,3},{3,1},{4,6},{6,4},{5,7},{7,5},{8,10},{10,8},{9,1... | collective-permute-start | bytes 663560 | tf_op jit(solution)/shard_map/ppermute | solution.py:22
  98.5 1.3 collective-permute-start.30
  98.5 1.5 collective-permute-start.31
  104.8 36.9 %copy-start.2 = (f32[125,500]{0,1:T(8,128)S(1)}, f32[125,500]{0,1:T(8,128)}, u32[]{:S(2)}) copy-start(f32[125,500]{0,1:T(8,128)} %param.8) | copy-start | bytes 750004
  104.8 43.2 %copy-start.4 = (f32[125,96]{0,1:T(8,128)S(1)}, f32[125,96]{0,1:T(8,128)}, u32[]{:S(2)}) copy-start(f32[125,96]{0,1:T(8,128)} %param.9) | copy-start | bytes 144004
  120.9 5.4 %collective-permute-start.33 = (f32[48,128]{1,0:T(8,128)S(1)}, f32[48,128]{1,0:T(8,128)S(1)}, u32[]{:S(2)}, u32[]{:S(2)}) collective-permute-start(f32[48,128]{1,0:T(8,128)S(1)} %reduce_sum.9), channel_id=1, source_target_pairs={{0,128},{64,192},{128,0},{192,64},{1,129},{65,193},{129,1},{193,65... | collective-permute-start | bytes 73736 | tf_op jit(solution)/shard_map/ppermute | solution.py:26
  121.6 4.9 %collective-permute-start.34 = (f32[48,128]{1,0:T(8,128)S(1)}, f32[48,128]{1,0:T(8,128)S(1)}, u32[]{:S(2)}, u32[]{:S(2)}) collective-permute-start(f32[48,128]{1,0:T(8,128)S(1)} %reduce_sum.9), channel_id=1, source_target_pairs={{0,64},{64,0},{128,192},{192,128},{1,65},{65,1},{129,193},{193,129... | collective-permute-start | bytes 73736 | tf_op jit(solution)/shard_map/ppermute | solution.py:26
  124.5 5.0 %collective-permute-start.35 = (f32[48,128]{1,0:T(8,128)S(1)}, f32[48,128]{1,0:T(8,128)S(1)}, u32[]{:S(2)}, u32[]{:S(2)}) collective-permute-start(f32[48,128]{1,0:T(8,128)S(1)} %reduce_sum.9), channel_id=1, source_target_pairs={{0,192},{64,128},{128,64},{192,0},{1,193},{65,129},{129,65},{193,1... | collective-permute-start | bytes 73736 | tf_op jit(solution)/shard_map/ppermute | solution.py:26
  141.9 1.3 collective-permute-start.36
  143.3 5.1 %collective-permute-start.37 = (f32[104,125]{1,0:T(8,128)S(1)}, f32[104,125]{1,0:T(8,128)S(1)}, u32[]{:S(2)}, u32[]{:S(2)}) collective-permute-start(f32[104,125]{1,0:T(8,128)S(1)} %add.15.a_ref), channel_id=1, source_target_pairs={{0,1},{1,0},{4,5},{5,4},{2,3},{3,2},{6,7},{7,6},{8,9},{9,8},{12,13... | collective-permute-start | bytes 156008 | tf_op jit(solution)/shard_map/ppermute | solution.py:26
  143.4 7.4 %collective-permute-start.38 = (f32[104,125]{1,0:T(8,128)S(1)}, f32[104,125]{1,0:T(8,128)S(1)}, u32[]{:S(2)}, u32[]{:S(2)}) collective-permute-start(f32[104,125]{1,0:T(8,128)S(1)} %add.15.a_ref), channel_id=1, source_target_pairs={{0,4},{1,5},{4,0},{5,1},{2,6},{3,7},{6,2},{7,3},{8,12},{9,13},{12,... | collective-permute-start | bytes 156008 | tf_op jit(solution)/shard_map/ppermute | solution.py:26
  147.8 5.3 %collective-permute-start.39 = (f32[104,125]{1,0:T(8,128)S(1)}, f32[104,125]{1,0:T(8,128)S(1)}, u32[]{:S(2)}, u32[]{:S(2)}) collective-permute-start(f32[104,125]{1,0:T(8,128)S(1)} %add.15.a_ref), channel_id=1, source_target_pairs={{0,5},{1,4},{4,1},{5,0},{2,7},{3,6},{6,3},{7,2},{8,13},{9,12},{12,... | collective-permute-start | bytes 156008 | tf_op jit(solution)/shard_map/ppermute | solution.py:26
